TPU v7x, 32 devices: a whole 2x2x4 slice. The times are simulated.
32 devices in a mesh: fsdp: 16 (over z, x, core), rep: 2 (over y).
Axes of the slice: x: 2, y: 2, z: 4, core: 2. Of those that a mesh axis runs over, the one named last changes fastest.
Arguments:
- tokens: bfloat16 [64, 512, 768], P(('fsdp', 'rep')), may hold values from -6 to 6
- segments: int32 [64, 512], P(('fsdp', 'rep')), may hold values from 0 to 7, never falling along the last dimension, each value on 1 to 128 neighbouring positions
- w_query: bfloat16 [768, 768], P('fsdp'), may hold values from -0.21875 to 0.21875
- b_query: bfloat16 [768], P('fsdp'), may hold values from -3 to 3
- w_key: bfloat16 [768, 768], P('fsdp'), may hold values from -0.21875 to 0.21875
- w_value: bfloat16 [768, 768], P('fsdp'), may hold values from -0.21875 to 0.21875
- b_value: bfloat16 [768], P('fsdp'), may hold values from -3 to 3
- w_out: bfloat16 [768, 768], P('fsdp'), may hold values from -1.75 to 1.75
- b_out: bfloat16 [768], P('fsdp'), may hold values from -3 to 3
- gain1: bfloat16 [768], P('fsdp'), may hold values from 0.5 to 1.5
- shift1: bfloat16 [768], P('fsdp'), may hold values from -2 to 2
- w_up: bfloat16 [768, 3072], P('fsdp'), may hold values from -0.21875 to 0.21875
- b_up: bfloat16 [3072], P('fsdp'), may hold values from -3 to 3
- w_down: bfloat16 [3072, 768], P('fsdp'), may hold values from -0.109375 to 0.109375
- b_down: bfloat16 [768], P('fsdp'), may hold values from -3 to 3
- gain2: bfloat16 [768], P('fsdp'), may hold values from 0.5 to 1.5
- shift2: bfloat16 [768], P('fsdp'), may hold values from -2 to 2
- out_grad: bfloat16 [64, 512, 768], P(('fsdp', 'rep')), may hold values from -6 to 6
Outputs:
- output: bfloat16 [64, 512, 768], P(('fsdp', 'rep'))
- pooled: float32 [64, 8, 768], P(('fsdp', 'rep'))
- grad_tokens: bfloat16 [64, 512, 768], P(('fsdp', 'rep'))
- grad_w_query: float32 [768, 768], P('fsdp')
- grad_b_query: float32 [768], P('fsdp')
- grad_w_key: float32 [768, 768], P('fsdp')
- grad_w_value: float32 [768, 768], P('fsdp')
- grad_b_value: float32 [768], P('fsdp')
- grad_w_out: float32 [768, 768], P('fsdp')
- grad_b_out: float32 [768], P('fsdp')
- grad_gain1: float32 [768], P('fsdp')
- grad_shift1: float32 [768], P('fsdp')
- grad_w_up: float32 [768, 3072], P('fsdp')
- grad_b_up: float32 [3072], P('fsdp')
- grad_w_down: float32 [3072, 768], P('fsdp')
- grad_b_down: float32 [768], P('fsdp')
- grad_gain2: float32 [768], P('fsdp')
- grad_shift2: float32 [768], P('fsdp')
Inputs may be any that keep to these rules, and one draw needn't show every extreme that they name: `segments`: along each row the segment ids never fall and take every value from 0 to 7; a text has at most 128 tokens, and in every row one text has exactly 128.
All inputs are finite; a program needn't handle non-finite values.
Results may differ from a plain program's by a relative error of at most 0.015.
Values may be sent and summed in bfloat16 or wider, within the bound.
A program may use at most 192 MiB of HBM per device.

v0:
```python
import math

import jax
import jax.numpy as jnp
from jax import lax
from jax.sharding import PartitionSpec as P

HEAD = 64
SEGS = 8
MICRO = 2


norm_eps = 1e-05
masked_score = -1e30


def product(left, right):
    return jnp.dot(left, right, preferred_element_type=jnp.float32)


def inner_rows(left, right):
    return lax.dot_general(
        left, right, (((0,), (0,)), ((), ())), preferred_element_type=jnp.float32
    )


def times_transposed(left, right):
    return lax.dot_general(
        left, right, (((1,), (1,)), ((), ())), preferred_element_type=jnp.float32
    )


def norm_parts(hidden):
    center = hidden - jnp.mean(hidden, axis=-1, keepdims=True)
    inverse = lax.rsqrt(jnp.mean(center * center, axis=-1, keepdims=True) + norm_eps)
    return (center * inverse, inverse)


def norm_back(grad, normal, inverse, gain):
    scaled = grad * gain
    return inverse * (
        scaled
        - jnp.mean(scaled, axis=-1, keepdims=True)
        - normal * jnp.mean(scaled * normal, axis=-1, keepdims=True)
    )


def split_heads(matrix, row_count, seq_length, head_count):
    return (
        matrix.reshape(row_count, seq_length, head_count, HEAD)
        .transpose(0, 2, 1, 3)
        .reshape(row_count * head_count, seq_length, HEAD)
    )


def join_heads(stacked, row_count, seq_length, head_count):
    return (
        stacked.reshape(row_count, head_count, seq_length, HEAD)
        .transpose(0, 2, 1, 3)
        .reshape(row_count * seq_length, head_count * HEAD)
    )


def masked_scores(query_head, key_head, segment_row):
    scores = times_transposed(query_head, key_head) * HEAD ** (-0.5)
    same = segment_row[:, None] == segment_row[None, :]
    return jnp.where(same, scores, masked_score)


def head_forward(operands):
    query_head, key_head, value_head, segment_row = operands
    scores = masked_scores(query_head, key_head, segment_row)
    peak = jnp.max(scores, axis=-1, keepdims=True)
    expo = jnp.exp(scores - peak)
    total = jnp.sum(expo, axis=-1, keepdims=True)
    probs = (expo / total).astype(jnp.bfloat16)
    mixed = product(probs, value_head).astype(jnp.bfloat16)
    return (mixed, (peak + jnp.log(total))[:, 0])


def head_backward(operands):
    query_head, key_head, value_head, segment_row, logsum, grad_mixed = operands
    scores = masked_scores(query_head, key_head, segment_row)
    probs = jnp.exp(scores - logsum[:, None])
    grad_value = inner_rows(probs.astype(jnp.bfloat16), grad_mixed)
    grad_probs = times_transposed(grad_mixed, value_head)
    inner = jnp.sum(probs * grad_probs, axis=-1, keepdims=True)
    grad_scores = (probs * (grad_probs - inner)).astype(jnp.bfloat16)
    grad_query = product(grad_scores, key_head) * HEAD ** (-0.5)
    grad_key = inner_rows(grad_scores, query_head) * HEAD ** (-0.5)
    return (
        grad_query.astype(jnp.bfloat16),
        grad_key.astype(jnp.bfloat16),
        grad_value.astype(jnp.bfloat16),
    )


def column_sum(matrix):
    return jnp.sum(matrix, axis=0, dtype=jnp.float32)


def gelu_slope(hidden):
    return 0.5 * (1.0 + lax.erf(hidden / math.sqrt(2.0))) + hidden * jnp.exp(
        -0.5 * hidden * hidden
    ) / math.sqrt(2.0 * math.pi)


def fetch_weights(
    w_query,
    b_query,
    w_key,
    w_value,
    b_value,
    w_out,
    b_out,
    gain1,
    shift1,
    w_up,
    b_up,
    w_down,
    b_down,
    gain2,
    shift2,
):
    return (
        lax.all_gather(w_query, "fsdp", axis=0, tiled=True),
        lax.all_gather(b_query, "fsdp", axis=0, tiled=True),
        lax.all_gather(w_key, "fsdp", axis=0, tiled=True),
        lax.all_gather(w_value, "fsdp", axis=0, tiled=True),
        lax.all_gather(b_value, "fsdp", axis=0, tiled=True),
        lax.all_gather(w_out, "fsdp", axis=0, tiled=True),
        lax.all_gather(b_out, "fsdp", axis=0, tiled=True),
        lax.all_gather(gain1, "fsdp", axis=0, tiled=True),
        lax.all_gather(shift1, "fsdp", axis=0, tiled=True),
        lax.all_gather(w_up, "fsdp", axis=0, tiled=True),
        lax.all_gather(b_up, "fsdp", axis=0, tiled=True),
        lax.all_gather(w_down, "fsdp", axis=0, tiled=True),
        lax.all_gather(b_down, "fsdp", axis=0, tiled=True),
        lax.all_gather(gain2, "fsdp", axis=0, tiled=True),
        lax.all_gather(shift2, "fsdp", axis=0, tiled=True),
    )


def local(
    tokens,
    segments,
    w_query,
    b_query,
    w_key,
    w_value,
    b_value,
    w_out,
    b_out,
    gain1,
    shift1,
    w_up,
    b_up,
    w_down,
    b_down,
    gain2,
    shift2,
    out_grad,
):
    row_count = tokens.shape[0] // MICRO
    seq_length = tokens.shape[1]
    model_width = tokens.shape[2]
    head_count = model_width // HEAD
    slot_ids = jnp.arange(SEGS, dtype=jnp.int32)
    shards = (
        w_query,
        b_query,
        w_key,
        w_value,
        b_value,
        w_out,
        b_out,
        gain1,
        shift1,
        w_up,
        b_up,
        w_down,
        b_down,
        gain2,
        shift2,
    )
    out_parts = []
    pooled_parts = []
    input_parts = []
    share_total = None
    for micro_index in range(MICRO):
        first_row = micro_index * row_count
        gathered = fetch_weights(*shards)
        (
            query_weight,
            query_bias,
            key_weight,
            value_weight,
            value_bias,
            out_weight,
            out_bias,
            first_gain,
            first_shift,
            up_weight,
            up_bias,
            down_weight,
            down_bias,
            second_gain,
            second_shift,
        ) = gathered
        tok_block = tokens[first_row : first_row + row_count]
        seg_block = segments[first_row : first_row + row_count]
        tok_rows = tok_block.reshape(row_count * seq_length, model_width)
        queries = (product(tok_rows, query_weight) + query_bias).astype(jnp.bfloat16)
        key_rows = product(tok_rows, key_weight).astype(jnp.bfloat16)
        values = (product(tok_rows, value_weight) + value_bias).astype(jnp.bfloat16)
        head_segments = jnp.broadcast_to(
            seg_block[:, None, :], (row_count, head_count, seq_length)
        ).reshape(row_count * head_count, seq_length)
        query_heads = split_heads(queries, row_count, seq_length, head_count)
        key_heads = split_heads(key_rows, row_count, seq_length, head_count)
        value_heads = split_heads(values, row_count, seq_length, head_count)
        mixed_heads, logsums = lax.map(
            head_forward, (query_heads, key_heads, value_heads, head_segments)
        )
        attended = join_heads(mixed_heads, row_count, seq_length, head_count)
        branch = product(attended, out_weight) + out_bias
        first_normal, first_inverse = norm_parts(tok_rows.astype(jnp.float32) + branch)
        normed = first_normal * first_gain + first_shift
        normed_low = normed.astype(jnp.bfloat16)
        hidden = product(normed_low, up_weight) + up_bias
        active = jax.nn.gelu(hidden, approximate=False).astype(jnp.bfloat16)
        fed = product(active, down_weight) + down_bias
        second_normal, second_inverse = norm_parts(normed + fed)
        result = second_normal * second_gain + second_shift
        out_parts.append(result.astype(jnp.bfloat16).reshape(row_count, seq_length, model_width))
        onehot = (seg_block[:, :, None] == slot_ids[None, None, :]).astype(jnp.float32)
        counts = jnp.sum(onehot, axis=1)
        pooled_sum = jnp.einsum(
            "rls,rld->rsd",
            onehot,
            result.reshape(row_count, seq_length, model_width),
            precision=lax.Precision.HIGHEST,
        )
        pooled_parts.append(pooled_sum / counts[:, :, None])
        grad_result = (
            out_grad[first_row : first_row + row_count]
            .reshape(row_count * seq_length, model_width)
            .astype(jnp.float32)
        )
        grad_gain2 = jnp.sum(grad_result * second_normal, axis=0)
        grad_shift2 = jnp.sum(grad_result, axis=0)
        grad_second = norm_back(grad_result, second_normal, second_inverse, second_gain)
        grad_fed = grad_second.astype(jnp.bfloat16)
        grad_b_down = column_sum(grad_fed)
        grad_w_down = inner_rows(active, grad_fed)
        grad_hidden = (times_transposed(grad_fed, down_weight) * gelu_slope(hidden)).astype(
            jnp.bfloat16
        )
        grad_b_up = column_sum(grad_hidden)
        grad_w_up = inner_rows(normed_low, grad_hidden)
        grad_normed = grad_second + times_transposed(grad_hidden, up_weight)
        grad_gain1 = jnp.sum(grad_normed * first_normal, axis=0)
        grad_shift1 = jnp.sum(grad_normed, axis=0)
        grad_first = norm_back(grad_normed, first_normal, first_inverse, first_gain)
        grad_branch = grad_first.astype(jnp.bfloat16)
        grad_b_out = column_sum(grad_branch)
        grad_w_out = inner_rows(attended, grad_branch)
        grad_attended = times_transposed(grad_branch, out_weight).astype(jnp.bfloat16)
        grad_mixed = split_heads(grad_attended, row_count, seq_length, head_count)
        grad_qh, grad_kh, grad_vh = lax.map(
            head_backward, (query_heads, key_heads, value_heads, head_segments, logsums, grad_mixed)
        )
        grad_queries = join_heads(grad_qh, row_count, seq_length, head_count)
        grad_keys = join_heads(grad_kh, row_count, seq_length, head_count)
        grad_values = join_heads(grad_vh, row_count, seq_length, head_count)
        grad_w_query = inner_rows(tok_rows, grad_queries)
        grad_b_query = column_sum(grad_queries)
        grad_w_key = inner_rows(tok_rows, grad_keys)
        grad_w_value = inner_rows(tok_rows, grad_values)
        grad_b_value = column_sum(grad_values)
        grad_input = (
            grad_first
            + times_transposed(grad_queries, query_weight)
            + times_transposed(grad_keys, key_weight)
            + times_transposed(grad_values, value_weight)
        )
        input_parts.append(
            grad_input.astype(jnp.bfloat16).reshape(row_count, seq_length, model_width)
        )
        shares = (
            lax.psum_scatter(grad_w_query, "fsdp", scatter_dimension=0, tiled=True),
            lax.psum_scatter(grad_b_query, "fsdp", scatter_dimension=0, tiled=True),
            lax.psum_scatter(grad_w_key, "fsdp", scatter_dimension=0, tiled=True),
            lax.psum_scatter(grad_w_value, "fsdp", scatter_dimension=0, tiled=True),
            lax.psum_scatter(grad_b_value, "fsdp", scatter_dimension=0, tiled=True),
            lax.psum_scatter(grad_w_out, "fsdp", scatter_dimension=0, tiled=True),
            lax.psum_scatter(grad_b_out, "fsdp", scatter_dimension=0, tiled=True),
            lax.psum_scatter(grad_gain1, "fsdp", scatter_dimension=0, tiled=True),
            lax.psum_scatter(grad_shift1, "fsdp", scatter_dimension=0, tiled=True),
            lax.psum_scatter(grad_w_up, "fsdp", scatter_dimension=0, tiled=True),
            lax.psum_scatter(grad_b_up, "fsdp", scatter_dimension=0, tiled=True),
            lax.psum_scatter(grad_w_down, "fsdp", scatter_dimension=0, tiled=True),
            lax.psum_scatter(grad_b_down, "fsdp", scatter_dimension=0, tiled=True),
            lax.psum_scatter(grad_gain2, "fsdp", scatter_dimension=0, tiled=True),
            lax.psum_scatter(grad_shift2, "fsdp", scatter_dimension=0, tiled=True),
        )
        share_total = (
            tuple(shares)
            if share_total is None
            else tuple((old + new for old, new in zip(share_total, shares)))
        )
    totals = (
        lax.psum(share_total[0].astype(jnp.bfloat16), "rep").astype(jnp.float32),
        lax.psum(share_total[1].astype(jnp.bfloat16), "rep").astype(jnp.float32),
        lax.psum(share_total[2].astype(jnp.bfloat16), "rep").astype(jnp.float32),
        lax.psum(share_total[3].astype(jnp.bfloat16), "rep").astype(jnp.float32),
        lax.psum(share_total[4].astype(jnp.bfloat16), "rep").astype(jnp.float32),
        lax.psum(share_total[5].astype(jnp.bfloat16), "rep").astype(jnp.float32),
        lax.psum(share_total[6].astype(jnp.bfloat16), "rep").astype(jnp.float32),
        lax.psum(share_total[7].astype(jnp.bfloat16), "rep").astype(jnp.float32),
        lax.psum(share_total[8].astype(jnp.bfloat16), "rep").astype(jnp.float32),
        lax.psum(share_total[9].astype(jnp.bfloat16), "rep").astype(jnp.float32),
        lax.psum(share_total[10].astype(jnp.bfloat16), "rep").astype(jnp.float32),
        lax.psum(share_total[11].astype(jnp.bfloat16), "rep").astype(jnp.float32),
        lax.psum(share_total[12].astype(jnp.bfloat16), "rep").astype(jnp.float32),
        lax.psum(share_total[13].astype(jnp.bfloat16), "rep").astype(jnp.float32),
        lax.psum(share_total[14].astype(jnp.bfloat16), "rep").astype(jnp.float32),
    )
    output = jnp.concatenate(out_parts, axis=0)
    pooled = jnp.concatenate(pooled_parts, axis=0)
    grad_tokens = jnp.concatenate(input_parts, axis=0)
    return (output, pooled, grad_tokens) + tuple(totals)


def solution(mesh):
    placed = (
        P(("fsdp", "rep"), None, None),
        P(("fsdp", "rep"), None),
        P("fsdp", None),
        P("fsdp"),
        P("fsdp", None),
        P("fsdp", None),
        P("fsdp"),
        P("fsdp", None),
        P("fsdp"),
        P("fsdp"),
        P("fsdp"),
        P("fsdp", None),
        P("fsdp"),
        P("fsdp", None),
        P("fsdp"),
        P("fsdp"),
        P("fsdp"),
        P(("fsdp", "rep"), None, None),
    )
    return jax.shard_map(
        local,
        mesh=mesh,
        in_specs=placed,
        out_specs=(
            P(("fsdp", "rep"), None, None),
            P(("fsdp", "rep"), None, None),
            P(("fsdp", "rep"), None, None),
            P("fsdp", None),
            P("fsdp"),
            P("fsdp", None),
            P("fsdp", None),
            P("fsdp"),
            P("fsdp", None),
            P("fsdp"),
            P("fsdp"),
            P("fsdp"),
            P("fsdp", None),
            P("fsdp"),
            P("fsdp", None),
            P("fsdp"),
            P("fsdp"),
            P("fsdp"),
        ),
        check_vma=False,
    )
```

profile of v0, /device:TPU:0, one launch (start us, length us, event | category | flops | bytes accessed | tf_op | source)
XLA Modules:
  0.0 1139.6 jit_solution(12741274807909366759)
XLA Ops:
  21.4 63.3 %all-reduce.19 = (bf16[768]{0:T(1024)(128)(2,1)S(1)}, bf16[768]{0:T(1024)(128)(2,1)S(1)}, bf16[768]{0:T(1024)(128)(2,1)S(1)}, bf16[768]{0:T(1024)(128)(2,1)S(1)}...) all-reduce(bf16[768]{0:T(1024)(128)(2,1)S(1)} %dynamic-update-slice, ...), channel_id=1, replica_groups=mesh['fsdp'=16,'rep'=2] {'fsdp'}, use_global_device_ids=true, to_apply=%add | all-reduce | flops 9216 | bytes 36864
  91.1 2.9 convolution_convert_fusion.6
  98.8 32.1 %all-gather.11.cloned.1.call-done = bf16[768,768]{1,0:T(8,128)(2,1)} async-done(((bf16[48,768]{1,0:T(8,128)(2,1)}), bf16[768,768]{1,0:T(8,128)(2,1)}) %all-gather.11.cloned.1.call-update) | async-done | bytes 1179664 | tf_op jit(solution)/shard_map/all_gather | solution.py:129
  130.8 2.9 add_convert_fusion.2
  139.5 40.1 %while.53 = (s32[]{:T(128)}, bf16[12,512,64]{1,2,0:T(8,128)(2,1)}, f32[12,512]{1,0:T(8,128)S(1)}, s32[12,512]{1,0:T(8,128)S(1)}, bf16[12,512,64]{2,1,0:T(8,128)(...) while((s32[]{:T(128)}, bf16[12,512,64]{1,2,0:T(8,128)(2,1)}, ...), condition=%wide.region_11.12_spmd, body=%wide.region_8.11_spmd.sunk | while | flops 69500416 | bytes 3635309 | solution.py:222
  191.0 2.9 convolution_convert_fusion.7
  198.7 3.0 add_convert_fusion.4
  207.4 40.9 %while.52 = (s32[]{:T(128)}, bf16[12,512,64]{1,2,0:T(8,128)(2,1)}, f32[12,512]{1,0:T(8,128)S(1)}, s32[12,512]{1,0:T(8,128)S(1)}, bf16[12,512,64]{2,1,0:T(8,128)(...) while((s32[]{:T(128)}, bf16[12,512,64]{1,2,0:T(8,128)(2,1)}, ...), condition=%wide.region_3.4_spmd, body=%wide.region_0.3_spmd.sunk | while | flops 69500416 | bytes 3635309 | solution.py:222
  252.3 5.4 fusion.200
  260.4 31.4 %fusion.90 = (bf16[512,3072]{1,0:T(8,128)(2,1)}, bf16[512,3072]{1,0:T(8,128)(2,1)}, f32[512,3072]{1,0:T(8,128)}) fusion(f32[3072]{0:T(1024)S(1)} %convert_element_type.322, f32[512,3072]{1,0:T(8,128)S(1)} %fusion.200, bf16[768,3072]{1,0:T(8,128)(2,1)S(1)} %copy-done.47, f32[512,768]{1,0:T(8,128)S(1)} %copy-done.37, f32[768]{0:T(1024)S(1)} %convert_element_type.320, ...), kind=kOutput, calls=%fused_computation.122 | convolution fusion | flops 2625503232 | bytes 25188352 | tf_op jit(solution)/shard_map/dot_general | solution.py:18
  291.9 6.2 fusion.214
  307.3 8.2 convert_reduce_fusion.1
  315.5 3.1 multiply_reduce_fusion.3
  318.6 4.6 convert_reduce_fusion
  323.3 4.8 convert_reduce_fusion.7
  336.3 115.8 %while.55 = (s32[]{:T(128)}, bf16[12,512,64]{1,2,0:T(8,128)(2,1)}, bf16[12,512,64]{1,2,0:T(8,128)(2,1)}, bf16[12,512,64]{1,2,0:T(8,128)(2,1)}, s32[12,512]{1,0:T...) while((s32[]{:T(128)}, bf16[12,512,64]{1,2,0:T(8,128)(2,1)}, ...), condition=%wide.region_31.32_spmd, body=%wide.region_29.31_spmd.sunk | while | flops 170556928 | bytes 8871037 | solution.py:270
  452.1 3.4 convolution_convert_fusion.5
  460.8 116.0 %while.54 = (s32[]{:T(128)}, bf16[12,512,64]{1,2,0:T(8,128)(2,1)}, bf16[12,512,64]{1,2,0:T(8,128)(2,1)}, bf16[12,512,64]{1,2,0:T(8,128)(2,1)}, s32[12,512]{1,0:T...) while((s32[]{:T(128)}, bf16[12,512,64]{1,2,0:T(8,128)(2,1)}, ...), condition=%wide.region_24.25_spmd, body=%wide.region_22.24_spmd.sunk | while | flops 170556928 | bytes 8871037 | solution.py:270
  581.3 3.2 copy.122
  589.1 3.1 copy.124
  596.9 3.1 copy.126
  605.2 5.4 fusion.202
  610.6 5.8 convolution_add_fusion.1
  616.5 5.2 fusion.196
  621.8 5.3 convolution_add_fusion
  632.1 59.7 %all-reduce.18 = (bf16[768]{0:T(1024)(128)(2,1)S(1)}, bf16[768]{0:T(1024)(128)(2,1)S(1)}, bf16[768]{0:T(1024)(128)(2,1)S(1)}, bf16[768]{0:T(1024)(128)(2,1)S(1)}...) all-reduce(f32[768]{0:T(1024)S(1)} %reshape.519, ...), channel_id=18, replica_groups=mesh['fsdp'=16,'rep'=2] {'fsdp'}, use_global_device_ids=true, to_apply=%region_36.37.clone | all-reduce | flops 9216 | bytes 55296
  692.5 5.2 all-reduce.20
  717.6 60.9 %reduce-scatter.23.cloned.1.call-done = f32[48,768]{1,0:T(8,128)} async-done(((f32[768,768]{1,0:T(8,128)}), f32[48,768]{1,0:T(8,128)}) %reduce-scatter.23.cloned.1.call-update) | async-done | bytes 147472
  780.3 64.4 %reduce-scatter.13.cloned.1.call-done = f32[48,768]{1,0:T(8,128)} async-done(((f32[768,768]{1,0:T(8,128)}), f32[48,768]{1,0:T(8,128)}) %reduce-scatter.13.cloned.1.call-update) | async-done | bytes 147472 | tf_op jit(solution)/shard_map/reduce_scatter | solution.py:296
  846.2 113.0 %reduce-scatter.15.cloned.1.call-done = f32[48,3072]{1,0:T(8,128)} async-done(((f32[768,3072]{1,0:T(8,128)}), f32[48,3072]{1,0:T(8,128)}) %reduce-scatter.15.cloned.1.call-update) | async-done | bytes 589840 | tf_op jit(solution)/shard_map/reduce_scatter | solution.py:300
  961.0 113.9 %reduce-scatter.17.cloned.1.call-done = f32[192,768]{1,0:T(8,128)} async-done(((f32[3072,768]{1,0:T(8,128)}), f32[192,768]{1,0:T(8,128)}) %reduce-scatter.17.cloned.1.call-update) | async-done | bytes 589840 | tf_op jit(solution)/shard_map/reduce_scatter | solution.py:302
  1081.3 41.9 %all-reduce.24.cloned.1.call-done = (bf16[48,768]{0,1:T(8,128)(2,1)}, bf16[48,768]{0,1:T(8,128)(2,1)}, bf16[48,768]{0,1:T(8,128)(2,1)}, bf16[48,768]{1,0:T(8,128...) async-done(((bf16[48,768]{0,1:T(8,128)(2,1)}, bf16[48,768]{0,1:T(8,128)(2,1)}, bf16[48,768]{0,1:T(8,128)(2,1)}, bf16[48,768]{1,0:T(8,128)(2,1)}, ...) | async-done | bytes 884752 | tf_op jit(solution)/shard_map/psum | solution.py:313
  (641 shorter events, 455.9 us)
Async XLA Ops:
  7.2 78.3 %all-gather.7.cloned.1.call-start = ((), (), s32[]{:S(2)}) async-start(), calls=%async_computation.6 | async-start | bytes 1253376 | tf_op jit(solution)/shard_map/all_gather | solution.py:126
  7.9 83.2 %all-gather.9.cloned.1.call-start = ((), (), s32[]{:S(2)}) async-start(), calls=%async_computation.7 | async-start | bytes 1253376 | tf_op jit(solution)/shard_map/all_gather | solution.py:128
  8.7 122.2 %all-gather.11.cloned.1.call-start = ((), (), s32[]{:S(2)}) async-start(), calls=%async_computation.8 | async-start | bytes 1253376 | tf_op jit(solution)/shard_map/all_gather | solution.py:129
  9.4 170.2 %all-gather.13.cloned.1.call-start = ((), (), s32[]{:S(2)}) async-start(), calls=%async_computation.9 | async-start | bytes 1253376 | tf_op jit(solution)/shard_map/all_gather | solution.py:131
  10.0 242.3 %all-gather.15.cloned.1.call-start = ((), (), s32[]{:S(2)}) async-start(), calls=%async_computation.10 | async-start | bytes 5013504 | tf_op jit(solution)/shard_map/all_gather | solution.py:135
  10.6 281.3 %all-gather.17.cloned.1.call-start = ((), (), s32[]{:S(2)}) async-start(), calls=%async_computation.11 | async-start | bytes 5013504 | tf_op jit(solution)/shard_map/all_gather | solution.py:137
  11.1 703.0 %reduce-scatter.19.cloned.1.call-start = ((), (), s32[]{:S(2)}) async-start(), calls=%async_computation.15 | async-start | bytes 2506752
  85.4 53.1 %copy-start.45 = (s32[1,512]{1,0:T(1,128)}, s32[1,512]{1,0:T(1,128)S(1)}, u32[]{:S(2)}) copy-start(s32[1,512]{1,0:T(1,128)S(1)} %get-tuple-element.533) | copy-start | bytes 6148
  85.4 121.0 %copy-start.43 = (s32[1,512]{1,0:T(1,128)}, s32[1,512]{1,0:T(1,128)S(1)}, u32[]{:S(2)}) copy-start(s32[1,512]{1,0:T(1,128)S(1)} %get-tuple-element.532) | copy-start | bytes 6148
  252.3 8.2 copy-start.37
  252.3 8.1 copy-start.47
  291.9 6.5 slice-start.2
  291.9 6.5 copy-start.18
  291.9 6.5 slice-start.3
  298.1 6.8 copy-start.2
  304.9 10.6 slice-start
  304.9 13.7 %slice-start.4 = ((s8[6291456]{0:T(1024)(128)(4,1)}), s8[4194304]{0:T(1024)(128)(4,1)S(1)}, s32[]{:S(2)}) async-start(s8[6291456]{0:T(1024)(128)(4,1)} %bitcast.468), calls=%async_computation.23 | async-start | bytes 8388608
  307.3 8.2 copy-start.22
  307.3 16.1 %copy-start.20 = (f32[512,768]{1,0:T(8,128)}, f32[512,768]{1,0:T(8,128)S(1)}, u32[]{:S(2)}) copy-start(f32[512,768]{1,0:T(8,128)S(1)} %get-tuple-element.506) | copy-start | bytes 4718596
  307.3 8.2 slice-start.1
  307.3 11.4 slice-start.5
  584.5 131.4 %reduce-scatter.21.cloned.1.call-start = ((), (), s32[]{:S(2)}) async-start(), calls=%async_computation.16 | async-start | bytes 2506752
  592.2 186.3 %reduce-scatter.23.cloned.1.call-start = ((), (), s32[]{:S(2)}) async-start(), calls=%async_computation.17 | async-start | bytes 2506752
  600.0 244.6 %reduce-scatter.13.cloned.1.call-start = ((), (), s32[]{:S(2)}) async-start(), calls=%async_computation.12 | async-start | bytes 2506752 | tf_op jit(solution)/shard_map/reduce_scatter | solution.py:296
  605.1 354.0 %reduce-scatter.15.cloned.1.call-start = ((), (), s32[]{:S(2)}) async-start(), calls=%async_computation.13 | async-start | bytes 10027008 | tf_op jit(solution)/shard_map/reduce_scatter | solution.py:300
  605.2 5.4 copy-start.28
  616.5 5.3 copy-start.21
  616.5 458.3 %reduce-scatter.17.cloned.1.call-start = ((), (), s32[]{:S(2)}) async-start(), calls=%async_computation.14 | async-start | bytes 10027008 | tf_op jit(solution)/shard_map/reduce_scatter | solution.py:302
  627.2 496.1 %all-reduce.24.cloned.1.call-start = ((), (), s32[]{:S(2)}) async-start(), calls=%async_computation.18 | async-start | bytes 2506752 | tf_op jit(solution)/shard_map/psum | solution.py:313
  630.5 74.4 %copy-start.3 = (f32[512,768]{1,0:T(8,128)S(1)}, f32[512,768]{1,0:T(8,128)}, u32[]{:S(2)}) copy-start(f32[512,768]{1,0:T(8,128)} %copy-done.2) | copy-start | bytes 4718596
  846.2 230.6 %copy-start.17 = (bf16[12,512,64]{1,2,0:T(8,128)(2,1)S(1)}, bf16[12,512,64]{1,2,0:T(8,128)(2,1)}, u32[]{:S(2)}) copy-start(bf16[12,512,64]{1,2,0:T(8,128)(2,1)} %get-tuple-element.205) | copy-start | bytes 2359300
  1123.3 8.5 copy-start.38
  (41 other events, 96.9 us)
Sparse Core Ops, SparseCore 0:
  10.3 41.2 all-gather.6
  53.8 37.2 all-gather.8
  93.4 37.3 all-gather.10
  133.0 37.3 all-gather.12
  172.6 52.1 all-gather.14
  226.9 51.9 all-gather.16
  584.6 61.6 reduce-scatter.18
  650.6 62.1 reduce-scatter.20
  716.6 61.9 reduce-scatter.22
  782.6 61.9 reduce-scatter.12
  848.8 110.3 reduce-scatter.14
  963.7 111.1 reduce-scatter.16
  1078.1 45.1 all-reduce.23
where the time goes:
time: 1160 us; the launch traced here: 1140 us
  waiting for transfers between devices  430 us (37%)
  matrix products  408 us (35%)
  blocking collectives  128 us (11%)
  local copies, waits for them, and re-layouts  116 us (10%)
  other arithmetic  36.6 us (3%)
  between operations  18.1 us (2%)
    dot_general x60, matrix products, product(): return jnp.dot(left, right, preferred_element_type=jnp.float32)  153 us
    dot_general x84, matrix products, times_transposed(): lax.dot_general(left, right, (((1,), (1,)), ((), ())), preferred_element_...  126 us
    dot_general x60, matrix products, inner_rows(): lax.dot_general(left, right, (((0,), (0,)), ((), ())), preferred_element_...  126 us
    unnamed x2, blocking collectives  123 us
    reduce_scatter x1, waiting for transfers between devices, local(): lax.psum_scatter(grad_w_down, 'fsdp', scatter_dimension=0, tiled=True)  114 us
    reduce_scatter x1, waiting for transfers between devices, local(): lax.psum_scatter(grad_w_up, 'fsdp', scatter_dimension=0, tiled=True)  113 us
    unnamed x16, waiting for transfers between devices  64.7 us
    reduce_scatter x1, waiting for transfers between devices, local(): lax.psum_scatter(grad_w_out, 'fsdp', scatter_dimension=0, tiled=True)  64.4 us
  transfers between devices with their start and end apart: 13, of which 7 were waited for; matrix products, arithmetic and copies ran while one was open for 22% of the time, Pallas kernels for 0%

commit v1 on v0

v1 whole, which is shorter than its diff:
```python
import functools
import math

import jax
import jax.numpy as jnp
from jax import lax
from jax.experimental import pallas as pl
from jax.experimental.pallas import tpu as pltpu
from jax.sharding import PartitionSpec as P

BF = jnp.bfloat16
F32 = jnp.float32
HEAD = 64
SEGS = 8
BLOCK = 128
EPS = 1e-5
MASKED = -1e30
MESH = pl.DeviceIdType.MESH
VMEM_LIMIT = 61 * 2**20


def nn(a, b):
    return lax.dot_general(a, b, (((1,), (0,)), ((), ())), preferred_element_type=F32)


def nt(a, b):
    return lax.dot_general(a, b, (((1,), (1,)), ((), ())), preferred_element_type=F32)


def tn(a, b):
    return lax.dot_general(a, b, (((0,), (0,)), ((), ())), preferred_element_type=F32)


def rmean(t):
    return jnp.mean(t, axis=-1, keepdims=True)


def csum(t):
    return jnp.sum(t, axis=0, keepdims=True)


def loop(count, step):
    def body(i, carry):
        step(i)
        return carry

    lax.fori_loop(0, count, body, 0)


def ds(start, size, multiple=None):
    if not isinstance(start, int):
        start = pl.multiple_of(start, multiple or size)
    return pl.ds(start, size)


def key_windows(length):
    blocks = length // BLOCK
    spans, offsets, total = [], [], 0
    for qb in range(blocks):
        span = (max(qb - 1, 0), min(qb + 2, blocks))
        spans.append(span)
        offsets.append(total)
        total += (span[1] - span[0]) * BLOCK
    return spans, offsets, total


def stack2(pair):
    lane = lax.broadcasted_iota(jnp.int32, pair.shape, 1)
    zero = jnp.zeros_like(pair)
    return jnp.concatenate(
        [jnp.where(lane < HEAD, pair, zero), jnp.where(lane < HEAD, zero, pair)], axis=0
    )


def unstack_t(both):
    return jnp.concatenate([both[:HEAD, :BLOCK], both[HEAD:, BLOCK:]], axis=0).T


def make_bias(seg, bias):
    rows, length = seg.shape
    spans, offsets, _ = key_windows(length)
    for row in range(rows):
        ids = seg[row : row + 1, :].astype(F32)
        keys = jnp.broadcast_to(ids, (BLOCK, length)).T
        for qb, (k0, k1) in enumerate(spans):
            same = keys[k0 * BLOCK : k1 * BLOCK, :] == ids[:, qb * BLOCK : (qb + 1) * BLOCK]
            bias[row, offsets[qb] : offsets[qb] + (k1 - k0) * BLOCK, :] = jnp.where(
                same, 0.0, MASKED
            )


def attend_pair(i, length, pairs, q, k, v, o, probs, bias):
    spans, offsets, _ = key_windows(length)
    row, pair = i // pairs, i % pairs
    r0, c = pl.multiple_of(row * length, length), ds(pair * BLOCK, BLOCK)
    vt = v[pl.ds(r0, length), c].T
    for qb, (k0, k1) in enumerate(spans):
        n, at = (k1 - k0) * BLOCK, offsets[qb]
        mine = pl.ds(r0 + qb * BLOCK, BLOCK)
        q2 = stack2(q[mine, c] * BF(HEAD**-0.5))
        s = nt(k[pl.ds(r0 + k0 * BLOCK, n), c], q2)
        b = bias[row, at : at + n, :]
        s = s + jnp.concatenate([b, b], axis=1)
        e = jnp.exp(s - jnp.max(s, axis=0, keepdims=True))
        p = (e * (1.0 / jnp.sum(e, axis=0, keepdims=True))).astype(BF)
        probs[i, at : at + n, :] = p
        o[mine, c] = unstack_t(nn(vt[:, k0 * BLOCK : k1 * BLOCK], p)).astype(BF)


def attend_back_pair(i, length, pairs, q, k, v, do, probs, dq, dk, dv, dk_sum, dv_sum):
    spans, offsets, _ = key_windows(length)
    last = len(spans) - 1
    row, pair = i // pairs, i % pairs
    r0, c = pl.multiple_of(row * length, length), ds(pair * BLOCK, BLOCK)
    kt = k[pl.ds(r0, length), c].T
    for qb, (k0, k1) in enumerate(spans):
        n, at = (k1 - k0) * BLOCK, offsets[qb]
        mine = pl.ds(r0 + qb * BLOCK, BLOCK)
        q2 = stack2(q[mine, c] * BF(HEAD**-0.5))
        do2 = stack2(do[mine, c])
        dp = nt(v[pl.ds(r0 + k0 * BLOCK, n), c], do2)
        low = probs[i, at : at + n, :]
        p = low.astype(F32)
        d_s = (p * (dp - jnp.sum(p * dp, axis=0, keepdims=True))).astype(BF)
        dv_part = nn(low, do2)
        dk_part = nn(d_s, q2)
        for kb in range(k0, k1):
            part = slice((kb - k0) * BLOCK, (kb - k0 + 1) * BLOCK)
            held = slice(kb * BLOCK, (kb + 1) * BLOCK)
            a, b = dv_part[part], dk_part[part]
            if qb != max(kb - 1, 0):
                a, b = a + dv_sum[held, :], b + dk_sum[held, :]
            if qb == min(kb + 1, last):
                there = pl.ds(r0 + kb * BLOCK, BLOCK)
                dv[there, c] = a.astype(BF)
                dk[there, c] = b.astype(BF)
            else:
                dv_sum[held, :] = a
                dk_sum[held, :] = b
        dqt = nn(kt[:, k0 * BLOCK : k1 * BLOCK], d_s)
        dq[mine, c] = (unstack_t(dqt) * HEAD**-0.5).astype(BF)


class Place:
    def __init__(self, depth):
        self.depth = depth
        self.f = lax.axis_index("fsdp")
        self.y = lax.axis_index("rep")
        self.c = self.f % 2
        self.x = self.f // 2 % 2
        self.z = self.f // 4
        self.sib = (self.f + 1 - 2 * self.c, self.y)
        self.xn = (self.f + 2 - 4 * self.x, self.y)
        self.yn = (self.f, 1 - self.y)
        self.up = (self.f + 4, self.y)
        self.down = (self.f - 4, self.y)

    def barrier(self):
        sem = pltpu.get_barrier_semaphore()
        for who in (self.sib, self.xn, self.yn):
            pl.semaphore_signal(sem, inc=1, device_id=who, device_id_type=MESH)

        @pl.when(self.z > 0)
        def _():
            pl.semaphore_signal(sem, inc=1, device_id=self.down, device_id_type=MESH)

        @pl.when(self.z < self.depth - 1)
        def _():
            pl.semaphore_signal(sem, inc=1, device_id=self.up, device_id_type=MESH)

        inner = (self.z > 0).astype(jnp.int32) + (self.z < self.depth - 1).astype(jnp.int32)
        pl.semaphore_wait(sem, 3 + inner)


def remote(src, dst, send, recv, who):
    return pltpu.make_async_remote_copy(
        src_ref=src, dst_ref=dst, send_sem=send, recv_sem=recv, device_id=who, device_id_type=MESH
    )


def gather_sems(groups, depth):
    return [
        pltpu.SemaphoreType.DMA((groups, 2, depth - 1)),
        pltpu.SemaphoreType.DMA((groups, depth)),
        pltpu.SemaphoreType.DMA((groups, depth)),
        pltpu.SemaphoreType.DMA((groups, 3, depth)),
    ] * 2 + [pltpu.SemaphoreType.DMA((groups,))]


class Gather:
    def __init__(self, place, g, shard, whole, sems):
        self.p, self.g, self.shard, self.whole = place, g, shard, whole
        self.sz, self.sx, self.sy, self.sc, self.rz, self.rx, self.ry, self.rc, self.own = sems
        self.rows, self.cols = shard.shape

    def piece(self, z, x, half=None):
        f = (z * 2 + x) * 2 + self.p.c
        at = self.whole.at[ds(f * self.rows, self.rows, 16)]
        if half is None:
            return at
        return self.whole.at[ds(f * self.rows, self.rows, 16), ds(half * (self.cols // 2), self.cols // 2)]

    def piece_of(self, z, x, c):
        return self.whole.at[ds(((z * 2 + x) * 2 + c) * self.rows, self.rows, 16)]

    def copy_z(self, direction, distance, z, src=None):
        dst = self.piece(z, self.p.x)
        return remote(
            dst if src is None else src,
            dst,
            self.sz.at[self.g, direction, distance],
            self.rz.at[self.g, direction, distance],
            self.p.up if direction == 0 else self.p.down,
        )

    def copy_x(self, z, src=None):
        dst = self.piece(z, self.p.x, self.p.y)
        return remote(dst if src is None else src, dst, self.sx.at[self.g, z], self.rx.at[self.g, z], self.p.xn)

    def copy_y(self, z):
        at = self.piece(z, 1 - self.p.x, self.p.y)
        return remote(at, at, self.sy.at[self.g, z], self.ry.at[self.g, z], self.p.yn)

    def copy_c(self, kind, z, src=None):
        if kind == 0:
            dst = self.piece(z, self.p.x)
        else:
            half = self.p.y if kind == 1 else 1 - self.p.y
            dst = self.piece(z, 1 - self.p.x, half)
        return remote(
            dst if src is None else src,
            dst,
            self.sc.at[self.g, kind, z],
            self.rc.at[self.g, kind, z],
            self.p.sib,
        )

    def local(self):
        return pltpu.make_async_copy(self.shard, self.piece(self.p.z, self.p.x), self.own.at[self.g])

    def z_step(self, k):
        p = self.p
        if k == 0:
            self.local().start()

            @pl.when(p.z < p.depth - 1)
            def _():
                self.copy_z(0, 0, p.z, self.shard).start()

            @pl.when(p.z > 0)
            def _():
                self.copy_z(1, 0, p.z, self.shard).start()

            half = self.shard.at[:, ds(p.y * (self.cols // 2), self.cols // 2)]
            self.copy_x(p.z, half).start()
            self.copy_c(0, p.z, self.shard).start()
            return

        for direction in (0, 1):
            z = p.z - k if direction == 0 else p.z + k

            @pl.when(z >= 0 if direction == 0 else z < p.depth)
            def _(direction=direction, z=z):
                self.copy_z(direction, k - 1, z).wait_recv()
                if k < p.depth - 1:

                    @pl.when(p.z < p.depth - 1 if direction == 0 else p.z > 0)
                    def _():
                        self.copy_z(direction, k, z).start()

                self.copy_x(z).start()
                self.copy_c(0, z).start()

    def at_distance(self, k, act):
        p = self.p
        if k == 0:
            act(p.z)
            return

        @pl.when(p.z - k >= 0)
        def _():
            act(p.z - k)

        @pl.when(p.z + k < p.depth)
        def _():
            act(p.z + k)

    def x_step(self, k):
        def act(z):
            self.copy_x_in(z).wait_recv()
            self.copy_y_out(z).start()
            self.copy_c(1, z).start()

        self.at_distance(k, act)

    def copy_x_in(self, z):
        at = self.piece(z, 1 - self.p.x, self.p.y)
        return remote(at, at, self.sx.at[self.g, z], self.rx.at[self.g, z], self.p.xn)

    def copy_y_out(self, z):
        return self.copy_y(z)

    def copy_y_in(self, z):
        at = self.piece(z, 1 - self.p.x, 1 - self.p.y)
        return remote(at, at, self.sy.at[self.g, z], self.ry.at[self.g, z], self.p.yn)

    def y_step(self, k):
        def act(z):
            self.copy_y_in(z).wait_recv()
            self.copy_c(2, z).start()

        self.at_distance(k, act)

    def core_in(self, kind, z):
        p = self.p
        at = self.whole.at[ds(((z * 2 + (p.x if kind == 0 else 1 - p.x)) * 2 + 1 - p.c) * self.rows, self.rows, 16)]
        if kind:
            half = p.y if kind == 1 else 1 - p.y
            at = self.whole.at[
                ds(((z * 2 + 1 - p.x) * 2 + 1 - p.c) * self.rows, self.rows, 16),
                ds(half * (self.cols // 2), self.cols // 2),
            ]
        return remote(at, at, self.sc.at[self.g, kind, z], self.rc.at[self.g, kind, z], p.sib)

    def c_step(self):
        self.local().wait()
        for kind in range(3):
            for z in range(self.p.depth):
                self.core_in(kind, z).wait_recv()

    def end(self):
        p = self.p
        for k in range(p.depth - 1):
            @pl.when((p.z < p.depth - 1) & (p.z - k >= 0))
            def _():
                self.copy_z(0, k, p.z - k).wait_send()

            @pl.when((p.z > 0) & (p.z + k < p.depth))
            def _():
                self.copy_z(1, k, p.z + k).wait_send()

        for z in range(p.depth):
            self.copy_x(z).wait_send()
            self.copy_y(z).wait_send()
            for kind in range(3):
                self.copy_c(kind, z).wait_send()

    def steps(self):
        d = self.p.depth
        out = []
        for n in range(d + 2):
            def step(n=n):
                if n < d:
                    self.z_step(n)
                if 0 <= n - 1 < d:
                    self.x_step(n - 1)
                if 0 <= n - 2 < d:
                    self.y_step(n - 2)
            out.append(step)
        out.append(self.c_step)
        return out


def scatter_sems(groups, depth):
    kinds = [(groups, 2), (groups,), (groups,), (groups, 2, depth), (groups,)]
    return [pltpu.SemaphoreType.DMA(k) for k in kinds] * 2 + [pltpu.SemaphoreType.DMA((groups, 2))]


def scatter_buffers(rows, cols, depth):
    return [
        pltpu.VMEM((depth, 2, rows, cols), BF),
        pltpu.VMEM((2, depth, rows, cols), BF),
        pltpu.VMEM((depth, rows, cols // 2), BF),
        pltpu.VMEM((depth, rows, cols // 2), BF),
        pltpu.VMEM((2, depth, rows, cols), BF),
        pltpu.VMEM((rows, cols), BF),
    ]


def add_into(depth, rows, target, other):
    piece = min(rows, 48)
    parts = rows // piece

    def step(i):
        z, at = i // parts, ds(i % parts * piece, piece, 16)
        t = target(z, at)
        t[...] = t[...] + other(z, at)[...]

    loop(depth * parts, step)


class Scatter:
    def __init__(self, place, g, grad, out, buffers, sems):
        self.p, self.g, self.grad, self.out = place, g, grad, out
        self.acc, self.in_c, self.in_y, self.in_x, self.in_z, self.in_f = buffers
        (self.sc, self.sy, self.sx, self.sz, self.sf, self.rc, self.ry, self.rx, self.rz, self.rf, self.own) = sems
        self.depth, _, self.rows, self.cols = self.acc.shape

    def half(self, h):
        return ds(h * (self.cols // 2), self.cols // 2)

    def copy_c(self, x):
        p = self.p
        return remote(self.grad.at[:, x, 1 - p.c], self.in_c.at[x], self.sc.at[self.g, x], self.rc.at[self.g, x], p.sib)

    def load(self, x):
        return pltpu.make_async_copy(self.grad.at[:, x, self.p.c], self.acc.at[:, x], self.own.at[self.g, x])

    def copy_y(self):
        p = self.p
        return remote(
            self.acc.at[:, 1 - p.x, :, self.half(1 - p.y)], self.in_y, self.sy.at[self.g], self.ry.at[self.g], p.yn
        )

    def copy_x(self):
        p = self.p
        return remote(
            self.acc.at[:, 1 - p.x, :, self.half(p.y)], self.in_x, self.sx.at[self.g], self.rx.at[self.g], p.xn
        )

    def copy_z(self, direction, z):
        p = self.p
        return remote(
            self.acc.at[z, p.x],
            self.in_z.at[direction, z],
            self.sz.at[self.g, direction, z],
            self.rz.at[self.g, direction, z],
            p.up if direction == 0 else p.down,
        )

    def copy_f(self):
        p = self.p
        return remote(self.acc.at[p.z, p.x], self.in_f, self.sf.at[self.g], self.rf.at[self.g], p.yn)

    def begin(self):
        for turn in (0, 1):
            x = 1 - self.p.x if turn == 0 else self.p.x
            self.copy_c(x).start()
            self.load(x).start()

    def cores(self, turn):
        p = self.p
        x = 1 - p.x if turn == 0 else p.x
        self.load(x).wait()
        self.copy_c(x).wait_recv()
        add_into(
            self.depth,
            self.rows,
            lambda z, at: self.acc.at[z, x, at],
            lambda z, at: self.in_c.at[x, z, at],
        )
        if turn == 0:
            self.copy_y().start()

    def over_y(self):
        p = self.p
        self.copy_y().wait_recv()
        add_into(
            self.depth,
            self.rows,
            lambda z, at: self.acc.at[z, 1 - p.x, at, self.half(p.y)],
            lambda z, at: self.in_y.at[z, at],
        )
        self.copy_x().start()

    def over_x(self):
        p = self.p
        self.copy_x().wait_recv()
        add_into(
            self.depth,
            self.rows,
            lambda z, at: self.acc.at[z, p.x, at, self.half(p.y)],
            lambda z, at: self.in_x.at[z, at],
        )

    def line(self, wave):
        p, top = self.p, self.depth - 1
        for direction in (0, 1):
            place = p.z if direction == 0 else top - p.z
            if wave == 0:

                @pl.when(place == 0)
                def _(direction=direction):
                    for far in range(top, 0, -1):
                        self.copy_z(direction, far if direction == 0 else top - far).start()

                continue

            @pl.when((place >= 1) & (place <= wave))
            def _(direction=direction, place=place):
                far = top - wave + place
                z = far if direction == 0 else top - far
                self.copy_z(direction, z).wait_recv()
                add_into(
                    1,
                    self.rows,
                    lambda _, at: self.acc.at[z, p.x, at],
                    lambda _, at: self.in_z.at[direction, z, at],
                )

                @pl.when(far > place)
                def _():
                    self.copy_z(direction, z).start()

    def share(self):
        self.copy_f().start()

    def finish(self):
        p = self.p
        self.copy_f().wait_recv()
        piece = min(self.rows, 48)

        def step(i):
            at = ds(i * piece, piece, 16)
            self.out[at, :] = self.acc[p.z, p.x, at, :].astype(F32) + self.in_f[at, :].astype(F32)

        loop(self.rows // piece, step)

    def end(self):
        p, top = self.p, self.depth - 1
        for x in (0, 1):
            self.copy_c(x).wait_send()
        self.copy_y().wait_send()
        self.copy_x().wait_send()
        for direction in (0, 1):
            for z in range(self.depth):

                @pl.when(p.z < z if direction == 0 else p.z > z)
                def _(direction=direction, z=z):
                    self.copy_z(direction, z).wait_send()

        self.copy_f().wait_send()

    def steps(self):
        def over_x_and_line():
            self.over_x()
            self.line(0)

        out = [lambda: self.cores(0), lambda: self.cores(1), self.over_y, over_x_and_line]
        for k in range(1, self.depth):
            out.append(functools.partial(self.line, k))
        out.append(self.share)
        out.append(self.finish)
        return out


def spread(width, owners_rows, parts):
    row = lax.broadcasted_iota(jnp.int32, (width, 1), 0)
    target = row
    for owner in range(1, width // owners_rows):
        target = target + jnp.where(row >= owner * owners_rows, (parts - 1) * owners_rows, 0)
    lane = lax.broadcasted_iota(jnp.int32, (width, width * parts), 1)
    return (lane == target).astype(BF)


def unpack_small(columns, shard, parts, vec, bup):
    rows = columns.astype(F32).T
    vec[...] = rows[:8, :]
    low = rows[8:16, :].astype(BF)
    width = 8 * shard
    place = spread(width, shard, parts)
    for t in range(columns.shape[0] // width):
        wide = nn(low[:, t * width : (t + 1) * width], place)
        total = wide[0:1]
        for i in range(1, parts):
            total = total + pltpu.roll(wide, i * shard, 1)[i : i + 1]
        bup[:, t * width * parts : (t + 1) * width * parts] = total


def pack_small(gv, gbu, shard, parts):
    width = 8 * shard
    model = gv.shape[1]
    place = spread(width, shard, parts)
    rows = []
    for i in range(parts):
        pieces = []
        for t in range(model // width):
            wide = jnp.broadcast_to(gbu[:, t * width * parts : (t + 1) * width * parts], (8, width * parts))
            if i:
                wide = pltpu.roll(wide, width * parts - i * shard, 1)
            pieces.append(nt(wide.astype(BF), place)[0:1])
        rows.append(jnp.concatenate(pieces, axis=1))
    blank = jnp.zeros((BLOCK - 8 - parts, model), F32)
    return jnp.concatenate([gv] + rows + [blank], axis=0).T.astype(BF)


ROWS = 256
CHUNK = 512


def phi_parts(u):
    cdf = 0.5 * (1.0 + lax.erf(u * math.sqrt(0.5)))
    pdf = jnp.exp(-0.5 * u * u) * (1.0 / math.sqrt(2.0 * math.pi))
    return cdf, pdf


def project(x, wa, vec, q, k, v):
    model = x.shape[1]

    def step(rt):
        rows = ds(rt * ROWS, ROWS)
        q[rows, :] = (nn(x[rows, :], wa[:, :model]) + vec[0:1, :]).astype(BF)
        k[rows, :] = nn(x[rows, :], wa[:, model : 2 * model]).astype(BF)
        v[rows, :] = (nn(x[rows, :], wa[:, 2 * model : 3 * model]) + vec[1:2, :]).astype(BF)

    loop(x.shape[0] // ROWS, step)


def ticked(count, step, ticks):
    def body(i):
        step(i)
        for n, tasks in enumerate(ticks):
            if tasks:

                @pl.when(i == n)
                def _(tasks=tasks):
                    for task in tasks:
                        task()

    loop(count, body)


def forward_kernel(depth, parts, *refs):
    (x, seg, sa, so, su, sd, q, k, v, o, probs, vec, bup, wa, wo, wu, wd, bias, *sems) = refs
    length, pairs = seg.shape[1], x.shape[1] // BLOCK
    place = Place(depth)
    ga, go, gu, gd = [
        Gather(place, g, shard, whole, sems)
        for g, (shard, whole) in enumerate(((sa, wa), (so, wo), (su, wu), (sd, wd)))
    ]
    a, b, c, d = ga.steps(), go.steps(), gu.steps(), gd.steps()
    place.barrier()
    for task in [a[0], a[1], b[0], a[2], c[0], a[3], d[0]]:
        task()
    make_bias(seg, bias)
    for task in a[4:]:
        task()
    model = x.shape[1]
    unpack_small(wa[:, 3 * model : 3 * model + BLOCK], sa.shape[0], parts, vec, bup)
    project(x, wa, vec, q, k, v)
    ticks = [[] for _ in range(seg.shape[0] * pairs)]
    order = [b[1], b[2], c[1], b[3], c[2], b[4], c[3], d[1], b[5], c[4], d[2], c[5], d[3]]
    for n, task in enumerate(order):
        ticks[min(n, len(ticks) - 1)].append(task)
    ticked(len(ticks), lambda i: attend_pair(i, length, pairs, q, k, v, o, probs, bias), ticks)
    for task in d[4:6] + [b[6], c[6], d[6]]:
        task()
    for one in (ga, go, gu, gd):
        one.end()


def mid_kernel(*refs):
    (x, o, og, seg, wo, wu, wd, vec, bup, out, pooled, g_down, g_up, g_out, do, dh1, gv, gbu,
     n1s, r1s, z_low, g, sl, df, dh2) = refs
    tokens, model = x.shape
    hidden = wu.shape[1]
    seqs, length = seg.shape
    gv[...] = jnp.zeros_like(gv)
    pooled[...] = jnp.zeros_like(pooled)

    def vrow(i):
        return vec[i : i + 1, :]

    def up(rt):
        rows = ds(rt * ROWS, ROWS)
        h = x[rows, :].astype(F32) + (nn(o[rows, :], wo[...]) + vrow(2))
        c = h - rmean(h)
        r = lax.rsqrt(rmean(c * c) + EPS)
        n = c * r
        n1s[rows, :] = n
        r1s[rows, :] = jnp.broadcast_to(r, (ROWS, BLOCK))
        z_low[rows, :] = (n * vrow(3) + vrow(4)).astype(BF)
        for cc in range(hidden // CHUNK):
            cs = slice(cc * CHUNK, (cc + 1) * CHUNK)
            u = nn(z_low[rows, :], wu[:, cs]) + bup[:, cs]
            cdf, pdf = phi_parts(u)
            g[rows, cs] = (u * cdf).astype(BF)
            sl[rows, cs] = (cdf + u * pdf).astype(BF)

    loop(tokens // ROWS, up)

    def down(rt):
        rows = ds(rt * ROWS, ROWS)
        h = (n1s[rows, :] * vrow(3) + vrow(4)) + (nn(g[rows, :], wd[...]) + vrow(5))
        c = h - rmean(h)
        r = lax.rsqrt(rmean(c * c) + EPS)
        n2 = c * r
        y = n2 * vrow(6) + vrow(7)
        y_low = y.astype(BF)
        out[rows, :] = y_low
        row = rt * ROWS // length
        ids = seg[pl.ds(row, 1), ds(rt * ROWS % length, ROWS)]
        onehot = (ids == lax.broadcasted_iota(jnp.int32, (SEGS, ROWS), 0)).astype(BF)
        pooled[row] = pooled[row] + (nn(onehot, y_low) + nn(onehot, (y - y_low.astype(F32)).astype(BF)))
        dy = og[rows, :].astype(F32)
        gv[6:7, :] += csum(dy * n2)
        gv[7:8, :] += csum(dy)
        e = dy * vrow(6)
        d = r * (e - rmean(e) - n2 * rmean(e * n2))
        dh2[rows, :] = d
        low = d.astype(BF)
        df[rows, :] = low
        gv[5:6, :] += csum(low.astype(F32))

    loop(tokens // ROWS, down)
    for row in range(seqs):
        onehot = (seg[row : row + 1, :] == lax.broadcasted_iota(jnp.int32, (SEGS, length), 0)).astype(F32)
        pooled[row] = pooled[row] / jnp.sum(onehot, axis=1, keepdims=True)

    def down_grad(cc):
        cs = ds(cc * CHUNK, CHUNK)
        g_down[cs, :] = tn(g[:, cs], df[...]).astype(BF)

    loop(hidden // CHUNK, down_grad)

    def up_back(cc):
        cs = ds(cc * CHUNK, CHUNK)
        total = jnp.zeros((1, CHUNK), F32)
        for rt in range(tokens // ROWS):
            rows = slice(rt * ROWS, (rt + 1) * ROWS)
            du = (nt(df[rows, :], wd[cs, :]) * sl[rows, cs].astype(F32)).astype(BF)
            sl[rows, cs] = du
            total += csum(du.astype(F32))
        gbu[:, cs] = total
        g_up[:, cs] = tn(z_low[...], sl[:, cs]).astype(BF)

    loop(hidden // CHUNK, up_back)

    def first_back(rt):
        rows = ds(rt * ROWS, ROWS)
        dz = dh2[rows, :] + nt(sl[rows, :], wu[...])
        n1 = n1s[rows, :]
        gv[3:4, :] += csum(dz * n1)
        gv[4:5, :] += csum(dz)
        e = dz * vrow(3)
        d = r1s[rows, 0:1] * (e - rmean(e) - n1 * rmean(e * n1))
        dh1[rows, :] = d
        da = d.astype(BF)
        df[rows, :] = da
        gv[2:3, :] += csum(da.astype(F32))
        do[rows, :] = nt(da, wo[...]).astype(BF)

    loop(tokens // ROWS, first_back)

    def out_grad_step(cc):
        cs = ds(cc * (model // 2), model // 2)
        g_out[cs, :] = tn(o[:, cs], df[...]).astype(BF)

    loop(2, out_grad_step)


def qkv_grads(x, dqkv, store):
    model = x.shape[1]
    part = model // 2
    for n, d in enumerate(dqkv):

        def step(t, n=n, d=d):
            store(n, t, tn(x[:, ds(t * part, part, BLOCK)], d[...]).astype(BF))

        loop(2, step)


def token_grads(dh1, dqkv, wa, out):
    model = dh1.shape[1]

    def step(rt):
        rows = ds(rt * ROWS, ROWS)
        total = dh1[rows, :]
        for n, d in enumerate(dqkv):
            total = total + nt(d[rows, :], wa[:, n * model : (n + 1) * model])
        out[rows, :] = total.astype(BF)

    loop(dh1.shape[0] // ROWS, step)


def schedule(sizes, begins, gather_gbs=90.0, core_gbs=350.0, delay=1.5):
    import heapq

    free = {"y": 0.0, "x": 0.0, "z": 0.0, "c": 0.0}
    heap, found = [], []

    def send(link, at, size):
        rate = core_gbs if link == "c" else gather_gbs / 2
        start = max(at, free[link])
        free[link] = start + size / rate * 1e-3
        return free[link] + delay

    for g, size in enumerate(sizes):
        heapq.heappush(heap, (begins[g], g, -1))
    while heap:
        at, g, step = heapq.heappop(heap)
        size = sizes[g]
        if step >= 0:
            found.append((at, g, step))
        if step == -1:
            heapq.heappush(heap, (send("c", at, 4 * size), g, 0))
            heapq.heappush(heap, (send("c", at, 4 * size), g, 1))
        elif step == 0:
            heapq.heappush(heap, (send("y", at + 0.5, 2 * size), g, 2))
        elif step == 2:
            heapq.heappush(heap, (send("x", at + 0.5, 2 * size), g, 3))
        elif step in (3, 4, 5):
            heapq.heappush(heap, (send("z", at + 0.5, size), g, step + 1))
        elif step == 6:
            heapq.heappush(heap, (at + 0.2, g, 7))
        elif step == 7:
            heapq.heappush(heap, (send("y", at, size), g, 8))
    return found


def backward_kernel(depth, parts, length, cuts, *refs):
    count = len(cuts)
    (q, k, v, do, probs, x, dh1, wa, g_down, g_up, g_out, gv, gbu, gtok, oa, oo, ou, od, small,
     dq, dk, dv, dk_sum, dv_sum, g_all, *rest) = refs
    sets = [rest[6 * n : 6 * n + 6] for n in range(count)]
    sems = rest[6 * count :]
    pairs = x.shape[1] // BLOCK
    model = x.shape[1]
    place = Place(depth)
    sources = {"a": (g_all, oa), "o": (g_out, oo), "u": (g_up, ou), "d": (g_down, od)}
    scatters = []
    for n, (name, r0, rows, c0, cols) in enumerate(cuts):
        grad, out = sources[name]
        scatters.append(
            Scatter(place, n, grad.at[:, :, :, r0 : r0 + rows, c0 : c0 + cols], out.at[r0 : r0 + rows, c0 : c0 + cols], sets[n], sems)
        )
    steps = [s.steps() for s in scatters]
    early = [n for n, cut in enumerate(cuts) if cut[0] != "a"]
    late = [n for n, cut in enumerate(cuts) if cut[0] == "a"]
    iterations = x.shape[0] // length * pairs
    per, tail = 2.3, 8.0
    begins = [0.0 if n in early else per * iterations + tail for n in range(count)]
    sizes = [rows * cols * 2 for _, _, rows, _, cols in cuts]
    found = schedule(sizes, begins)
    ticks = [[] for _ in range(iterations)]
    after = []
    for at, g, step in found:
        n = int(at // per)
        (ticks[n] if n < iterations else after).append(steps[g][step])
    place.barrier()
    for n in early:
        scatters[n].begin()
    ticked(
        iterations,
        lambda i: attend_back_pair(i, length, pairs, q, k, v, do, probs, dq, dk, dv, dk_sum, dv_sum),
        ticks,
    )
    half = model // 2
    owners = half // oo.shape[0]

    def store(n, t, value):
        shaped = value.reshape(owners // 4, 2, 2, oo.shape[0], model)
        g_all[pl.ds(t * (owners // 4), owners // 4), :, :, :, n * model : (n + 1) * model] = shaped

    qkv_grads(x, (dq, dk, dv), store)
    bq, bv = csum(dq[...].astype(F32)), csum(dv[...].astype(F32))
    vectors = jnp.concatenate([bq, bv, gv[2:8, :]], axis=0)
    columns = pack_small(vectors, gbu[...], oo.shape[0], parts)
    shaped = columns.reshape(depth, 2, 2, oo.shape[0], BLOCK)
    g_all[:, :, :, :, 3 * model : 3 * model + BLOCK] = shaped
    g_all[:, :, :, :, 3 * model + BLOCK :] = jnp.zeros_like(shaped)
    for n in late:
        scatters[n].begin()
    token_grads(dh1, (dq, dk, dv), wa, gtok)
    for task in after:
        task()
    for s in scatters:
        s.end()
    last = oa[:, 3 * model : 3 * model + BLOCK]
    square = jnp.concatenate([last, jnp.zeros((BLOCK - last.shape[0], BLOCK), F32)], axis=0).T
    small[...] = square[:16, :]


V = pl.BlockSpec(memory_space=pltpu.VMEM)
ANY = pl.BlockSpec(memory_space=pl.ANY)
sds = jax.ShapeDtypeStruct


def params(collective_id=None):
    if collective_id is None:
        return pltpu.CompilerParams(vmem_limit_bytes=VMEM_LIMIT)
    return pltpu.CompilerParams(
        vmem_limit_bytes=VMEM_LIMIT, collective_id=collective_id, has_side_effects=True
    )


def run_forward(depth, x, seg, sa, so, su, sd):
    tokens, model = x.shape
    owners = depth * 4
    hidden = su.shape[1]
    parts = hidden // model
    seqs, length = seg.shape
    band = key_windows(length)[2]
    act = sds((tokens, model), BF)
    wholes = [sds((owners * s.shape[0], s.shape[1]), BF) for s in (sa, so, su, sd)]
    return pl.pallas_call(
        functools.partial(forward_kernel, depth, parts),
        out_shape=(act, act, act, act, sds((seqs * model // BLOCK, band, 2 * BLOCK), BF),
                   sds((8, model), F32), sds((1, hidden), F32), *wholes),
        in_specs=[V, V, ANY, ANY, ANY, ANY],
        out_specs=(V,) * 8 + (ANY,) * 3,
        scratch_shapes=[pltpu.VMEM((seqs, band, BLOCK), F32)] + gather_sems(4, depth),
        compiler_params=params(0),
        name="forward",
    )(x, seg, sa, so, su, sd)


def run_mid(x, o, og, seg, wo, wu, wd, vec, bup):
    tokens, model = x.shape
    hidden = wu.shape[1]
    wide = pltpu.VMEM((tokens, hidden), BF)
    act = sds((tokens, model), BF)
    return pl.pallas_call(
        mid_kernel,
        out_shape=(act, sds((seg.shape[0], SEGS, model), F32), sds(wd.shape, BF), sds(wu.shape, BF), sds(wo.shape, BF),
                   act, sds((tokens, model), F32), sds((8, model), F32), sds((1, hidden), F32)),
        in_specs=[V] * 9,
        out_specs=(V,) * 9,
        scratch_shapes=[pltpu.VMEM((tokens, model), F32), pltpu.VMEM((tokens, BLOCK), F32), pltpu.VMEM((tokens, model), BF),
                        wide, wide, pltpu.VMEM((tokens, model), BF), pltpu.VMEM((tokens, model), F32)],
        compiler_params=params(),
        name="middle",
    )(x, o, og, seg, wo, wu, wd, vec, bup)


def run_backward(depth, length, shards, q, k, v, do, probs, x, dh1, wa, g_down, g_up, g_out, gv, gbu):
    tokens, model = x.shape
    sa, so, su, sd = shards
    parts = su[1] // model

    def owned(t, s):
        return t.reshape(depth, 2, 2, *s)

    cuts = [("o", 0, so[0], 0, so[1])]
    for part in range(2):
        cuts.append(("d", part * (sd[0] // 2), sd[0] // 2, 0, sd[1]))
    for part in range(2):
        cuts.append(("u", 0, su[0], part * (su[1] // 2), su[1] // 2))
    for part in range(2):
        cuts.append(("a", 0, sa[0], part * (sa[1] // 2), sa[1] // 2))
    buffers = []
    for _, _, rows, _, cols in cuts:
        buffers += scatter_buffers(rows, cols, depth)
    act = pltpu.VMEM((tokens, model), BF)
    half_sum = pltpu.VMEM((length, BLOCK), F32)
    return pl.pallas_call(
        functools.partial(backward_kernel, depth, parts, length, tuple(cuts)),
        out_shape=(sds((tokens, model), BF), sds(sa, F32), sds(so, F32), sds(su, F32), sds(sd, F32), sds((16, BLOCK), F32)),
        in_specs=[V] * 8 + [ANY] * 3 + [V] * 2,
        out_specs=(V,) * 6,
        scratch_shapes=[act, act, act, half_sum, half_sum, pltpu.VMEM((depth, 2, 2, *sa), BF), *buffers,
                        *scatter_sems(len(cuts), depth)],
        compiler_params=params(1),
        name="backward",
    )(q, k, v, do, probs, x, dh1, wa, owned(g_down, sd), owned(g_up, su), owned(g_out, so), gv, gbu)


def local_ring(depth, *args):
    (tokens, segments, w_query, b_query, w_key, w_value, b_value, w_out, b_out, gain1, shift1, w_up, b_up, w_down,
     b_down, gain2, shift2, out_grad) = args
    seqs, length, model = tokens.shape
    shard = w_query.shape[0]
    parts = w_up.shape[1] // model
    x = tokens.reshape(seqs * length, model)
    og = out_grad.reshape(seqs * length, model)
    small = jnp.stack([b_query, b_value, b_out, gain1, shift1, b_down, gain2, shift2] + [
        b_up[i * shard : (i + 1) * shard] for i in range(parts)
    ], axis=1)
    small = jnp.pad(small, ((0, 0), (0, 2 * BLOCK - 8 - parts)))
    sa = jnp.concatenate([w_query, w_key, w_value, small], axis=1)
    q, k, v, o, probs, vec, bup, wa, wo, wu, wd = run_forward(depth, x, segments, sa, w_out, w_up, w_down)
    out, pooled, g_down, g_up, g_out, do, dh1, gv, gbu = run_mid(x, o, og, segments, wo, wu, wd, vec, bup)
    gtok, ga, go, gu, gd, gs = run_backward(
        depth, length, (sa.shape, w_out.shape, w_up.shape, w_down.shape),
        q, k, v, do, probs, x, dh1, wa, g_down, g_up, g_out, gv, gbu,
    )
    vectors = [gs[i, :shard] for i in range(8)]
    gbq, gbv, gbo, gg1, gs1, gbd, gg2, gs2 = vectors
    gb_up = gs[8 : 8 + parts, :shard].reshape(parts * shard)
    return (
        out.reshape(tokens.shape), pooled, gtok.reshape(tokens.shape),
        ga[:, :model], gbq, ga[:, model : 2 * model], ga[:, 2 * model : 3 * model], gbv,
        go, gbo, gg1, gs1, gu, gb_up, gd, gbd, gg2, gs2,
    )


def qkv_kernel(x, wa, vec, seg, q, k, v, o, probs, bias):
    length, pairs = seg.shape[1], x.shape[1] // BLOCK
    make_bias(seg, bias)
    project(x, wa, vec, q, k, v)
    loop(seg.shape[0] * pairs, lambda i: attend_pair(i, length, pairs, q, k, v, o, probs, bias))


def back_kernel(length, q, k, v, do, probs, x, dh1, wa, gtok, g_qkv, gb, dq, dk, dv, dk_sum, dv_sum):
    pairs, model = x.shape[1] // BLOCK, x.shape[1]
    loop(
        x.shape[0] // length * pairs,
        lambda i: attend_back_pair(i, length, pairs, q, k, v, do, probs, dq, dk, dv, dk_sum, dv_sum),
    )

    def store(n, t, value):
        g_qkv[ds(t * (model // 2), model // 2), n * model : (n + 1) * model] = value

    qkv_grads(x, (dq, dk, dv), store)
    token_grads(dh1, (dq, dk, dv), wa, gtok)
    gb[...] = jnp.concatenate([csum(dq[...].astype(F32)), csum(dv[...].astype(F32)), jnp.zeros((6, model), F32)], axis=0)


def local_plain(*args):
    (tokens, segments, w_query, b_query, w_key, w_value, b_value, w_out, b_out, gain1, shift1, w_up, b_up, w_down,
     b_down, gain2, shift2, out_grad) = args
    seqs, length, model = tokens.shape
    count = seqs * length
    band = key_windows(length)[2]
    x = tokens.reshape(count, model)
    og = out_grad.reshape(count, model)

    def gathered(t):
        return lax.all_gather(t, "fsdp", axis=0, tiled=True)

    wa = gathered(jnp.concatenate([w_query, w_key, w_value], axis=1))
    small = gathered(jnp.stack([b_query, b_value, b_out, gain1, shift1, b_down, gain2, shift2], axis=1))
    vec = small.T.astype(F32)
    bup = gathered(b_up).astype(F32)[None]
    wo, wu, wd = gathered(w_out), gathered(w_up), gathered(w_down)
    act = sds((count, model), BF)
    q, k, v, o, probs = pl.pallas_call(
        qkv_kernel,
        out_shape=(act, act, act, act, sds((seqs * model // BLOCK, band, 2 * BLOCK), BF)),
        in_specs=[V] * 4,
        out_specs=(V,) * 5,
        scratch_shapes=[pltpu.VMEM((seqs, band, BLOCK), F32)],
        compiler_params=params(),
        name="attention",
    )(x, wa, vec, segments)
    out, pooled, g_down, g_up, g_out, do, dh1, gv, gbu = run_mid(x, o, og, segments, wo, wu, wd, vec, bup)
    kept = pltpu.VMEM((count, model), BF)
    part = pltpu.VMEM((length, BLOCK), F32)
    gtok, g_qkv, gb = pl.pallas_call(
        functools.partial(back_kernel, length),
        out_shape=(act, sds((model, 3 * model), BF), sds((8, model), F32)),
        in_specs=[V] * 8,
        out_specs=(V,) * 3,
        scratch_shapes=[kept, kept, kept, part, part],
        compiler_params=params(),
        name="attention_back",
    )(q, k, v, do, probs, x, dh1, wa)
    vectors = jnp.concatenate([gb[:2], gv[2:8]], axis=0).T

    def shared(t):
        mine = lax.psum_scatter(t.astype(F32), "fsdp", scatter_dimension=0, tiled=True)
        return lax.psum(mine.astype(BF), "rep").astype(F32)

    ga, gs = shared(g_qkv), shared(vectors)
    go, gu, gd, gb_up = shared(g_out), shared(g_up), shared(g_down), shared(gbu[0])
    gbq, gbv, gbo, gg1, gs1, gbd, gg2, gs2 = [gs[:, i] for i in range(8)]
    return (
        out.reshape(tokens.shape), pooled, gtok.reshape(tokens.shape),
        ga[:, :model], gbq, ga[:, model : 2 * model], ga[:, 2 * model :], gbv,
        go, gbo, gg1, gs1, gu, gb_up, gd, gbd, gg2, gs2,
    )


def solution(mesh):
    rows = P(("fsdp", "rep"))
    split = P("fsdp")
    placed = (rows, rows) + (split,) * 15 + (rows,)
    results = (rows,) * 3 + (split,) * 15
    owners = mesh.shape["fsdp"]

    def whole(*args):
        shard = args[2].shape[0] // owners
        ring = owners % 4 == 0 and mesh.shape["rep"] == 2 and shard % 16 == 0
        body = functools.partial(local_ring, owners // 4) if ring else local_plain
        return jax.shard_map(body, mesh=mesh, in_specs=placed, out_specs=results, check_vma=False)(*args)

    return whole
```

time: 1160 us -> 278 us (0.24); the launches traced: 1140 us -> 278 us
  waiting for transfers between devices: 430 us -> 0 us
  matrix products: 408 us -> 0 us
  Pallas kernels: 0 us -> 264 us
  blocking collectives: 128 us -> 0 us
  local copies, waits for them, and re-layouts: 116 us -> 11.5 us
  other arithmetic: 36.6 us -> 1.67 us
  between operations: 18.1 us -> 0.68 us
    dot_general x206 -> x0, matrix products: 408 us -> none  [the longest x60 153 us: product(): return jnp.dot(left, right, preferred_element_type=jnp.float32)]
    reduce_scatter x3 -> x0, waiting for transfers between devices: 291 us -> none  [the longest x1 114 us: local(): lax.psum_scatter(grad_w_down, 'fsdp', scatter_dimension=0, tiled=True)]
    pallas_call x0 -> x3, Pallas kernels: none -> 264 us  [the longest x1 107 us: run_backward(): pl.pallas_call(functools.partial(backward_kernel, depth, parts, length, t...]
    unnamed x2 -> x0, blocking collectives: 123 us -> none
    unnamed x16 -> x0, waiting for transfers between devices: 64.7 us -> none
    psum x1 -> x0, waiting for transfers between devices: 41.9 us -> none  [local(): lax.psum(share_total[0].astype(jnp.bfloat16), 'rep').astype(jnp.float32)]
    unnamed x157 -> x10, local copies, waits for them, and re-layouts: 40.3 us -> 5.06 us
    dynamic_slice x72 -> x0, local copies, waits for them, and re-layouts: 35.1 us -> none  [the longest x48 17.6 us: local(): lax.map(head_forward, (query_heads, key_heads, value_heads, head_segments))]
  transfers between devices with their start and end apart: 13 -> 0, of which waited for: 7 -> 0; matrix products, arithmetic and copies ran while one was open for 22% -> 0% of each run, Pallas kernels for 0% -> 0%
where the time goes in v1:
time: 278 us
  Pallas kernels  264 us (95%)
  local copies, waits for them, and re-layouts  11.5 us (4%)
    pallas_call x1, Pallas kernels, run_backward(): pl.pallas_call(functools.partial(backward_kernel, depth, parts, length, t...  107 us
    pallas_call x1, Pallas kernels, run_forward(): pl.pallas_call(functools.partial(forward_kernel, depth, parts), out_shape...  93.6 us
    pallas_call x1, Pallas kernels, run_mid(): pl.pallas_call(mid_kernel, out_shape=(act, sds((seg.shape[0], SEGS, model...  63.1 us

profile of v1, /device:TPU:0, one launch (start us, length us, event | category | flops | bytes accessed | tf_op | source)
XLA Modules:
  0.0 277.8 jit_solution(11399368906971891480)
XLA Ops:
  0.7 0.9 slice_bitcast_fusion.8
  1.5 0.8 stack.51
  2.4 0.1 copy.48
  2.5 1.7 fusion.1.refs_2_
  4.1 93.6 %forward.1 = (bf16[1024,768]{1,0:T(8,128)(2,1)}, bf16[1024,768]{1,0:T(8,128)(2,1)}, bf16[1024,768]{1,0:T(8,128)(2,1)}, bf16[1024,768]{1,0:T(8,128)(2,1)}, bf16[1...) custom-call(bf16[1024,768]{1,0:T(8,128)(2,1)} %bitcast.39, ...), custom_call_target="tpu_custom_call" | custom-call | tf_op jit(solution)/shard_map/forward/pallas_call | solution.py:896
  97.8 63.1 %middle.1 = (bf16[1024,768]{1,0:T(8,128)(2,1)}, f32[2,8,768]{2,1,0:T(8,128)}, bf16[3072,768]{1,0:T(8,128)(2,1)}, bf16[768,3072]{1,0:T(8,128)(2,1)}, bf16[768,768...) custom-call(bf16[1024,768]{1,0:T(8,128)(2,1)} %bitcast.40, ...), custom_call_target="tpu_custom_call" | custom-call | tf_op jit(solution)/shard_map/middle/pallas_call | solution.py:913
  160.8 107.3 %backward.1 = (bf16[1024,768]{1,0:T(8,128)(2,1)}, f32[48,2560]{1,0:T(8,128)}, f32[48,768]{1,0:T(8,128)}, f32[48,3072]{1,0:T(8,128)}, f32[192,768]{1,0:T(8,128)}, /*index=5*/f32[16,128]{1,0:T(8,128)}) custom-call(bf16[1024,768]{1,0:T(8,128)(2,1)} %get-tuple-element.52.refs_0_, bf16[1024,768]{1,0:T(8,128)(2,1)} %get-tuple-element.53.refs_1_, ...), custom_call_target="tpu_custom_call" | custom-call | tf_op jit(solution)/shard_map/backward/pallas_call | solution.py:946
  268.1 0.7 slice.60
  268.8 1.5 slice_bitcast_fusion
  270.3 0.6 reshape.67
  270.9 1.8 fusion.2
  272.8 0.0 copy-start.2
  272.8 0.0 copy-start.1
  272.8 0.0 copy-start
  272.8 2.8 copy.53
  275.5 0.0 copy-done.2
  275.5 0.7 copy.54
  276.2 0.0 copy-done.1
  276.2 0.8 copy.55
  277.0 0.0 copy-done
  277.0 0.8 copy.56
Async XLA Ops:
  272.8 2.8 copy-start.2
  272.8 3.4 %copy-start.1 = (f32[48,3072]{1,0:T(8,128)S(1)}, f32[48,3072]{1,0:T(8,128)}, u32[]{:S(2)}) copy-start(f32[48,3072]{1,0:T(8,128)} %get-tuple-element.115) | copy-start | bytes 1769476
  272.8 4.2 %copy-start = (f32[192,768]{1,0:T(8,128)S(1)}, f32[192,768]{1,0:T(8,128)}, u32[]{:S(2)}) copy-start(f32[192,768]{1,0:T(8,128)} %get-tuple-element.117) | copy-start | bytes 1769476

commit v2 on v1

--- a/solution.py
+++ b/solution.py
@@ -1,4 +1,5 @@
 import functools
+import heapq
 import math
 
 import jax
@@ -16,7 +17,7 @@
 EPS = 1e-5
 MASKED = -1e30
 MESH = pl.DeviceIdType.MESH
-VMEM_LIMIT = 61 * 2**20
+VMEM_LIMIT = int(63.5 * 2**20)
 
 
 def nn(a, b):
@@ -76,50 +77,48 @@
     return jnp.concatenate([both[:HEAD, :BLOCK], both[HEAD:, BLOCK:]], axis=0).T
 
 
-def make_bias(seg, bias):
+def make_bias(seg, bias_at):
     rows, length = seg.shape
-    spans, offsets, _ = key_windows(length)
+    spans, _, _ = key_windows(length)
     for row in range(rows):
         ids = seg[row : row + 1, :].astype(F32)
         keys = jnp.broadcast_to(ids, (BLOCK, length)).T
         for qb, (k0, k1) in enumerate(spans):
             same = keys[k0 * BLOCK : k1 * BLOCK, :] == ids[:, qb * BLOCK : (qb + 1) * BLOCK]
-            bias[row, offsets[qb] : offsets[qb] + (k1 - k0) * BLOCK, :] = jnp.where(
-                same, 0.0, MASKED
-            )
-
-
-def attend_pair(i, length, pairs, q, k, v, o, probs, bias):
-    spans, offsets, _ = key_windows(length)
+            bias_at(row, qb)[...] = jnp.where(same, 0.0, MASKED)
+
+
+def attend_pair(i, length, pairs, q, k, v, o, probs_at, bias_at):
+    spans, _, _ = key_windows(length)
     row, pair = i // pairs, i % pairs
     r0, c = pl.multiple_of(row * length, length), ds(pair * BLOCK, BLOCK)
     vt = v[pl.ds(r0, length), c].T
     for qb, (k0, k1) in enumerate(spans):
-        n, at = (k1 - k0) * BLOCK, offsets[qb]
+        n = (k1 - k0) * BLOCK
         mine = pl.ds(r0 + qb * BLOCK, BLOCK)
         q2 = stack2(q[mine, c] * BF(HEAD**-0.5))
         s = nt(k[pl.ds(r0 + k0 * BLOCK, n), c], q2)
-        b = bias[row, at : at + n, :]
+        b = bias_at(row, qb)[...]
         s = s + jnp.concatenate([b, b], axis=1)
         e = jnp.exp(s - jnp.max(s, axis=0, keepdims=True))
         p = (e * (1.0 / jnp.sum(e, axis=0, keepdims=True))).astype(BF)
-        probs[i, at : at + n, :] = p
+        probs_at(i, qb)[...] = p
         o[mine, c] = unstack_t(nn(vt[:, k0 * BLOCK : k1 * BLOCK], p)).astype(BF)
 
 
-def attend_back_pair(i, length, pairs, q, k, v, do, probs, dq, dk, dv, dk_sum, dv_sum):
-    spans, offsets, _ = key_windows(length)
+def attend_back_pair(i, length, pairs, q, k, v, do, probs_at, dq, dk, dv, dk_sum, dv_sum):
+    spans, _, _ = key_windows(length)
     last = len(spans) - 1
     row, pair = i // pairs, i % pairs
     r0, c = pl.multiple_of(row * length, length), ds(pair * BLOCK, BLOCK)
     kt = k[pl.ds(r0, length), c].T
     for qb, (k0, k1) in enumerate(spans):
-        n, at = (k1 - k0) * BLOCK, offsets[qb]
+        n = (k1 - k0) * BLOCK
         mine = pl.ds(r0 + qb * BLOCK, BLOCK)
         q2 = stack2(q[mine, c] * BF(HEAD**-0.5))
         do2 = stack2(do[mine, c])
         dp = nt(v[pl.ds(r0 + k0 * BLOCK, n), c], do2)
-        low = probs[i, at : at + n, :]
+        low = probs_at(i, qb)[...]
         p = low.astype(F32)
         d_s = (p * (dp - jnp.sum(p * dp, axis=0, keepdims=True))).astype(BF)
         dv_part = nn(low, do2)
@@ -192,16 +191,15 @@
         self.p, self.g, self.shard, self.whole = place, g, shard, whole
         self.sz, self.sx, self.sy, self.sc, self.rz, self.rx, self.ry, self.rc, self.own = sems
         self.rows, self.cols = shard.shape
+        self.done = False
 
     def piece(self, z, x, half=None):
-        f = (z * 2 + x) * 2 + self.p.c
-        at = self.whole.at[ds(f * self.rows, self.rows, 16)]
+        return self.piece_of(z, x, self.p.c, half)
+
+    def piece_of(self, z, x, c, half=None):
         if half is None:
-            return at
-        return self.whole.at[ds(f * self.rows, self.rows, 16), ds(half * (self.cols // 2), self.cols // 2)]
-
-    def piece_of(self, z, x, c):
-        return self.whole.at[ds(((z * 2 + x) * 2 + c) * self.rows, self.rows, 16)]
+            return self.whole.at[z, x, c]
+        return self.whole.at[z, x, c, :, ds(half * (self.cols // 2), self.cols // 2)]
 
     def copy_z(self, direction, distance, z, src=None):
         dst = self.piece(z, self.p.x)
@@ -313,16 +311,14 @@
 
     def core_in(self, kind, z):
         p = self.p
-        at = self.whole.at[ds(((z * 2 + (p.x if kind == 0 else 1 - p.x)) * 2 + 1 - p.c) * self.rows, self.rows, 16)]
-        if kind:
-            half = p.y if kind == 1 else 1 - p.y
-            at = self.whole.at[
-                ds(((z * 2 + 1 - p.x) * 2 + 1 - p.c) * self.rows, self.rows, 16),
-                ds(half * (self.cols // 2), self.cols // 2),
-            ]
+        if kind == 0:
+            at = self.piece_of(z, p.x, 1 - p.c)
+        else:
+            at = self.piece_of(z, 1 - p.x, 1 - p.c, p.y if kind == 1 else 1 - p.y)
         return remote(at, at, self.sc.at[self.g, kind, z], self.rc.at[self.g, kind, z], p.sib)
 
     def c_step(self):
+        self.done = True
         self.local().wait()
         for kind in range(3):
             for z in range(self.p.depth):
@@ -362,17 +358,16 @@
 
 
 def scatter_sems(groups, depth):
-    kinds = [(groups, 2), (groups,), (groups,), (groups, 2, depth), (groups,)]
+    kinds = [(groups, 2), (groups,), (groups,), (groups, 2, depth - 1), (groups,)]
     return [pltpu.SemaphoreType.DMA(k) for k in kinds] * 2 + [pltpu.SemaphoreType.DMA((groups, 2))]
 
 
 def scatter_buffers(rows, cols, depth):
     return [
-        pltpu.VMEM((depth, 2, rows, cols), BF),
         pltpu.VMEM((2, depth, rows, cols), BF),
         pltpu.VMEM((depth, rows, cols // 2), BF),
         pltpu.VMEM((depth, rows, cols // 2), BF),
-        pltpu.VMEM((2, depth, rows, cols), BF),
+        pltpu.VMEM((2, depth - 1, rows, cols), BF),
         pltpu.VMEM((rows, cols), BF),
     ]
 
@@ -390,11 +385,11 @@
 
 
 class Scatter:
-    def __init__(self, place, g, grad, out, buffers, sems):
-        self.p, self.g, self.grad, self.out = place, g, grad, out
-        self.acc, self.in_c, self.in_y, self.in_x, self.in_z, self.in_f = buffers
-        (self.sc, self.sy, self.sx, self.sz, self.sf, self.rc, self.ry, self.rx, self.rz, self.rf, self.own) = sems
-        self.depth, _, self.rows, self.cols = self.acc.shape
+    def __init__(self, place, g, grad, landing, buffers, sems):
+        self.p, self.g, self.grad, self.landing = place, g, grad, landing
+        self.in_c, self.in_y, self.in_x, self.in_z, self.in_f = buffers
+        (self.sc, self.sy, self.sx, self.sz, self.sf, self.rc, self.ry, self.rx, self.rz, self.rf, self.out) = sems
+        _, self.depth, self.rows, self.cols = self.in_c.shape
 
     def half(self, h):
         return ds(h * (self.cols // 2), self.cols // 2)
@@ -403,50 +398,44 @@
         p = self.p
         return remote(self.grad.at[:, x, 1 - p.c], self.in_c.at[x], self.sc.at[self.g, x], self.rc.at[self.g, x], p.sib)
 
-    def load(self, x):
-        return pltpu.make_async_copy(self.grad.at[:, x, self.p.c], self.acc.at[:, x], self.own.at[self.g, x])
-
     def copy_y(self):
         p = self.p
         return remote(
-            self.acc.at[:, 1 - p.x, :, self.half(1 - p.y)], self.in_y, self.sy.at[self.g], self.ry.at[self.g], p.yn
+            self.grad.at[:, 1 - p.x, p.c, :, self.half(1 - p.y)], self.in_y, self.sy.at[self.g], self.ry.at[self.g], p.yn
         )
 
     def copy_x(self):
         p = self.p
         return remote(
-            self.acc.at[:, 1 - p.x, :, self.half(p.y)], self.in_x, self.sx.at[self.g], self.rx.at[self.g], p.xn
+            self.grad.at[:, 1 - p.x, p.c, :, self.half(p.y)], self.in_x, self.sx.at[self.g], self.rx.at[self.g], p.xn
         )
 
-    def copy_z(self, direction, z):
+    def copy_z(self, direction, z, slot):
         p = self.p
         return remote(
-            self.acc.at[z, p.x],
-            self.in_z.at[direction, z],
-            self.sz.at[self.g, direction, z],
-            self.rz.at[self.g, direction, z],
+            self.grad.at[z, p.x, p.c],
+            self.in_z.at[direction, slot],
+            self.sz.at[self.g, direction, slot],
+            self.rz.at[self.g, direction, slot],
             p.up if direction == 0 else p.down,
         )
 
     def copy_f(self):
         p = self.p
-        return remote(self.acc.at[p.z, p.x], self.in_f, self.sf.at[self.g], self.rf.at[self.g], p.yn)
+        return remote(self.grad.at[p.z, p.x, p.c], self.in_f, self.sf.at[self.g], self.rf.at[self.g], p.yn)
 
     def begin(self):
-        for turn in (0, 1):
-            x = 1 - self.p.x if turn == 0 else self.p.x
-            self.copy_c(x).start()
-            self.load(x).start()
+        self.copy_c(1 - self.p.x).start()
+        self.copy_c(self.p.x).start()
 
     def cores(self, turn):
         p = self.p
         x = 1 - p.x if turn == 0 else p.x
-        self.load(x).wait()
         self.copy_c(x).wait_recv()
         add_into(
             self.depth,
             self.rows,
-            lambda z, at: self.acc.at[z, x, at],
+            lambda z, at: self.grad.at[z, x, p.c, at],
             lambda z, at: self.in_c.at[x, z, at],
         )
         if turn == 0:
@@ -458,7 +447,7 @@
         add_into(
             self.depth,
             self.rows,
-            lambda z, at: self.acc.at[z, 1 - p.x, at, self.half(p.y)],
+            lambda z, at: self.grad.at[z, 1 - p.x, p.c, at, self.half(p.y)],
             lambda z, at: self.in_y.at[z, at],
         )
         self.copy_x().start()
@@ -469,7 +458,7 @@
         add_into(
             self.depth,
             self.rows,
-            lambda z, at: self.acc.at[z, p.x, at, self.half(p.y)],
+            lambda z, at: self.grad.at[z, p.x, p.c, at, self.half(p.y)],
             lambda z, at: self.in_x.at[z, at],
         )
 
@@ -482,7 +471,7 @@
                 @pl.when(place == 0)
                 def _(direction=direction):
                     for far in range(top, 0, -1):
-                        self.copy_z(direction, far if direction == 0 else top - far).start()
+                        self.copy_z(direction, far if direction == 0 else top - far, far - 1).start()
 
                 continue
 
@@ -490,31 +479,41 @@
             def _(direction=direction, place=place):
                 far = top - wave + place
                 z = far if direction == 0 else top - far
-                self.copy_z(direction, z).wait_recv()
+                slot = top - wave
+                self.copy_z(direction, z, slot).wait_recv()
                 add_into(
                     1,
                     self.rows,
-                    lambda _, at: self.acc.at[z, p.x, at],
-                    lambda _, at: self.in_z.at[direction, z, at],
+                    lambda _, at: self.grad.at[z, p.x, p.c, at],
+                    lambda _, at: self.in_z.at[direction, slot, at],
                 )
-
-                @pl.when(far > place)
-                def _():
-                    self.copy_z(direction, z).start()
+                if slot > 0:
+                    self.copy_z(direction, z, slot - 1).start()
 
     def share(self):
         self.copy_f().start()
+
+    def copy_out(self, n):
+        view, result = self.landing[n]
+        return pltpu.make_async_copy(view, result, self.out.at[self.g, n])
 
     def finish(self):
         p = self.p
         self.copy_f().wait_recv()
         piece = min(self.rows, 48)
-
-        def step(i):
-            at = ds(i * piece, piece, 16)
-            self.out[at, :] = self.acc[p.z, p.x, at, :].astype(F32) + self.in_f[at, :].astype(F32)
-
-        loop(self.rows // piece, step)
+        c0 = 0
+        for n, (view, result) in enumerate(self.landing):
+            cols = view.shape[1]
+
+            def step(i, view=view, c0=c0, cols=cols):
+                at = ds(i * piece, piece, 16)
+                cs = pl.ds(c0, cols)
+                view[at, :] = self.grad[p.z, p.x, p.c, at, cs].astype(F32) + self.in_f[at, cs].astype(F32)
+
+            loop(self.rows // piece, step)
+            if result is not None:
+                self.copy_out(n).start()
+            c0 += cols
 
     def end(self):
         p, top = self.p, self.depth - 1
@@ -523,13 +522,17 @@
         self.copy_y().wait_send()
         self.copy_x().wait_send()
         for direction in (0, 1):
-            for z in range(self.depth):
-
-                @pl.when(p.z < z if direction == 0 else p.z > z)
-                def _(direction=direction, z=z):
-                    self.copy_z(direction, z).wait_send()
+            place = p.z if direction == 0 else top - p.z
+            for slot in range(top):
+
+                @pl.when(place + slot < top)
+                def _(direction=direction, slot=slot):
+                    self.copy_z(direction, 0, slot).wait_send()
 
         self.copy_f().wait_send()
+        for n, (_, result) in enumerate(self.landing):
+            if result is not None:
+                self.copy_out(n).wait()
 
     def steps(self):
         def over_x_and_line():
@@ -537,11 +540,9 @@
             self.line(0)
 
         out = [lambda: self.cores(0), lambda: self.cores(1), self.over_y, over_x_and_line]
-        for k in range(1, self.depth):
-            out.append(functools.partial(self.line, k))
-        out.append(self.share)
-        out.append(self.finish)
-        return out
+        for wave in range(1, self.depth):
+            out.append(functools.partial(self.line, wave))
+        return out + [self.share, self.finish]
 
 
 def spread(width, owners_rows, parts):
@@ -594,6 +595,485 @@
     return cdf, pdf
 
 
+V = pl.BlockSpec(memory_space=pltpu.VMEM)
+ANY = pl.BlockSpec(memory_space=pl.ANY)
+sds = jax.ShapeDtypeStruct
+
+
+def params(collective_id=None):
+    if collective_id is None:
+        return pltpu.CompilerParams(vmem_limit_bytes=VMEM_LIMIT)
+    return pltpu.CompilerParams(
+        vmem_limit_bytes=VMEM_LIMIT, collective_id=collective_id, has_side_effects=True
+    )
+
+
+class Links:
+    rate = {"c": 350.0, "x": 45.0, "y": 45.0, "z": 45.0}
+    lag = 1.5
+
+    def __init__(self):
+        self.free = dict.fromkeys(self.rate, 0.0)
+        self.heap = []
+        self.count = 0
+
+    def send(self, link, at, size):
+        self.free[link] = max(at, self.free[link]) + size / self.rate[link] * 1e-3
+        return self.free[link] + self.lag
+
+    def push(self, at, task, then=None):
+        self.count += 1
+        heapq.heappush(self.heap, (at, self.count, task, then))
+
+    def gather(self, gather, at):
+        size = gather.rows * gather.cols * 2
+        depth = gather.p.depth
+
+        def zed(k):
+            def then(now):
+                if k < depth - 1:
+                    self.push(self.send("z", now, size), lambda: gather.z_step(k + 1), zed(k + 1))
+                self.push(self.send("x", now, size / 2), lambda: gather.x_step(k), ex(k))
+
+            return then
+
+        def ex(k):
+            return lambda now: self.push(
+                self.send("y", now, size / 2), lambda: gather.y_step(k), lambda now: None if k < depth - 1
+                else self.push(now + 2.0, gather.c_step)
+            )
+
+        self.push(at, lambda: gather.z_step(0), zed(0))
+
+    def scatter(self, scatter, at):
+        size = scatter.rows * scatter.cols * 2
+        steps = scatter.steps()
+        last = len(steps) - 1
+
+        def after(n):
+            def then(now):
+                now = now + 0.3
+                if n == 0:
+                    self.push(self.send("y", now, 2 * size), steps[2], after(2))
+                elif n == 2:
+                    self.push(self.send("x", now, 2 * size), steps[3], after(3))
+                elif 3 <= n < last - 2:
+                    self.push(self.send("z", now, size), steps[n + 1], after(n + 1))
+                elif n == last - 2:
+                    self.push(now, steps[last - 1], after(last - 1))
+                elif n == last - 1:
+                    self.push(self.send("y", now, size), steps[last])
+
+            return then
+
+        self.push(self.send("c", at, 4 * size), steps[0], after(0))
+        self.push(self.send("c", at, 4 * size), steps[1])
+
+    def due(self, now):
+        found = []
+        while self.heap and self.heap[0][0] <= now:
+            at, _, task, then = heapq.heappop(self.heap)
+            found.append(task)
+            if then:
+                then(at)
+        return found
+
+    def all(self):
+        return self.due(float("inf"))
+
+    def next(self):
+        return self.heap[0][0]
+
+
+class Clock:
+    def __init__(self, links):
+        self.links, self.now = links, 0.0
+
+    def run(self, tasks):
+        for task in tasks:
+            task()
+
+    def spend(self, time):
+        self.now += time
+        self.run(self.links.due(self.now))
+
+    def until(self, gather):
+        while not gather.done:
+            self.now = max(self.now, self.links.next())
+            self.run(self.links.due(self.now))
+
+    def loop(self, count, step, time):
+        ticks = []
+        for _ in range(count):
+            self.now += time
+            ticks.append(self.links.due(self.now))
+
+        def body(i):
+            step(i)
+            for n, tasks in enumerate(ticks):
+                if tasks:
+
+                    @pl.when(i == n)
+                    def _(tasks=tasks):
+                        self.run(tasks)
+
+        loop(count, body)
+
+
+def layer_kernel(depth, parts, cuts, *refs):
+    it = iter(refs)
+
+    def take(n):
+        return [next(it) for _ in range(n)]
+
+    x_in, seg, sa, so, su, sd, og_in = take(7)
+    out, pooled, gtok, gq, gk, gv_w, go_w, gu_w, gd_w, small, p_main, p_last = take(12)
+    x, q, k, v, o, z_low, df, n1s, dh, r1s, g, sl, stage = take(13)
+    wa, wo, wu, wd, gv, gbu, vec, bup, dk_sum, dv_sum = take(10)
+    sets = [take(5) for _ in cuts]
+    gsems, ssems, msem, osem, psem = take(9), take(11), *take(3)
+
+    seqs, length = seg.shape
+    tokens, model = x.shape
+    hidden = g.shape[1]
+    shard = so.shape[0]
+    pairs = model // BLOCK
+    spans, offsets, _ = key_windows(length)
+    final = len(spans) - 1
+    tiles = tokens // ROWS
+
+    def span_rows(qb):
+        return (spans[qb][1] - spans[qb][0]) * BLOCK
+
+    def bias_at(row, qb):
+        at = 0 if qb == final else offsets[qb]
+        lane = (row * 2 + (1 if qb == final else 0)) * BLOCK
+        return dh.at[at : at + span_rows(qb), ds(lane, BLOCK)]
+
+    def probs_at(i, qb):
+        held, at = (sl, 0) if qb == final else (g, offsets[qb])
+        return held.at[at : at + span_rows(qb), ds(i * 2 * BLOCK, 2 * BLOCK)]
+
+    place = Place(depth)
+    links = Links()
+    clock = Clock(links)
+    loads = [pltpu.make_async_copy(x_in, x, msem.at[0]), pltpu.make_async_copy(og_in, df, msem.at[1])]
+    for load in loads:
+        load.start()
+    gathers = [
+        Gather(place, n, s, w, gsems) for n, (s, w) in enumerate(((sa, wa), (so, wo), (su, wu), (sd, wd)))
+    ]
+    for gather, at in zip(gathers, BEGINS):
+        links.gather(gather, at)
+    place.barrier()
+    clock.spend(1.0)
+    make_bias(seg, bias_at)
+    loads[0].wait()
+    clock.until(gathers[0])
+    unpack_small(wa[:, :, :, :, 3 * model : 3 * model + BLOCK].reshape(model, BLOCK), shard, parts, vec, bup)
+
+    def vrow(i):
+        return vec[i : i + 1, :]
+
+    def project(rt):
+        rows = ds(rt * ROWS, ROWS)
+        for n, (to, bias) in enumerate(((q, 0), (k, None), (v, 1))):
+            weight = wa[:, :, :, :, n * model : (n + 1) * model].reshape(model, model)
+            value = nn(x[rows, :], weight)
+            to[rows, :] = (value if bias is None else value + vrow(bias)).astype(BF)
+
+    clock.loop(tiles, project, 1.5)
+
+    def copy_probs(i, which, back=False):
+        lanes = ds(i * 2 * BLOCK, 2 * BLOCK)
+        here = g.at[:, lanes] if which == 0 else sl.at[: span_rows(final), lanes]
+        there = (p_main if which == 0 else p_last).at[:, lanes]
+        return pltpu.make_async_copy(here, there, psem.at[which, i])
+
+    def attend(i):
+        attend_pair(i, length, pairs, q, k, v, o, probs_at, bias_at)
+        copy_probs(i, 0).start()
+        copy_probs(i, 1).start()
+
+    clock.loop(seqs * pairs, attend, 2.1)
+    for i in range(seqs * pairs):
+        copy_probs(i, 0).wait()
+        copy_probs(i, 1).wait()
+
+    def up(rt):
+        rows = ds(rt * ROWS, ROWS)
+        h = x[rows, :].astype(F32) + (nn(o[rows, :], wo[...].reshape(model, model)) + vrow(2))
+        c = h - rmean(h)
+        r = lax.rsqrt(rmean(c * c) + EPS)
+        n = c * r
+        n1s[rows, :] = n
+        r1s[rows, :] = jnp.broadcast_to(r, (ROWS, BLOCK))
+        z_low[rows, :] = (n * vrow(3) + vrow(4)).astype(BF)
+        for cc in range(hidden // CHUNK):
+            cs = slice(cc * CHUNK, (cc + 1) * CHUNK)
+            u = nn(z_low[rows, :], wu[:, :, :, :, cs].reshape(model, CHUNK)) + bup[:, cs]
+            cdf, pdf = phi_parts(u)
+            g[rows, cs] = (u * cdf).astype(BF)
+            sl[rows, cs] = (cdf + u * pdf).astype(BF)
+
+    clock.until(gathers[1])
+    clock.until(gathers[2])
+    clock.loop(tiles, up, 5.0)
+    clock.until(gathers[3])
+    for gather in gathers:
+        gather.end()
+    loads[1].wait()
+    gv[...] = jnp.zeros_like(gv)
+    pooled[...] = jnp.zeros_like(pooled)
+
+    def copy_tile(rt):
+        return pltpu.make_async_copy(stage.at[rt % 2], out.at[ds(rt * ROWS, ROWS)], osem.at[rt % 2])
+
+    def down(rt):
+        rows = ds(rt * ROWS, ROWS)
+        h = (n1s[rows, :] * vrow(3) + vrow(4)) + (nn(g[rows, :], wd[...].reshape(hidden, model)) + vrow(5))
+        c = h - rmean(h)
+        r = lax.rsqrt(rmean(c * c) + EPS)
+        n2 = c * r
+        y = n2 * vrow(6) + vrow(7)
+        y_low = y.astype(BF)
+
+        @pl.when(rt >= 2)
+        def _():
+            copy_tile(rt - 2).wait()
+
+        stage[rt % 2] = y_low
+        copy_tile(rt).start()
+        row = rt * ROWS // length
+        ids = seg[pl.ds(row, 1), ds(rt * ROWS % length, ROWS)]
+        onehot = (ids == lax.broadcasted_iota(jnp.int32, (SEGS, ROWS), 0)).astype(BF)
+        pooled[row] = pooled[row] + (nn(onehot, y_low) + nn(onehot, (y - y_low.astype(F32)).astype(BF)))
+        dy = df[rows, :].astype(F32)
+        gv[6:7, :] += csum(dy * n2)
+        gv[7:8, :] += csum(dy)
+        e = dy * vrow(6)
+        d = r * (e - rmean(e) - n2 * rmean(e * n2))
+        dh[rows, :] = d
+        low = d.astype(BF)
+        df[rows, :] = low
+        gv[5:6, :] += csum(low.astype(F32))
+
+    clock.loop(tiles, down, 3.0)
+    for rt in (tiles - 2, tiles - 1):
+        copy_tile(rt).wait()
+    for row in range(seqs):
+        onehot = (seg[row : row + 1, :] == lax.broadcasted_iota(jnp.int32, (SEGS, length), 0)).astype(F32)
+        pooled[row] = pooled[row] / jnp.sum(onehot, axis=1, keepdims=True)
+
+    pair_rows = 2 * sd.shape[0]
+
+    def up_back(cc):
+        cs = ds(cc * pair_rows, pair_rows, BLOCK)
+        zz, xx = cc // 2, cc % 2
+        weight = wd[zz, xx].reshape(pair_rows, model)
+        total = jnp.zeros((1, pair_rows), F32)
+        for rt in range(tiles):
+            rows = slice(rt * ROWS, (rt + 1) * ROWS)
+            du = (nt(df[rows, :], weight) * sl[rows, cs].astype(F32)).astype(BF)
+            sl[rows, cs] = du
+            total += csum(du.astype(F32))
+        gbu[:, cs] = total
+        wd[zz, xx] = tn(g[:, cs], df[...]).astype(BF).reshape(2, sd.shape[0], model)
+
+    clock.loop(hidden // pair_rows, up_back, 1.8)
+
+    at = 0
+    blocks = {}
+    for name, rows, cols in (("d", sd.shape[0], model), ("o", shard, model), ("u", shard, hidden),
+                             ("q", shard, model), ("k", shard, model), ("v", shard, model)):
+        blocks[name] = [at + n * rows for n in range(cols // model)]
+        at += rows * (cols // model)
+    blocks["small"] = [at]
+    results = {"d": gd_w, "o": go_w, "u": gu_w, "q": gq, "k": gk, "v": gv_w}
+    weights = {"d": wd, "o": wo, "u": wu, "q": wa, "k": wa, "v": wa}
+    first = {"q": 0, "k": model, "v": 2 * model}
+    scatters = {}
+    for n, (name, r0, rows, c0, cols) in enumerate(cuts):
+        landing = []
+        for c in range(c0, c0 + cols, model):
+            width = min(model, c0 + cols - c)
+            base = blocks["small" if width < model else name][0 if width < model else c // model] + r0
+            view = n1s.at[base : base + rows, 0:width]
+            result = None if width < model else results[name].at[r0 : r0 + rows, c : c + width]
+            landing.append((view, result))
+        c1 = c0 + first.get(name, 0)
+        scatters.setdefault(name, []).append(
+            Scatter(place, n, weights[name].at[:, :, :, r0 : r0 + rows, c1 : c1 + cols], landing, sets[n], ssems)
+        )
+
+    def send_home(name):
+        for s in scatters[name]:
+            s.begin()
+            links.scatter(s, clock.now)
+
+    send_home("d")
+    bring = [
+        pltpu.make_async_copy(p_main, g, msem.at[2]),
+        pltpu.make_async_copy(p_last, sl.at[: span_rows(final)], msem.at[3]),
+    ]
+    bring[0].start()
+
+    def first_back(rt):
+        rows = ds(rt * ROWS, ROWS)
+        dz = dh[rows, :] + nt(sl[rows, :], wu[...].reshape(model, hidden))
+        n1 = n1s[rows, :]
+        gv[3:4, :] += csum(dz * n1)
+        gv[4:5, :] += csum(dz)
+        e = dz * vrow(3)
+        d = r1s[rows, 0:1] * (e - rmean(e) - n1 * rmean(e * n1))
+        dh[rows, :] = d
+        da = d.astype(BF)
+        df[rows, :] = da
+        gv[2:3, :] += csum(da.astype(F32))
+
+    clock.loop(tiles, first_back, 2.0)
+
+    def up_grad(cc):
+        cs = ds(cc * CHUNK, CHUNK)
+        wu[:, :, :, :, cs] = tn(z_low[...], sl[:, cs]).astype(BF).reshape(depth, 2, 2, shard, CHUNK)
+
+    clock.loop(hidden // CHUNK, up_grad, 1.0)
+    send_home("u")
+    bring[1].start()
+    do = z_low
+
+    def out_back(rt):
+        rows = ds(rt * ROWS, ROWS)
+        do[rows, :] = nt(df[rows, :], wo[...].reshape(model, model)).astype(BF)
+
+    clock.loop(tiles, out_back, 0.4)
+    half = model // 2
+
+    def halves(n, to, left, right):
+        def step(t):
+            value = tn(left[:, ds(t * half, half, BLOCK)], right[...]).astype(BF)
+            to[pl.ds(t * (depth // 2), depth // 2), :, :, :, n * model : (n + 1) * model] = value.reshape(
+                depth // 2, 2, 2, shard, model
+            )
+
+        clock.loop(2, step, 0.8)
+
+    halves(0, wo, o, df)
+    send_home("o")
+    bring[0].wait()
+    bring[1].wait()
+    clock.loop(
+        seqs * pairs,
+        lambda i: attend_back_pair(i, length, pairs, q, k, v, do, probs_at, q, k, v, dk_sum, dv_sum),
+        2.2,
+    )
+
+    def copy_tokens(rt):
+        rows = ds(rt * ROWS, ROWS)
+        return pltpu.make_async_copy(o.at[rows], gtok.at[rows], psem.at[0, rt])
+
+    for n, (name, d) in enumerate((("q", q), ("k", k), ("v", v))):
+
+        def token_step(rt, n=n, d=d):
+            rows = ds(rt * ROWS, ROWS)
+            weight = wa[:, :, :, :, n * model : (n + 1) * model].reshape(model, model)
+            total = dh[rows, :] + nt(d[rows, :], weight)
+            if n < 2:
+                dh[rows, :] = total
+            else:
+                o[rows, :] = total.astype(BF)
+                copy_tokens(rt).start()
+
+        clock.loop(tiles, token_step, 0.4)
+        halves(n, wa, x, d)
+        if name == "v":
+            bq, bv = csum(q[...].astype(F32)), csum(v[...].astype(F32))
+            vectors = jnp.concatenate([bq, bv, gv[2:8, :]], axis=0)
+            columns = pack_small(vectors, gbu[...], shard, parts).reshape(depth, 2, 2, shard, BLOCK)
+            wa[:, :, :, :, 3 * model : 3 * model + BLOCK] = columns
+        send_home(name)
+    clock.run(links.all())
+    for group in scatters.values():
+        for s in group:
+            s.end()
+    for rt in range(tiles):
+        copy_tokens(rt).wait()
+    base = blocks["small"][0]
+    last = n1s[base : base + shard, :BLOCK]
+    square = jnp.concatenate([last, jnp.zeros((BLOCK - shard, BLOCK), F32)], axis=0).T
+    small[...] = square[:16, :]
+
+
+BEGINS = (0.0, 6.0, 9.0, 14.0)
+
+
+def run_layer(depth, x, seg, sa, so, su, sd, og):
+    tokens, model = x.shape
+    hidden = su.shape[1]
+    parts = hidden // model
+    seqs, length = seg.shape
+    spans, offsets, band = key_windows(length)
+    final_rows = band - offsets[-1]
+    shard = so.shape[0]
+    cuts = []
+    for part in range(2):
+        cuts.append(("d", part * (sd.shape[0] // 2), sd.shape[0] // 2, 0, model))
+    for part in range(2):
+        cuts.append(("u", 0, shard, part * (hidden // 2), hidden // 2))
+    cuts.append(("o", 0, shard, 0, model))
+    cuts += [("q", 0, shard, 0, model), ("k", 0, shard, 0, model), ("v", 0, shard, 0, model + 2 * BLOCK)]
+    buffers = []
+    for _, _, rows, _, cols in cuts:
+        buffers += scatter_buffers(rows, cols, depth)
+
+    def own(s):
+        return pltpu.VMEM((depth, 2, 2, *s.shape), BF)
+
+    act, wide = pltpu.VMEM((tokens, model), BF), pltpu.VMEM((tokens, hidden), BF)
+    full = pltpu.VMEM((tokens, model), F32)
+    part = pltpu.VMEM((length, BLOCK), F32)
+    weight = sds((shard, model), F32)
+    iterations = seqs * model // BLOCK
+    return pl.pallas_call(
+        functools.partial(layer_kernel, depth, parts, tuple(cuts)),
+        out_shape=(sds((tokens, model), BF), sds((seqs, SEGS, model), F32), sds((tokens, model), BF),
+                   weight, weight, weight, weight, sds(su.shape, F32), sds(sd.shape, F32), sds((16, BLOCK), F32),
+                   sds((tokens, hidden), BF), sds((final_rows, hidden), BF)),
+        in_specs=[ANY, V, ANY, ANY, ANY, ANY, ANY],
+        out_specs=(ANY, V, ANY) + (ANY,) * 6 + (V, ANY, ANY),
+        scratch_shapes=[act] * 7 + [full, full, pltpu.VMEM((tokens, BLOCK), F32), wide, wide,
+                        pltpu.VMEM((2, ROWS, model), BF), own(sa), own(so), own(su), own(sd),
+                        pltpu.VMEM((8, model), F32), pltpu.VMEM((1, hidden), F32), pltpu.VMEM((8, model), F32),
+                        pltpu.VMEM((1, hidden), F32), part, part, *buffers, *gather_sems(4, depth),
+                        *scatter_sems(len(cuts), depth), pltpu.SemaphoreType.DMA((4,)), pltpu.SemaphoreType.DMA((2,)),
+                        pltpu.SemaphoreType.DMA((2, iterations))],
+        compiler_params=params(0),
+        name="layer",
+    )(x, seg, sa, so, su, sd, og)
+
+
+def local_ring(depth, *args):
+    (tokens, segments, w_query, b_query, w_key, w_value, b_value, w_out, b_out, gain1, shift1, w_up, b_up, w_down,
+     b_down, gain2, shift2, out_grad) = args
+    seqs, length, model = tokens.shape
+    shard = w_query.shape[0]
+    parts = w_up.shape[1] // model
+    x = tokens.reshape(seqs * length, model)
+    og = out_grad.reshape(seqs * length, model)
+    small = jnp.stack([b_query, b_value, b_out, gain1, shift1, b_down, gain2, shift2] + [
+        b_up[i * shard : (i + 1) * shard] for i in range(parts)
+    ], axis=1)
+    small = jnp.pad(small, ((0, 0), (0, 2 * BLOCK - 8 - parts)))
+    sa = jnp.concatenate([w_query, w_key, w_value, small], axis=1)
+    out, pooled, gtok, gq, gk, gv, go, gu, gd, gs, _, _ = run_layer(depth, x, segments, sa, w_out, w_up, w_down, og)
+    gbq, gbv, gbo, gg1, gs1, gbd, gg2, gs2 = [gs[i, :shard] for i in range(8)]
+    gb_up = gs[8 : 8 + parts, :shard].reshape(parts * shard)
+    return (
+        out.reshape(tokens.shape), pooled, gtok.reshape(tokens.shape),
+        gq, gbq, gk, gv, gbv, go, gbo, gg1, gs1, gu, gb_up, gd, gbd, gg2, gs2,
+    )
+
+
 def project(x, wa, vec, q, k, v):
     model = x.shape[1]
 
@@ -604,49 +1084,6 @@
         v[rows, :] = (nn(x[rows, :], wa[:, 2 * model : 3 * model]) + vec[1:2, :]).astype(BF)
 
     loop(x.shape[0] // ROWS, step)
-
-
-def ticked(count, step, ticks):
-    def body(i):
-        step(i)
-        for n, tasks in enumerate(ticks):
-            if tasks:
-
-                @pl.when(i == n)
-                def _(tasks=tasks):
-                    for task in tasks:
-                        task()
-
-    loop(count, body)
-
-
-def forward_kernel(depth, parts, *refs):
-    (x, seg, sa, so, su, sd, q, k, v, o, probs, vec, bup, wa, wo, wu, wd, bias, *sems) = refs
-    length, pairs = seg.shape[1], x.shape[1] // BLOCK
-    place = Place(depth)
-    ga, go, gu, gd = [
-        Gather(place, g, shard, whole, sems)
-        for g, (shard, whole) in enumerate(((sa, wa), (so, wo), (su, wu), (sd, wd)))
-    ]
-    a, b, c, d = ga.steps(), go.steps(), gu.steps(), gd.steps()
-    place.barrier()
-    for task in [a[0], a[1], b[0], a[2], c[0], a[3], d[0]]:
-        task()
-    make_bias(seg, bias)
-    for task in a[4:]:
-        task()
-    model = x.shape[1]
-    unpack_small(wa[:, 3 * model : 3 * model + BLOCK], sa.shape[0], parts, vec, bup)
-    project(x, wa, vec, q, k, v)
-    ticks = [[] for _ in range(seg.shape[0] * pairs)]
-    order = [b[1], b[2], c[1], b[3], c[2], b[4], c[3], d[1], b[5], c[4], d[2], c[5], d[3]]
-    for n, task in enumerate(order):
-        ticks[min(n, len(ticks) - 1)].append(task)
-    ticked(len(ticks), lambda i: attend_pair(i, length, pairs, q, k, v, o, probs, bias), ticks)
-    for task in d[4:6] + [b[6], c[6], d[6]]:
-        task()
-    for one in (ga, go, gu, gd):
-        one.end()
 
 
 def mid_kernel(*refs):
@@ -773,138 +1210,6 @@
     loop(dh1.shape[0] // ROWS, step)
 
 
-def schedule(sizes, begins, gather_gbs=90.0, core_gbs=350.0, delay=1.5):
-    import heapq
-
-    free = {"y": 0.0, "x": 0.0, "z": 0.0, "c": 0.0}
-    heap, found = [], []
-
-    def send(link, at, size):
-        rate = core_gbs if link == "c" else gather_gbs / 2
-        start = max(at, free[link])
-        free[link] = start + size / rate * 1e-3
-        return free[link] + delay
-
-    for g, size in enumerate(sizes):
-        heapq.heappush(heap, (begins[g], g, -1))
-    while heap:
-        at, g, step = heapq.heappop(heap)
-        size = sizes[g]
-        if step >= 0:
-            found.append((at, g, step))
-        if step == -1:
-            heapq.heappush(heap, (send("c", at, 4 * size), g, 0))
-            heapq.heappush(heap, (send("c", at, 4 * size), g, 1))
-        elif step == 0:
-            heapq.heappush(heap, (send("y", at + 0.5, 2 * size), g, 2))
-        elif step == 2:
-            heapq.heappush(heap, (send("x", at + 0.5, 2 * size), g, 3))
-        elif step in (3, 4, 5):
-            heapq.heappush(heap, (send("z", at + 0.5, size), g, step + 1))
-        elif step == 6:
-            heapq.heappush(heap, (at + 0.2, g, 7))
-        elif step == 7:
-            heapq.heappush(heap, (send("y", at, size), g, 8))
-    return found
-
-
-def backward_kernel(depth, parts, length, cuts, *refs):
-    count = len(cuts)
-    (q, k, v, do, probs, x, dh1, wa, g_down, g_up, g_out, gv, gbu, gtok, oa, oo, ou, od, small,
-     dq, dk, dv, dk_sum, dv_sum, g_all, *rest) = refs
-    sets = [rest[6 * n : 6 * n + 6] for n in range(count)]
-    sems = rest[6 * count :]
-    pairs = x.shape[1] // BLOCK
-    model = x.shape[1]
-    place = Place(depth)
-    sources = {"a": (g_all, oa), "o": (g_out, oo), "u": (g_up, ou), "d": (g_down, od)}
-    scatters = []
-    for n, (name, r0, rows, c0, cols) in enumerate(cuts):
-        grad, out = sources[name]
-        scatters.append(
-            Scatter(place, n, grad.at[:, :, :, r0 : r0 + rows, c0 : c0 + cols], out.at[r0 : r0 + rows, c0 : c0 + cols], sets[n], sems)
-        )
-    steps = [s.steps() for s in scatters]
-    early = [n for n, cut in enumerate(cuts) if cut[0] != "a"]
-    late = [n for n, cut in enumerate(cuts) if cut[0] == "a"]
-    iterations = x.shape[0] // length * pairs
-    per, tail = 2.3, 8.0
-    begins = [0.0 if n in early else per * iterations + tail for n in range(count)]
-    sizes = [rows * cols * 2 for _, _, rows, _, cols in cuts]
-    found = schedule(sizes, begins)
-    ticks = [[] for _ in range(iterations)]
-    after = []
-    for at, g, step in found:
-        n = int(at // per)
-        (ticks[n] if n < iterations else after).append(steps[g][step])
-    place.barrier()
-    for n in early:
-        scatters[n].begin()
-    ticked(
-        iterations,
-        lambda i: attend_back_pair(i, length, pairs, q, k, v, do, probs, dq, dk, dv, dk_sum, dv_sum),
-        ticks,
-    )
-    half = model // 2
-    owners = half // oo.shape[0]
-
-    def store(n, t, value):
-        shaped = value.reshape(owners // 4, 2, 2, oo.shape[0], model)
-        g_all[pl.ds(t * (owners // 4), owners // 4), :, :, :, n * model : (n + 1) * model] = shaped
-
-    qkv_grads(x, (dq, dk, dv), store)
-    bq, bv = csum(dq[...].astype(F32)), csum(dv[...].astype(F32))
-    vectors = jnp.concatenate([bq, bv, gv[2:8, :]], axis=0)
-    columns = pack_small(vectors, gbu[...], oo.shape[0], parts)
-    shaped = columns.reshape(depth, 2, 2, oo.shape[0], BLOCK)
-    g_all[:, :, :, :, 3 * model : 3 * model + BLOCK] = shaped
-    g_all[:, :, :, :, 3 * model + BLOCK :] = jnp.zeros_like(shaped)
-    for n in late:
-        scatters[n].begin()
-    token_grads(dh1, (dq, dk, dv), wa, gtok)
-    for task in after:
-        task()
-    for s in scatters:
-        s.end()
-    last = oa[:, 3 * model : 3 * model + BLOCK]
-    square = jnp.concatenate([last, jnp.zeros((BLOCK - last.shape[0], BLOCK), F32)], axis=0).T
-    small[...] = square[:16, :]
-
-
-V = pl.BlockSpec(memory_space=pltpu.VMEM)
-ANY = pl.BlockSpec(memory_space=pl.ANY)
-sds = jax.ShapeDtypeStruct
-
-
-def params(collective_id=None):
-    if collective_id is None:
-        return pltpu.CompilerParams(vmem_limit_bytes=VMEM_LIMIT)
-    return pltpu.CompilerParams(
-        vmem_limit_bytes=VMEM_LIMIT, collective_id=collective_id, has_side_effects=True
-    )
-
-
-def run_forward(depth, x, seg, sa, so, su, sd):
-    tokens, model = x.shape
-    owners = depth * 4
-    hidden = su.shape[1]
-    parts = hidden // model
-    seqs, length = seg.shape
-    band = key_windows(length)[2]
-    act = sds((tokens, model), BF)
-    wholes = [sds((owners * s.shape[0], s.shape[1]), BF) for s in (sa, so, su, sd)]
-    return pl.pallas_call(
-        functools.partial(forward_kernel, depth, parts),
-        out_shape=(act, act, act, act, sds((seqs * model // BLOCK, band, 2 * BLOCK), BF),
-                   sds((8, model), F32), sds((1, hidden), F32), *wholes),
-        in_specs=[V, V, ANY, ANY, ANY, ANY],
-        out_specs=(V,) * 8 + (ANY,) * 3,
-        scratch_shapes=[pltpu.VMEM((seqs, band, BLOCK), F32)] + gather_sems(4, depth),
-        compiler_params=params(0),
-        name="forward",
-    )(x, seg, sa, so, su, sd)
-
-
 def run_mid(x, o, og, seg, wo, wu, wd, vec, bup):
     tokens, model = x.shape
     hidden = wu.shape[1]
@@ -923,79 +1228,28 @@
     )(x, o, og, seg, wo, wu, wd, vec, bup)
 
 
-def run_backward(depth, length, shards, q, k, v, do, probs, x, dh1, wa, g_down, g_up, g_out, gv, gbu):
-    tokens, model = x.shape
-    sa, so, su, sd = shards
-    parts = su[1] // model
-
-    def owned(t, s):
-        return t.reshape(depth, 2, 2, *s)
-
-    cuts = [("o", 0, so[0], 0, so[1])]
-    for part in range(2):
-        cuts.append(("d", part * (sd[0] // 2), sd[0] // 2, 0, sd[1]))
-    for part in range(2):
-        cuts.append(("u", 0, su[0], part * (su[1] // 2), su[1] // 2))
-    for part in range(2):
-        cuts.append(("a", 0, sa[0], part * (sa[1] // 2), sa[1] // 2))
-    buffers = []
-    for _, _, rows, _, cols in cuts:
-        buffers += scatter_buffers(rows, cols, depth)
-    act = pltpu.VMEM((tokens, model), BF)
-    half_sum = pltpu.VMEM((length, BLOCK), F32)
-    return pl.pallas_call(
-        functools.partial(backward_kernel, depth, parts, length, tuple(cuts)),
-        out_shape=(sds((tokens, model), BF), sds(sa, F32), sds(so, F32), sds(su, F32), sds(sd, F32), sds((16, BLOCK), F32)),
-        in_specs=[V] * 8 + [ANY] * 3 + [V] * 2,
-        out_specs=(V,) * 6,
-        scratch_shapes=[act, act, act, half_sum, half_sum, pltpu.VMEM((depth, 2, 2, *sa), BF), *buffers,
-                        *scatter_sems(len(cuts), depth)],
-        compiler_params=params(1),
-        name="backward",
-    )(q, k, v, do, probs, x, dh1, wa, owned(g_down, sd), owned(g_up, su), owned(g_out, so), gv, gbu)
-
-
-def local_ring(depth, *args):
-    (tokens, segments, w_query, b_query, w_key, w_value, b_value, w_out, b_out, gain1, shift1, w_up, b_up, w_down,
-     b_down, gain2, shift2, out_grad) = args
-    seqs, length, model = tokens.shape
-    shard = w_query.shape[0]
-    parts = w_up.shape[1] // model
-    x = tokens.reshape(seqs * length, model)
-    og = out_grad.reshape(seqs * length, model)
-    small = jnp.stack([b_query, b_value, b_out, gain1, shift1, b_down, gain2, shift2] + [
-        b_up[i * shard : (i + 1) * shard] for i in range(parts)
-    ], axis=1)
-    small = jnp.pad(small, ((0, 0), (0, 2 * BLOCK - 8 - parts)))
-    sa = jnp.concatenate([w_query, w_key, w_value, small], axis=1)
-    q, k, v, o, probs, vec, bup, wa, wo, wu, wd = run_forward(depth, x, segments, sa, w_out, w_up, w_down)
-    out, pooled, g_down, g_up, g_out, do, dh1, gv, gbu = run_mid(x, o, og, segments, wo, wu, wd, vec, bup)
-    gtok, ga, go, gu, gd, gs = run_backward(
-        depth, length, (sa.shape, w_out.shape, w_up.shape, w_down.shape),
-        q, k, v, do, probs, x, dh1, wa, g_down, g_up, g_out, gv, gbu,
-    )
-    vectors = [gs[i, :shard] for i in range(8)]
-    gbq, gbv, gbo, gg1, gs1, gbd, gg2, gs2 = vectors
-    gb_up = gs[8 : 8 + parts, :shard].reshape(parts * shard)
-    return (
-        out.reshape(tokens.shape), pooled, gtok.reshape(tokens.shape),
-        ga[:, :model], gbq, ga[:, model : 2 * model], ga[:, 2 * model : 3 * model], gbv,
-        go, gbo, gg1, gs1, gu, gb_up, gd, gbd, gg2, gs2,
-    )
+def plain_views(length, bias, probs):
+    spans, offsets, _ = key_windows(length)
+
+    def view(held):
+        return lambda i, qb: held.at[i, pl.ds(offsets[qb], (spans[qb][1] - spans[qb][0]) * BLOCK)]
+
+    return view(bias), view(probs)
 
 
 def qkv_kernel(x, wa, vec, seg, q, k, v, o, probs, bias):
     length, pairs = seg.shape[1], x.shape[1] // BLOCK
-    make_bias(seg, bias)
+    bias_at, probs_at = plain_views(length, bias, probs)
+    make_bias(seg, bias_at)
     project(x, wa, vec, q, k, v)
-    loop(seg.shape[0] * pairs, lambda i: attend_pair(i, length, pairs, q, k, v, o, probs, bias))
+    loop(seg.shape[0] * pairs, lambda i: attend_pair(i, length, pairs, q, k, v, o, probs_at, bias_at))
 
 
 def back_kernel(length, q, k, v, do, probs, x, dh1, wa, gtok, g_qkv, gb, dq, dk, dv, dk_sum, dv_sum):
     pairs, model = x.shape[1] // BLOCK, x.shape[1]
     loop(
         x.shape[0] // length * pairs,
-        lambda i: attend_back_pair(i, length, pairs, q, k, v, do, probs, dq, dk, dv, dk_sum, dv_sum),
+        lambda i: attend_back_pair(i, length, pairs, q, k, v, do, plain_views(length, None, probs)[1], dq, dk, dv, dk_sum, dv_sum),
     )
 
     def store(n, t, value):

time: 278 us -> 233 us (0.84)
  Pallas kernels: 264 us -> 216 us
    pallas_call x3 -> x1, Pallas kernels: 264 us -> 216 us  [run_layer(): pl.pallas_call(functools.partial(layer_kernel, depth, parts, tuple(cuts))...]
    unnamed x10 -> x25, local copies, waits for them, and re-layouts: 5.06 us -> 8.84 us
where the time goes in v2:
time: 233 us; the launch traced here: 232 us
  Pallas kernels  216 us (93%)
  local copies, waits for them, and re-layouts  13.5 us (6%)
    pallas_call x1, Pallas kernels, run_layer(): pl.pallas_call(functools.partial(layer_kernel, depth, parts, tuple(cuts))...  216 us
    unnamed x25, local copies, waits for them, and re-layouts  8.84 us

profile of v2, /device:TPU:0, one launch (start us, length us, event | category | flops | bytes accessed | tf_op | source)
XLA Modules:
  0.0 232.2 jit_solution(13894789568120027514)
XLA Ops:
  0.7 0.9 slice_bitcast_fusion.8
  1.5 0.8 stack.51
  2.4 0.1 copy.48
  2.5 1.7 fusion.1.refs_2_
  4.1 216.4 %layer.1 = (bf16[1024,768]{1,0:T(8,128)(2,1)}, f32[2,8,768]{2,1,0:T(8,128)}, bf16[1024,768]{1,0:T(8,128)(2,1)}, f32[48,768]{1,0:T(8,128)}, f32[48,768]{1,0:T(8,1...) custom-call(bf16[1024,768]{1,0:T(8,128)(2,1)} %bitcast.36, ...), custom_call_target="tpu_custom_call" | custom-call | tf_op jit(solution)/shard_map/layer/pallas_call | solution.py:1037
  220.5 0.7 slice.48
  221.2 1.5 slice_bitcast_fusion
  222.7 0.6 reshape.55
  223.4 0.0 copy-start.7
  223.4 0.0 copy-start
  223.4 2.8 %copy.58 = bf16[2,512,768]{2,1,0:T(8,128)(2,1)} copy(bf16[2,512,768]{2,1,0:T(8,128)(2,1)} %bitcast.39) | data formatting | bytes 3145728
  226.1 0.0 copy-done.7
  226.1 0.6 copy.59
  226.8 0.0 copy-done
  226.8 0.0 copy-start.6
  226.8 0.0 copy-start.5
  226.8 0.0 copy-start.4
  226.8 0.0 copy-start.3
  226.8 0.0 copy-start.2
  226.8 1.1 copy.60
  227.9 0.0 copy-done.6
  227.9 0.7 copy.61
  228.6 0.0 copy-done.5
  228.6 0.7 copy.62
  229.3 0.0 copy-done.4
  229.3 0.7 copy.63
  229.9 0.0 copy-done.3
  229.9 0.7 copy.64
  230.6 0.0 copy-done.2
  230.6 0.8 copy.65
  231.4 0.0 copy-done.1
  231.4 0.8 copy.66
  (1 shorter events, 0.0 us)
Async XLA Ops:
  223.4 2.8 %copy-start.7 = (f32[2,8,768]{2,1,0:T(8,128)S(1)}, f32[2,8,768]{2,1,0:T(8,128)}, u32[]{:S(2)}) copy-start(f32[2,8,768]{2,1,0:T(8,128)} %get-tuple-element.69) | copy-start | bytes 147460
  223.4 3.4 %copy-start = (bf16[1024,768]{1,0:T(8,128)(2,1)S(1)}, bf16[1024,768]{1,0:T(8,128)(2,1)}, u32[]{:S(2)}) copy-start(bf16[1024,768]{1,0:T(8,128)(2,1)} %get-tuple-element.30) | copy-start | bytes 4718596
  226.8 1.2 copy-start.6
  226.8 1.8 copy-start.5
  226.8 2.5 %copy-start.4 = (f32[48,768]{1,0:T(8,128)S(1)}, f32[48,768]{1,0:T(8,128)}, u32[]{:S(2)}) copy-start(f32[48,768]{1,0:T(8,128)} %get-tuple-element.74) | copy-start | bytes 442372
  226.8 3.2 %copy-start.3 = (f32[48,768]{1,0:T(8,128)S(1)}, f32[48,768]{1,0:T(8,128)}, u32[]{:S(2)}) copy-start(f32[48,768]{1,0:T(8,128)} %get-tuple-element.76) | copy-start | bytes 442372
  226.8 3.8 %copy-start.2 = (f32[48,3072]{1,0:T(8,128)S(1)}, f32[48,3072]{1,0:T(8,128)}, u32[]{:S(2)}) copy-start(f32[48,3072]{1,0:T(8,128)} %get-tuple-element.80) | copy-start | bytes 1769476
  227.9 3.5 %copy-start.1 = (f32[192,768]{1,0:T(8,128)S(1)}, f32[192,768]{1,0:T(8,128)}, u32[]{:S(2)}) copy-start(f32[192,768]{1,0:T(8,128)} %get-tuple-element.82) | copy-start | bytes 1769476

commit v3 on v2

--- a/solution.py
+++ b/solution.py
@@ -88,37 +88,37 @@
             bias_at(row, qb)[...] = jnp.where(same, 0.0, MASKED)
 
 
-def attend_pair(i, length, pairs, q, k, v, o, probs_at, bias_at):
+def attend_pair(row, length, q, k, v, o, probs_at, bias_at):
     spans, _, _ = key_windows(length)
-    row, pair = i // pairs, i % pairs
-    r0, c = pl.multiple_of(row * length, length), ds(pair * BLOCK, BLOCK)
-    vt = v[pl.ds(r0, length), c].T
+    (q, cq), (k, ck), (v, cv), (o, co) = q, k, v, o
+    r0 = pl.multiple_of(row * length, length)
+    vt = v[pl.ds(r0, length), cv].T
     for qb, (k0, k1) in enumerate(spans):
         n = (k1 - k0) * BLOCK
         mine = pl.ds(r0 + qb * BLOCK, BLOCK)
-        q2 = stack2(q[mine, c] * BF(HEAD**-0.5))
-        s = nt(k[pl.ds(r0 + k0 * BLOCK, n), c], q2)
-        b = bias_at(row, qb)[...]
+        q2 = stack2(q[mine, cq] * BF(HEAD**-0.5))
+        s = nt(k[pl.ds(r0 + k0 * BLOCK, n), ck], q2)
+        b = bias_at(qb)[...]
         s = s + jnp.concatenate([b, b], axis=1)
         e = jnp.exp(s - jnp.max(s, axis=0, keepdims=True))
         p = (e * (1.0 / jnp.sum(e, axis=0, keepdims=True))).astype(BF)
-        probs_at(i, qb)[...] = p
-        o[mine, c] = unstack_t(nn(vt[:, k0 * BLOCK : k1 * BLOCK], p)).astype(BF)
-
-
-def attend_back_pair(i, length, pairs, q, k, v, do, probs_at, dq, dk, dv, dk_sum, dv_sum):
+        probs_at(qb)[...] = p
+        o[mine, co] = unstack_t(nn(vt[:, k0 * BLOCK : k1 * BLOCK], p)).astype(BF)
+
+
+def attend_back_pair(row, length, q, k, v, do, dq, probs_at, dk_sum, dv_sum):
     spans, _, _ = key_windows(length)
     last = len(spans) - 1
-    row, pair = i // pairs, i % pairs
-    r0, c = pl.multiple_of(row * length, length), ds(pair * BLOCK, BLOCK)
-    kt = k[pl.ds(r0, length), c].T
+    (q, cq), (k, ck), (v, cv), (do, co) = q, k, v, do
+    r0 = pl.multiple_of(row * length, length)
+    kt = k[pl.ds(r0, length), ck].T
     for qb, (k0, k1) in enumerate(spans):
         n = (k1 - k0) * BLOCK
         mine = pl.ds(r0 + qb * BLOCK, BLOCK)
-        q2 = stack2(q[mine, c] * BF(HEAD**-0.5))
-        do2 = stack2(do[mine, c])
-        dp = nt(v[pl.ds(r0 + k0 * BLOCK, n), c], do2)
-        low = probs_at(i, qb)[...]
+        q2 = stack2(q[mine, cq] * BF(HEAD**-0.5))
+        do2 = stack2(do[mine, co])
+        dp = nt(v[pl.ds(r0 + k0 * BLOCK, n), cv], do2)
+        low = probs_at(qb)[...]
         p = low.astype(F32)
         d_s = (p * (dp - jnp.sum(p * dp, axis=0, keepdims=True))).astype(BF)
         dv_part = nn(low, do2)
@@ -131,13 +131,13 @@
                 a, b = a + dv_sum[held, :], b + dk_sum[held, :]
             if qb == min(kb + 1, last):
                 there = pl.ds(r0 + kb * BLOCK, BLOCK)
-                dv[there, c] = a.astype(BF)
-                dk[there, c] = b.astype(BF)
+                v[there, cv] = a.astype(BF)
+                k[there, ck] = b.astype(BF)
             else:
                 dv_sum[held, :] = a
                 dk_sum[held, :] = b
         dqt = nn(kt[:, k0 * BLOCK : k1 * BLOCK], d_s)
-        dq[mine, c] = (unstack_t(dqt) * HEAD**-0.5).astype(BF)
+        dq[mine, co] = (unstack_t(dqt) * HEAD**-0.5).astype(BF)
 
 
 class Place:
@@ -182,15 +182,17 @@
         pltpu.SemaphoreType.DMA((groups, 2, depth - 1)),
         pltpu.SemaphoreType.DMA((groups, depth)),
         pltpu.SemaphoreType.DMA((groups, depth)),
-        pltpu.SemaphoreType.DMA((groups, 3, depth)),
+        pltpu.SemaphoreType.DMA((groups, depth + 1)),
+        pltpu.SemaphoreType.DMA((groups, depth)),
     ] * 2 + [pltpu.SemaphoreType.DMA((groups,))]
 
 
 class Gather:
-    def __init__(self, place, g, shard, whole, sems):
+    def __init__(self, place, g, shard, whole, sems, halved=False):
         self.p, self.g, self.shard, self.whole = place, g, shard, whole
-        self.sz, self.sx, self.sy, self.sc, self.rz, self.rx, self.ry, self.rc, self.own = sems
-        self.rows, self.cols = shard.shape
+        self.halved = halved
+        self.sz, self.sx, self.sy, self.sc, self.so, self.rz, self.rx, self.ry, self.rc, self.ro, self.own = sems
+        self.rows, self.cols = whole.shape[3:]
         self.done = False
 
     def piece(self, z, x, half=None):
@@ -202,7 +204,7 @@
         return self.whole.at[z, x, c, :, ds(half * (self.cols // 2), self.cols // 2)]
 
     def copy_z(self, direction, distance, z, src=None):
-        dst = self.piece(z, self.p.x)
+        dst = self.piece(z, self.p.x, self.p.y if self.halved else None)
         return remote(
             dst if src is None else src,
             dst,
@@ -219,19 +221,26 @@
         at = self.piece(z, 1 - self.p.x, self.p.y)
         return remote(at, at, self.sy.at[self.g, z], self.ry.at[self.g, z], self.p.yn)
 
-    def copy_c(self, kind, z, src=None):
-        if kind == 0:
-            dst = self.piece(z, self.p.x)
-        else:
-            half = self.p.y if kind == 1 else 1 - self.p.y
-            dst = self.piece(z, 1 - self.p.x, half)
-        return remote(
-            dst if src is None else src,
-            dst,
-            self.sc.at[self.g, kind, z],
-            self.rc.at[self.g, kind, z],
-            self.p.sib,
-        )
+    def copy_c(self, z, src=None):
+        dst = self.piece(z, self.p.x)
+        return remote(dst if src is None else src, dst, self.sc.at[self.g, z], self.rc.at[self.g, z], self.p.sib)
+
+    def copy_o(self, z):
+        at = self.piece(z, self.p.x, self.p.y)
+        return remote(at, at, self.so.at[self.g, z], self.ro.at[self.g, z], self.p.yn)
+
+    def o_step(self, k):
+        def act(z):
+            at = self.piece(z, self.p.x, 1 - self.p.y)
+            remote(at, at, self.so.at[self.g, z], self.ro.at[self.g, z], self.p.yn).wait_recv()
+            self.copy_c(z).start()
+
+        self.at_distance(k, act)
+
+    def copy_column(self):
+        at = self.whole.at[:, 1 - self.p.x, self.p.c]
+        n = self.p.depth
+        return remote(at, at, self.sc.at[self.g, n], self.rc.at[self.g, n], self.p.sib)
 
     def local(self):
         return pltpu.make_async_copy(self.shard, self.piece(self.p.z, self.p.x), self.own.at[self.g])
@@ -239,19 +248,23 @@
     def z_step(self, k):
         p = self.p
         if k == 0:
-            self.local().start()
+            if self.shard is None:
+                shard, half = self.piece(p.z, p.x), self.piece(p.z, p.x, p.y)
+            else:
+                self.local().start()
+                shard, half = self.shard, self.shard.at[:, ds(p.y * (self.cols // 2), self.cols // 2)]
+            mine = half if self.halved else shard
 
             @pl.when(p.z < p.depth - 1)
             def _():
-                self.copy_z(0, 0, p.z, self.shard).start()
+                self.copy_z(0, 0, p.z, mine).start()
 
             @pl.when(p.z > 0)
             def _():
-                self.copy_z(1, 0, p.z, self.shard).start()
-
-            half = self.shard.at[:, ds(p.y * (self.cols // 2), self.cols // 2)]
+                self.copy_z(1, 0, p.z, mine).start()
+
             self.copy_x(p.z, half).start()
-            self.copy_c(0, p.z, self.shard).start()
+            self.copy_c(p.z, shard).start()
             return
 
         for direction in (0, 1):
@@ -267,7 +280,10 @@
                         self.copy_z(direction, k, z).start()
 
                 self.copy_x(z).start()
-                self.copy_c(0, z).start()
+                if self.halved:
+                    self.copy_o(z).start()
+                else:
+                    self.copy_c(z).start()
 
     def at_distance(self, k, act):
         p = self.p
@@ -286,8 +302,7 @@
     def x_step(self, k):
         def act(z):
             self.copy_x_in(z).wait_recv()
-            self.copy_y_out(z).start()
-            self.copy_c(1, z).start()
+            self.copy_y(z).start()
 
         self.at_distance(k, act)
 
@@ -295,9 +310,6 @@
         at = self.piece(z, 1 - self.p.x, self.p.y)
         return remote(at, at, self.sx.at[self.g, z], self.rx.at[self.g, z], self.p.xn)
 
-    def copy_y_out(self, z):
-        return self.copy_y(z)
-
     def copy_y_in(self, z):
         at = self.piece(z, 1 - self.p.x, 1 - self.p.y)
         return remote(at, at, self.sy.at[self.g, z], self.ry.at[self.g, z], self.p.yn)
@@ -305,24 +317,21 @@
     def y_step(self, k):
         def act(z):
             self.copy_y_in(z).wait_recv()
-            self.copy_c(2, z).start()
 
         self.at_distance(k, act)
-
-    def core_in(self, kind, z):
-        p = self.p
-        if kind == 0:
-            at = self.piece_of(z, p.x, 1 - p.c)
-        else:
-            at = self.piece_of(z, 1 - p.x, 1 - p.c, p.y if kind == 1 else 1 - p.y)
-        return remote(at, at, self.sc.at[self.g, kind, z], self.rc.at[self.g, kind, z], p.sib)
+        if k == self.p.depth - 1:
+            self.copy_column().start()
 
     def c_step(self):
         self.done = True
-        self.local().wait()
-        for kind in range(3):
-            for z in range(self.p.depth):
-                self.core_in(kind, z).wait_recv()
+        if self.shard is not None:
+            self.local().wait()
+        p, n = self.p, self.p.depth
+        for z in range(n):
+            at = self.whole.at[z, p.x, 1 - p.c]
+            remote(at, at, self.sc.at[self.g, z], self.rc.at[self.g, z], p.sib).wait_recv()
+        at = self.whole.at[:, 1 - p.x, 1 - p.c]
+        remote(at, at, self.sc.at[self.g, n], self.rc.at[self.g, n], p.sib).wait_recv()
 
     def end(self):
         p = self.p
@@ -338,28 +347,19 @@
         for z in range(p.depth):
             self.copy_x(z).wait_send()
             self.copy_y(z).wait_send()
-            for kind in range(3):
-                self.copy_c(kind, z).wait_send()
-
-    def steps(self):
-        d = self.p.depth
-        out = []
-        for n in range(d + 2):
-            def step(n=n):
-                if n < d:
-                    self.z_step(n)
-                if 0 <= n - 1 < d:
-                    self.x_step(n - 1)
-                if 0 <= n - 2 < d:
-                    self.y_step(n - 2)
-            out.append(step)
-        out.append(self.c_step)
-        return out
+            self.copy_c(z).wait_send()
+            if self.halved:
+
+                @pl.when(p.z != z)
+                def _(z=z):
+                    self.copy_o(z).wait_send()
+
+        self.copy_column().wait_send()
 
 
 def scatter_sems(groups, depth):
     kinds = [(groups, 2), (groups,), (groups,), (groups, 2, depth - 1), (groups,)]
-    return [pltpu.SemaphoreType.DMA(k) for k in kinds] * 2 + [pltpu.SemaphoreType.DMA((groups, 2))]
+    return [pltpu.SemaphoreType.DMA(k) for k in kinds] * 2 + [pltpu.SemaphoreType.DMA((groups, 5))]
 
 
 def scatter_buffers(rows, cols, depth):
@@ -367,8 +367,18 @@
         pltpu.VMEM((2, depth, rows, cols), BF),
         pltpu.VMEM((depth, rows, cols // 2), BF),
         pltpu.VMEM((depth, rows, cols // 2), BF),
-        pltpu.VMEM((2, depth - 1, rows, cols), BF),
+        pltpu.VMEM((2 * depth - 3, rows, cols), BF),
         pltpu.VMEM((rows, cols), BF),
+    ]
+
+
+def scatter_half_buffers(rows, cols, depth):
+    return [
+        pltpu.VMEM((2, depth, rows, cols), BF),
+        pltpu.VMEM((depth, rows, cols // 2), BF),
+        pltpu.VMEM((depth, rows, cols), BF),
+        pltpu.VMEM((2 * depth - 3, rows, cols // 2), BF),
+        pltpu.VMEM((rows, cols // 2), BF),
     ]
 
 
@@ -385,6 +395,8 @@
 
 
 class Scatter:
+    first, second, along, last = ("y", 2), ("x", 2), 1.0, 1.0
+
     def __init__(self, place, g, grad, landing, buffers, sems):
         self.p, self.g, self.grad, self.landing = place, g, grad, landing
         self.in_c, self.in_y, self.in_x, self.in_z, self.in_f = buffers
@@ -410,11 +422,15 @@
             self.grad.at[:, 1 - p.x, p.c, :, self.half(p.y)], self.in_x, self.sx.at[self.g], self.rx.at[self.g], p.xn
         )
 
+    def line_slot(self, direction, slot):
+        far = self.depth - 2
+        return 2 * far if slot == far else 2 * slot + direction
+
     def copy_z(self, direction, z, slot):
         p = self.p
         return remote(
-            self.grad.at[z, p.x, p.c],
-            self.in_z.at[direction, slot],
+            self.line_piece(z),
+            self.in_z.at[self.line_slot(direction, slot)],
             self.sz.at[self.g, direction, slot],
             self.rz.at[self.g, direction, slot],
             p.up if direction == 0 else p.down,
@@ -423,6 +439,12 @@
     def copy_f(self):
         p = self.p
         return remote(self.grad.at[p.z, p.x, p.c], self.in_f, self.sf.at[self.g], self.rf.at[self.g], p.yn)
+
+    def receive(self):
+        self.copy_f().wait_recv()
+
+    def end_y(self):
+        self.copy_y().wait_send()
 
     def begin(self):
         self.copy_c(1 - self.p.x).start()
@@ -439,7 +461,13 @@
             lambda z, at: self.in_c.at[x, z, at],
         )
         if turn == 0:
-            self.copy_y().start()
+            self.begin_exchange()
+
+    def begin_exchange(self):
+        self.copy_y().start()
+
+    def line_piece(self, z):
+        return self.grad.at[z, self.p.x, self.p.c]
 
     def over_y(self):
         p = self.p
@@ -484,8 +512,8 @@
                 add_into(
                     1,
                     self.rows,
-                    lambda _, at: self.grad.at[z, p.x, p.c, at],
-                    lambda _, at: self.in_z.at[direction, slot, at],
+                    lambda _, at: self.line_piece(z).at[at],
+                    lambda _, at: self.in_z.at[self.line_slot(direction, slot), at],
                 )
                 if slot > 0:
                     self.copy_z(direction, z, slot - 1).start()
@@ -494,32 +522,38 @@
         self.copy_f().start()
 
     def copy_out(self, n):
-        view, result = self.landing[n]
+        _, view, result = self.landing[n]
         return pltpu.make_async_copy(view, result, self.out.at[self.g, n])
 
     def finish(self):
         p = self.p
-        self.copy_f().wait_recv()
+        self.receive()
         piece = min(self.rows, 48)
         c0 = 0
-        for n, (view, result) in enumerate(self.landing):
-            cols = view.shape[1]
+        for n, (cols, view, result) in enumerate(self.landing):
+            if view is None:
+                c0 += cols
+                continue
 
             def step(i, view=view, c0=c0, cols=cols):
                 at = ds(i * piece, piece, 16)
                 cs = pl.ds(c0, cols)
-                view[at, :] = self.grad[p.z, p.x, p.c, at, cs].astype(F32) + self.in_f[at, cs].astype(F32)
+                view[at, :] = self.total(at, cs)
 
             loop(self.rows // piece, step)
             if result is not None:
                 self.copy_out(n).start()
             c0 += cols
 
+    def total(self, at, cs):
+        p = self.p
+        return self.grad[p.z, p.x, p.c, at, cs].astype(F32) + self.in_f[at, cs].astype(F32)
+
     def end(self):
         p, top = self.p, self.depth - 1
         for x in (0, 1):
             self.copy_c(x).wait_send()
-        self.copy_y().wait_send()
+        self.end_y()
         self.copy_x().wait_send()
         for direction in (0, 1):
             place = p.z if direction == 0 else top - p.z
@@ -530,59 +564,127 @@
                     self.copy_z(direction, 0, slot).wait_send()
 
         self.copy_f().wait_send()
-        for n, (_, result) in enumerate(self.landing):
+        for n, (_, _, result) in enumerate(self.landing):
             if result is not None:
                 self.copy_out(n).wait()
 
+    def exchanges(self):
+        return [self.over_y, self.over_x]
+
     def steps(self):
-        def over_x_and_line():
-            self.over_x()
+        one, two = self.exchanges()
+
+        def two_and_line():
+            two()
             self.line(0)
 
-        out = [lambda: self.cores(0), lambda: self.cores(1), self.over_y, over_x_and_line]
+        out = [lambda: self.cores(0), lambda: self.cores(1), one, two_and_line]
         for wave in range(1, self.depth):
             out.append(functools.partial(self.line, wave))
         return out + [self.share, self.finish]
 
 
-def spread(width, owners_rows, parts):
+class HalfScatter(Scatter):
+    first, second, along, last = ("x", 4), ("y", 2), 0.5, 0.5
+
+    def copy_x(self):
+        p = self.p
+        return remote(self.grad.at[:, 1 - p.x, p.c], self.in_x, self.sx.at[self.g], self.rx.at[self.g], p.xn)
+
+    def copy_y(self):
+        p = self.p
+        return remote(
+            self.grad.at[:, p.x, p.c, :, self.half(1 - p.y)], self.in_y, self.sy.at[self.g], self.ry.at[self.g], p.yn
+        )
+
+    def begin_exchange(self):
+        self.copy_x().start()
+
+    def exchanges(self):
+        return [self.over_x, self.over_y]
+
+    def over_x(self):
+        p = self.p
+        self.copy_x().wait_recv()
+        add_into(
+            self.depth,
+            self.rows,
+            lambda z, at: self.grad.at[z, p.x, p.c, at],
+            lambda z, at: self.in_x.at[z, at],
+        )
+        self.copy_y().start()
+
+    def over_y(self):
+        p = self.p
+        self.copy_y().wait_recv()
+        add_into(
+            self.depth,
+            self.rows,
+            lambda z, at: self.line_piece(z).at[at],
+            lambda z, at: self.in_y.at[z, at],
+        )
+
+    def line_piece(self, z):
+        return self.grad.at[z, self.p.x, self.p.c, :, self.half(self.p.y)]
+
+    def copy_f(self):
+        return remote(self.line_piece(self.p.z), self.in_f, self.sf.at[self.g], self.rf.at[self.g], self.p.yn)
+
+    def receive(self):
+        p = self.p
+        self.copy_f().wait_recv()
+        self.copy_y().wait_send()
+        self.grad[p.z, p.x, p.c, :, self.half(1 - p.y)] = self.in_f[...]
+
+    def end_y(self):
+        pass
+
+    def total(self, at, cs):
+        p = self.p
+        return self.grad[p.z, p.x, p.c, at, cs].astype(F32)
+
+
+def spread(place, owners_rows, parts):
+    width = place.shape[0]
     row = lax.broadcasted_iota(jnp.int32, (width, 1), 0)
     target = row
     for owner in range(1, width // owners_rows):
         target = target + jnp.where(row >= owner * owners_rows, (parts - 1) * owners_rows, 0)
     lane = lax.broadcasted_iota(jnp.int32, (width, width * parts), 1)
-    return (lane == target).astype(BF)
-
-
-def unpack_small(columns, shard, parts, vec, bup):
+    place[...] = (lane == target).astype(BF)
+
+
+def unpack_small(columns, shard, parts, vec, bup, room):
     rows = columns.astype(F32).T
     vec[...] = rows[:8, :]
     low = rows[8:16, :].astype(BF)
     width = 8 * shard
-    place = spread(width, shard, parts)
+    place = room.at[:width, : width * parts]
+    spread(place, shard, parts)
     for t in range(columns.shape[0] // width):
-        wide = nn(low[:, t * width : (t + 1) * width], place)
+        wide = nn(low[:, t * width : (t + 1) * width], place[...])
         total = wide[0:1]
         for i in range(1, parts):
             total = total + pltpu.roll(wide, i * shard, 1)[i : i + 1]
         bup[:, t * width * parts : (t + 1) * width * parts] = total
 
 
-def pack_small(gv, gbu, shard, parts):
+def pack_small(gv, gbu, shard, parts, room):
     width = 8 * shard
+    wide = width * parts
     model = gv.shape[1]
-    place = spread(width, shard, parts)
-    rows = []
-    for i in range(parts):
-        pieces = []
-        for t in range(model // width):
-            wide = jnp.broadcast_to(gbu[:, t * width * parts : (t + 1) * width * parts], (8, width * parts))
-            if i:
-                wide = pltpu.roll(wide, width * parts - i * shard, 1)
-            pieces.append(nt(wide.astype(BF), place)[0:1])
-        rows.append(jnp.concatenate(pieces, axis=1))
-    blank = jnp.zeros((BLOCK - 8 - parts, model), F32)
-    return jnp.concatenate([gv] + rows + [blank], axis=0).T.astype(BF)
+    place = room.at[:width, :wide]
+    spread(place, shard, parts)
+    columns = jnp.concatenate([gv, jnp.zeros((BLOCK - 8, model), F32)], axis=0).T
+    found = []
+    for t in range(model // width):
+        piece = jnp.broadcast_to(gbu[:, t * wide : (t + 1) * wide], (8, wide))
+        rows = [jnp.zeros((8, wide), F32)]
+        for i in range(parts):
+            rows.append((pltpu.roll(piece, wide - i * shard, 1) if i else piece)[0:1])
+        rows.append(jnp.zeros((BLOCK - 8 - parts, wide), F32))
+        found.append(nt(place[...], jnp.concatenate(rows, axis=0).astype(BF)))
+    return (columns + jnp.concatenate(found, axis=0)).astype(BF)
 
 
 ROWS = 256
@@ -609,16 +711,17 @@
 
 
 class Links:
-    rate = {"c": 350.0, "x": 45.0, "y": 45.0, "z": 45.0}
-    lag = 1.5
+    core_rate = 350.0
 
     def __init__(self):
-        self.free = dict.fromkeys(self.rate, 0.0)
+        self.free = dict.fromkeys("cxyz", 0.0)
         self.heap = []
         self.count = 0
+        self.rate, self.lag = GATHER
 
     def send(self, link, at, size):
-        self.free[link] = max(at, self.free[link]) + size / self.rate[link] * 1e-3
+        rate = self.core_rate if link == "c" else self.rate
+        self.free[link] = max(at, self.free[link]) + size / rate * 1e-3
         return self.free[link] + self.lag
 
     def push(self, at, task, then=None):
@@ -627,13 +730,16 @@
 
     def gather(self, gather, at):
         size = gather.rows * gather.cols * 2
+        part = size / 2 if gather.halved else size
         depth = gather.p.depth
 
         def zed(k):
             def then(now):
                 if k < depth - 1:
-                    self.push(self.send("z", now, size), lambda: gather.z_step(k + 1), zed(k + 1))
+                    self.push(self.send("z", now, part), lambda: gather.z_step(k + 1), zed(k + 1))
                 self.push(self.send("x", now, size / 2), lambda: gather.x_step(k), ex(k))
+                if k and gather.halved:
+                    self.push(self.send("y", now, size / 2), lambda: gather.o_step(k))
 
             return then
 
@@ -654,15 +760,17 @@
             def then(now):
                 now = now + 0.3
                 if n == 0:
-                    self.push(self.send("y", now, 2 * size), steps[2], after(2))
+                    link, count = scatter.first
+                    self.push(self.send(link, now, count * size), steps[2], after(2))
                 elif n == 2:
-                    self.push(self.send("x", now, 2 * size), steps[3], after(3))
+                    link, count = scatter.second
+                    self.push(self.send(link, now, count * size), steps[3], after(3))
                 elif 3 <= n < last - 2:
-                    self.push(self.send("z", now, size), steps[n + 1], after(n + 1))
+                    self.push(self.send("z", now, scatter.along * size), steps[n + 1], after(n + 1))
                 elif n == last - 2:
                     self.push(now, steps[last - 1], after(last - 1))
                 elif n == last - 1:
-                    self.push(self.send("y", now, size), steps[last])
+                    self.push(self.send("y", now, scatter.last * size), steps[last])
 
             return then
 
@@ -720,22 +828,42 @@
         loop(count, body)
 
 
+def head_groups(pairs):
+    few = pairs // 3
+    return [(0, few), (few, pairs - few)]
+
+
+def group_columns(pairs):
+    groups = head_groups(pairs)
+    blank = 2 * BLOCK
+    return [(0, blank), (3 * groups[0][1] * BLOCK + blank, 0)]
+
+
+LIGHT = ("o", 0, 1)
+
+
+def column_cuts(model):
+    third = model // 3
+    return [(0, third), (third, model - third)]
+
+
 def layer_kernel(depth, parts, cuts, *refs):
     it = iter(refs)
 
     def take(n):
         return [next(it) for _ in range(n)]
 
-    x_in, seg, sa, so, su, sd, og_in = take(7)
+    x_in, seg, sq, sk, sv, small_in, so, su, sd, og_in = take(10)
     out, pooled, gtok, gq, gk, gv_w, go_w, gu_w, gd_w, small, p_main, p_last = take(12)
     x, q, k, v, o, z_low, df, n1s, dh, r1s, g, sl, stage = take(13)
-    wa, wo, wu, wd, gv, gbu, vec, bup, dk_sum, dv_sum = take(10)
+    wa, wo, wu, wd, gv, gbu, vec, bup = take(8)
     sets = [take(5) for _ in cuts]
-    gsems, ssems, msem, osem, psem = take(9), take(11), *take(3)
+    gsems, ssems, msem, osem, psem, asem = take(11), take(11), *take(4)
 
     seqs, length = seg.shape
     tokens, model = x.shape
     hidden = g.shape[1]
+    dk_sum, dv_sum = r1s.at[:length], r1s.at[length : 2 * length]
     shard = so.shape[0]
     pairs = model // BLOCK
     spans, offsets, _ = key_windows(length)
@@ -750,39 +878,71 @@
         lane = (row * 2 + (1 if qb == final else 0)) * BLOCK
         return dh.at[at : at + span_rows(qb), ds(lane, BLOCK)]
 
-    def probs_at(i, qb):
-        held, at = (sl, 0) if qb == final else (g, offsets[qb])
-        return held.at[at : at + span_rows(qb), ds(i * 2 * BLOCK, 2 * BLOCK)]
+    def probs_of(i):
+        def at(qb):
+            held, at = (sl, 0) if qb == final else (g, offsets[qb])
+            return held.at[at : at + span_rows(qb), ds(i * 2 * BLOCK, 2 * BLOCK)]
+
+        return at
+
+    groups = head_groups(pairs)
+    packed = group_columns(pairs)
+
+    def group_span(n):
+        first, size = groups[n]
+        return slice(first * BLOCK, (first + size) * BLOCK)
+
+    def weight_span(n, part):
+        width = groups[n][1] * BLOCK
+        return slice(packed[n][0] + part * width, packed[n][0] + (part + 1) * width)
+
+    def weight_of(span):
+        return wa[:, :, :, :, span].reshape(model, span.stop - span.start)
 
     place = Place(depth)
     links = Links()
     clock = Clock(links)
     loads = [pltpu.make_async_copy(x_in, x, msem.at[0]), pltpu.make_async_copy(og_in, df, msem.at[1])]
-    for load in loads:
+    mine = wa.at[place.z, place.x, place.c]
+    packs = [pltpu.make_async_copy(small_in, mine.at[:, 3 * groups[0][1] * BLOCK : packed[1][0]], asem.at[0])]
+    for n in range(len(groups)):
+        for part, source in enumerate((sq, sk, sv)):
+            there = mine.at[:, weight_span(n, part)]
+            packs.append(pltpu.make_async_copy(source.at[:, group_span(n)], there, asem.at[len(packs)]))
+    for load in packs + loads:
         load.start()
-    gathers = [
-        Gather(place, n, s, w, gsems) for n, (s, w) in enumerate(((sa, wa), (so, wo), (su, wu), (sd, wd)))
-    ]
+    early = packed[1][0]
+    sources = (
+        (None, wa.at[:, :, :, :, :early]),
+        (None, wa.at[:, :, :, :, early:]),
+        (so, wo), (su, wu), (sd, wd),
+    )
+    gathers = [Gather(place, n, s, w, gsems, n in HALVED) for n, (s, w) in enumerate(sources)]
     for gather, at in zip(gathers, BEGINS):
         links.gather(gather, at)
+    for load in packs:
+        load.wait()
     place.barrier()
     clock.spend(1.0)
     make_bias(seg, bias_at)
     loads[0].wait()
     clock.until(gathers[0])
-    unpack_small(wa[:, :, :, :, 3 * model : 3 * model + BLOCK].reshape(model, BLOCK), shard, parts, vec, bup)
+    at = packed[0][0] + 3 * groups[0][1] * BLOCK
+    unpack_small(wa[:, :, :, :, at : at + BLOCK].reshape(model, BLOCK), shard, parts, vec, bup, g)
 
     def vrow(i):
         return vec[i : i + 1, :]
 
-    def project(rt):
-        rows = ds(rt * ROWS, ROWS)
-        for n, (to, bias) in enumerate(((q, 0), (k, None), (v, 1))):
-            weight = wa[:, :, :, :, n * model : (n + 1) * model].reshape(model, model)
-            value = nn(x[rows, :], weight)
-            to[rows, :] = (value if bias is None else value + vrow(bias)).astype(BF)
-
-    clock.loop(tiles, project, 1.5)
+    def project(n):
+        here = group_span(n)
+
+        def step(rt):
+            rows = ds(rt * ROWS, ROWS)
+            for part, (to, bias) in enumerate(((q, 0), (k, None), (v, 1))):
+                value = nn(x[rows, :], weight_of(weight_span(n, part)))
+                to[rows, here] = (value if bias is None else value + vec[bias : bias + 1, here]).astype(BF)
+
+        clock.loop(tiles, step, 0.25 * groups[n][1])
 
     def copy_probs(i, which, back=False):
         lanes = ds(i * 2 * BLOCK, 2 * BLOCK)
@@ -790,36 +950,52 @@
         there = (p_main if which == 0 else p_last).at[:, lanes]
         return pltpu.make_async_copy(here, there, psem.at[which, i])
 
-    def attend(i):
-        attend_pair(i, length, pairs, q, k, v, o, probs_at, bias_at)
-        copy_probs(i, 0).start()
-        copy_probs(i, 1).start()
-
-    clock.loop(seqs * pairs, attend, 2.1)
+    def attend(n):
+        first, size = groups[n]
+
+        def step(j):
+            row, local = j // size, j % size
+            i = row * pairs + first + local
+            c = ds((first + local) * BLOCK, BLOCK)
+            attend_pair(row, length, (q, c), (k, c), (v, c), (o, c), probs_of(i), functools.partial(bias_at, row))
+            copy_probs(i, 0).start()
+            copy_probs(i, 1).start()
+
+        clock.loop(seqs * size, step, ATTEND)
+
+    for n in range(len(groups)):
+        clock.until(gathers[min(n, 1)])
+        project(n)
+        attend(n)
     for i in range(seqs * pairs):
         copy_probs(i, 0).wait()
         copy_probs(i, 1).wait()
 
-    def up(rt):
-        rows = ds(rt * ROWS, ROWS)
-        h = x[rows, :].astype(F32) + (nn(o[rows, :], wo[...].reshape(model, model)) + vrow(2))
-        c = h - rmean(h)
-        r = lax.rsqrt(rmean(c * c) + EPS)
-        n = c * r
-        n1s[rows, :] = n
-        r1s[rows, :] = jnp.broadcast_to(r, (ROWS, BLOCK))
-        z_low[rows, :] = (n * vrow(3) + vrow(4)).astype(BF)
-        for cc in range(hidden // CHUNK):
-            cs = slice(cc * CHUNK, (cc + 1) * CHUNK)
-            u = nn(z_low[rows, :], wu[:, :, :, :, cs].reshape(model, CHUNK)) + bup[:, cs]
-            cdf, pdf = phi_parts(u)
-            g[rows, cs] = (u * cdf).astype(BF)
-            sl[rows, cs] = (cdf + u * pdf).astype(BF)
-
-    clock.until(gathers[1])
+    chunks = hidden // CHUNK
+
+    def up(i):
+        rows = ds(i // chunks * ROWS, ROWS)
+
+        @pl.when(i % chunks == 0)
+        def _():
+            h = x[rows, :].astype(F32) + (nn(o[rows, :], wo[...].reshape(model, model)) + vrow(2))
+            c = h - rmean(h)
+            r = lax.rsqrt(rmean(c * c) + EPS)
+            n = c * r
+            n1s[rows, :] = n
+            r1s[rows, :] = jnp.broadcast_to(r, (ROWS, BLOCK))
+            z_low[rows, :] = (n * vrow(3) + vrow(4)).astype(BF)
+
+        cs = ds(i % chunks * CHUNK, CHUNK)
+        u = nn(z_low[rows, :], wu[:, :, :, :, cs].reshape(model, CHUNK)) + bup[:, cs]
+        cdf, pdf = phi_parts(u)
+        g[rows, cs] = (u * cdf).astype(BF)
+        sl[rows, cs] = (cdf + u * pdf).astype(BF)
+
     clock.until(gathers[2])
-    clock.loop(tiles, up, 5.0)
     clock.until(gathers[3])
+    clock.loop(tiles * chunks, up, 22.0 / (tiles * chunks))
+    clock.until(gathers[4])
     for gather in gathers:
         gather.end()
     loads[1].wait()
@@ -827,7 +1003,7 @@
     pooled[...] = jnp.zeros_like(pooled)
 
     def copy_tile(rt):
-        return pltpu.make_async_copy(stage.at[rt % 2], out.at[ds(rt * ROWS, ROWS)], osem.at[rt % 2])
+        return pltpu.make_async_copy(stage, out.at[ds(rt * ROWS, ROWS)], osem.at[0])
 
     def down(rt):
         rows = ds(rt * ROWS, ROWS)
@@ -838,11 +1014,11 @@
         y = n2 * vrow(6) + vrow(7)
         y_low = y.astype(BF)
 
-        @pl.when(rt >= 2)
+        @pl.when(rt > 0)
         def _():
-            copy_tile(rt - 2).wait()
-
-        stage[rt % 2] = y_low
+            copy_tile(rt - 1).wait()
+
+        stage[...] = y_low
         copy_tile(rt).start()
         row = rt * ROWS // length
         ids = seg[pl.ds(row, 1), ds(rt * ROWS % length, ROWS)]
@@ -859,8 +1035,7 @@
         gv[5:6, :] += csum(low.astype(F32))
 
     clock.loop(tiles, down, 3.0)
-    for rt in (tiles - 2, tiles - 1):
-        copy_tile(rt).wait()
+    copy_tile(tiles - 1).wait()
     for row in range(seqs):
         onehot = (seg[row : row + 1, :] == lax.broadcasted_iota(jnp.int32, (SEGS, length), 0)).astype(F32)
         pooled[row] = pooled[row] / jnp.sum(onehot, axis=1, keepdims=True)
@@ -869,8 +1044,7 @@
 
     def up_back(cc):
         cs = ds(cc * pair_rows, pair_rows, BLOCK)
-        zz, xx = cc // 2, cc % 2
-        weight = wd[zz, xx].reshape(pair_rows, model)
+        weight = wd[cc // 2, cc % 2].reshape(pair_rows, model)
         total = jnp.zeros((1, pair_rows), F32)
         for rt in range(tiles):
             rows = slice(rt * ROWS, (rt + 1) * ROWS)
@@ -878,38 +1052,50 @@
             sl[rows, cs] = du
             total += csum(du.astype(F32))
         gbu[:, cs] = total
-        wd[zz, xx] = tn(g[:, cs], df[...]).astype(BF).reshape(2, sd.shape[0], model)
-
-    clock.loop(hidden // pair_rows, up_back, 1.8)
-
+        wd[cc // 2, cc % 2] = tn(g[:, cs], df[...]).astype(BF).reshape(2, sd.shape[0], model)
+
+    clock.loop(hidden // pair_rows, up_back, 1.7)
+    links.rate, links.lag = SCATTER
+
+    base = {}
     at = 0
-    blocks = {}
-    for name, rows, cols in (("d", sd.shape[0], model), ("o", shard, model), ("u", shard, hidden),
-                             ("q", shard, model), ("k", shard, model), ("v", shard, model)):
-        blocks[name] = [at + n * rows for n in range(cols // model)]
-        at += rows * (cols // model)
-    blocks["small"] = [at]
+    for name, rows in (("d", sd.shape[0]), ("o", shard), ("u", shard * (hidden // model)), ("q", shard), ("k", shard),
+                       ("v", shard), ("small", shard)):
+        base[name] = at
+        at += rows
     results = {"d": gd_w, "o": go_w, "u": gu_w, "q": gq, "k": gk, "v": gv_w}
-    weights = {"d": wd, "o": wo, "u": wu, "q": wa, "k": wa, "v": wa}
-    first = {"q": 0, "k": model, "v": 2 * model}
+    weights = {"d": wd, "o": wo, "u": wu}
     scatters = {}
     for n, (name, r0, rows, c0, cols) in enumerate(cuts):
         landing = []
-        for c in range(c0, c0 + cols, model):
-            width = min(model, c0 + cols - c)
-            base = blocks["small" if width < model else name][0 if width < model else c // model] + r0
-            view = n1s.at[base : base + rows, 0:width]
-            result = None if width < model else results[name].at[r0 : r0 + rows, c : c + width]
-            landing.append((view, result))
-        c1 = c0 + first.get(name, 0)
-        scatters.setdefault(name, []).append(
-            Scatter(place, n, weights[name].at[:, :, :, r0 : r0 + rows, c1 : c1 + cols], landing, sets[n], ssems)
-        )
-
-    def send_home(name):
-        for s in scatters[name]:
-            s.begin()
-            links.scatter(s, clock.now)
+        if isinstance(name, int):
+            first, size = groups[name]
+            cs = slice(first * BLOCK, (first + size) * BLOCK)
+            spans_of = [(weight, cs.start + at, part * size * BLOCK + at) for part, weight in enumerate("qkv")
+                        for at in range(0, size * BLOCK, 2 * BLOCK)]
+            for weight, to, at in spans_of:
+                if c0 <= at < c0 + cols:
+                    ends = slice(to, to + 2 * BLOCK)
+                    landing.append((2 * BLOCK, n1s.at[base[weight] : base[weight] + shard, ends], results[weight].at[:, ends]))
+            if packed[name][1] and c0 + cols > 3 * size * BLOCK:
+                landing.append((BLOCK, n1s.at[base["small"] : base["small"] + shard, :BLOCK], None))
+            grad = wa.at[:, :, :, :, packed[name][0] + c0 : packed[name][0] + c0 + cols]
+        else:
+            for c in range(c0, c0 + cols, model):
+                top = base[name] + c // model * shard + r0
+                width = min(model, c0 + cols - c)
+                at = c % model
+                landing.append((width, n1s.at[top : top + rows, at : at + width],
+                                results[name].at[r0 : r0 + rows, c : c + width]))
+            grad = weights[name].at[:, :, :, r0 : r0 + rows, c0 : c0 + cols]
+        kind = HalfScatter if name in LIGHT else Scatter
+        scatters.setdefault(name, []).append(kind(place, n, grad, landing, sets[n], ssems))
+
+    def send_home(name, number=None):
+        for n, s in enumerate(scatters[name]):
+            if number is None or n == number:
+                s.begin()
+                links.scatter(s, clock.now)
 
     send_home("d")
     bring = [
@@ -933,12 +1119,16 @@
 
     clock.loop(tiles, first_back, 2.0)
 
-    def up_grad(cc):
-        cs = ds(cc * CHUNK, CHUNK)
-        wu[:, :, :, :, cs] = tn(z_low[...], sl[:, cs]).astype(BF).reshape(depth, 2, 2, shard, CHUNK)
-
-    clock.loop(hidden // CHUNK, up_grad, 1.0)
-    send_home("u")
+    quarter = hidden // 4
+    for n in range(2):
+
+        def up_grad(cc, n=n):
+            cs = ds((2 * n + cc) * quarter, quarter, BLOCK)
+            wu[:, :, :, :, cs] = tn(z_low[...], sl[:, cs]).astype(BF).reshape(depth, 2, 2, shard, quarter)
+
+        clock.loop(2, up_grad, 1.5)
+        send_home("u", n)
+
     bring[1].start()
     do = z_low
 
@@ -949,65 +1139,86 @@
     clock.loop(tiles, out_back, 0.4)
     half = model // 2
 
-    def halves(n, to, left, right):
+    def halves(left, right, columns, to, at, time):
+        width = columns.stop - columns.start
+
         def step(t):
-            value = tn(left[:, ds(t * half, half, BLOCK)], right[...]).astype(BF)
-            to[pl.ds(t * (depth // 2), depth // 2), :, :, :, n * model : (n + 1) * model] = value.reshape(
-                depth // 2, 2, 2, shard, model
-            )
-
-        clock.loop(2, step, 0.8)
-
-    halves(0, wo, o, df)
+            value = tn(left[:, ds(t * half, half, BLOCK)], right[:, columns]).astype(BF)
+            shaped = value.reshape(depth // 2, 2, 2, shard, width)
+            to[pl.ds(t * (depth // 2), depth // 2), :, :, :, at : at + width] = shaped
+
+        clock.loop(2, step, time)
+
+    halves(o, df, slice(0, model), wo, 0, 0.8)
     send_home("o")
     bring[0].wait()
     bring[1].wait()
-    clock.loop(
-        seqs * pairs,
-        lambda i: attend_back_pair(i, length, pairs, q, k, v, do, probs_at, q, k, v, dk_sum, dv_sum),
-        2.2,
-    )
+
+    dq = o
 
     def copy_tokens(rt):
         rows = ds(rt * ROWS, ROWS)
-        return pltpu.make_async_copy(o.at[rows], gtok.at[rows], psem.at[0, rt])
-
-    for n, (name, d) in enumerate((("q", q), ("k", k), ("v", v))):
-
-        def token_step(rt, n=n, d=d):
+        return pltpu.make_async_copy(x.at[rows], gtok.at[rows], psem.at[0, rt])
+
+    for n in reversed(range(len(groups))):
+        first, size = groups[n]
+        here = group_span(n)
+
+        def back(j, first=first, size=size):
+            row, local = j // size, j % size
+            c = ds((first + local) * BLOCK, BLOCK)
+            attend_back_pair(row, length, (q, c), (k, c), (v, c), (do, c), dq, probs_of(row * pairs + first + local),
+                             dk_sum, dv_sum)
+
+        clock.loop(seqs * size, back, BACK)
+
+        def token_step(rt, n=n, here=here):
             rows = ds(rt * ROWS, ROWS)
-            weight = wa[:, :, :, :, n * model : (n + 1) * model].reshape(model, model)
-            total = dh[rows, :] + nt(d[rows, :], weight)
-            if n < 2:
-                dh[rows, :] = total
-            else:
-                o[rows, :] = total.astype(BF)
-                copy_tokens(rt).start()
-
-        clock.loop(tiles, token_step, 0.4)
-        halves(n, wa, x, d)
-        if name == "v":
-            bq, bv = csum(q[...].astype(F32)), csum(v[...].astype(F32))
-            vectors = jnp.concatenate([bq, bv, gv[2:8, :]], axis=0)
-            columns = pack_small(vectors, gbu[...], shard, parts).reshape(depth, 2, 2, shard, BLOCK)
-            wa[:, :, :, :, 3 * model : 3 * model + BLOCK] = columns
-        send_home(name)
+            total = dh[rows, :]
+            for part, d in enumerate((dq, k, v)):
+                total = total + nt(d[rows, here], weight_of(weight_span(n, part)))
+            dh[rows, :] = total
+            gv[0:1, here] += csum(dq[rows, here].astype(F32))
+            gv[1:2, here] += csum(v[rows, here].astype(F32))
+
+        clock.loop(tiles, token_step, 0.25 * size)
+        for part, d in enumerate((dq, k, v)):
+            span = weight_span(n, part)
+            halves(x, d, here, wa, span.start, 0.15 * size)
+        if n == 0:
+            blank = packed[0][0] + 3 * size * BLOCK
+
+            @pl.when(place.z >= 0)
+            def _(blank=blank):
+                columns = pack_small(gv[...], gbu[...], shard, parts, g).reshape(depth, 2, 2, shard, BLOCK)
+                wa[:, :, :, :, blank : blank + BLOCK] = columns
+
+        send_home(n)
+
+    def token_out(rt):
+        rows = ds(rt * ROWS, ROWS)
+        x[rows, :] = dh[rows, :].astype(BF)
+        copy_tokens(rt).start()
+
+    clock.loop(tiles, token_out, 0.2)
     clock.run(links.all())
     for group in scatters.values():
         for s in group:
             s.end()
     for rt in range(tiles):
         copy_tokens(rt).wait()
-    base = blocks["small"][0]
-    last = n1s[base : base + shard, :BLOCK]
+    last = n1s[base["small"] : base["small"] + shard, :BLOCK]
     square = jnp.concatenate([last, jnp.zeros((BLOCK - shard, BLOCK), F32)], axis=0).T
     small[...] = square[:16, :]
 
 
-BEGINS = (0.0, 6.0, 9.0, 14.0)
-
-
-def run_layer(depth, x, seg, sa, so, su, sd, og):
+BEGINS = (0.0, 5.0, 13.0, 16.0, 24.0)
+HALVED = ()
+GATHER, SCATTER = (52.0, 3.0), (50.0, 2.0)
+ATTEND, BACK = 1.6, 1.7
+
+
+def run_layer(depth, x, seg, sq, sk, sv, small, so, su, sd, og):
     tokens, model = x.shape
     hidden = su.shape[1]
     parts = hidden // model
@@ -1016,22 +1227,24 @@
     final_rows = band - offsets[-1]
     shard = so.shape[0]
     cuts = []
-    for part in range(2):
-        cuts.append(("d", part * (sd.shape[0] // 2), sd.shape[0] // 2, 0, model))
+    for at, width in column_cuts(model):
+        cuts.append(("d", 0, sd.shape[0], at, width))
     for part in range(2):
         cuts.append(("u", 0, shard, part * (hidden // 2), hidden // 2))
     cuts.append(("o", 0, shard, 0, model))
-    cuts += [("q", 0, shard, 0, model), ("k", 0, shard, 0, model), ("v", 0, shard, 0, model + 2 * BLOCK)]
+    groups = head_groups(model // BLOCK)
+    for n, (_, blank) in enumerate(group_columns(model // BLOCK)):
+        width = 3 * groups[n][1] * BLOCK + blank
+        cuts += [(n, 0, shard, part * (width // 2), width // 2) for part in range(2)]
     buffers = []
-    for _, _, rows, _, cols in cuts:
-        buffers += scatter_buffers(rows, cols, depth)
+    for name, _, rows, _, cols in cuts:
+        buffers += (scatter_half_buffers if name in LIGHT else scatter_buffers)(rows, cols, depth)
 
     def own(s):
-        return pltpu.VMEM((depth, 2, 2, *s.shape), BF)
+        return pltpu.VMEM((depth, 2, 2, *s), BF)
 
     act, wide = pltpu.VMEM((tokens, model), BF), pltpu.VMEM((tokens, hidden), BF)
     full = pltpu.VMEM((tokens, model), F32)
-    part = pltpu.VMEM((length, BLOCK), F32)
     weight = sds((shard, model), F32)
     iterations = seqs * model // BLOCK
     return pl.pallas_call(
@@ -1039,17 +1252,52 @@
         out_shape=(sds((tokens, model), BF), sds((seqs, SEGS, model), F32), sds((tokens, model), BF),
                    weight, weight, weight, weight, sds(su.shape, F32), sds(sd.shape, F32), sds((16, BLOCK), F32),
                    sds((tokens, hidden), BF), sds((final_rows, hidden), BF)),
-        in_specs=[ANY, V, ANY, ANY, ANY, ANY, ANY],
+        in_specs=[ANY, V] + [ANY] * 8,
         out_specs=(ANY, V, ANY) + (ANY,) * 6 + (V, ANY, ANY),
-        scratch_shapes=[act] * 7 + [full, full, pltpu.VMEM((tokens, BLOCK), F32), wide, wide,
-                        pltpu.VMEM((2, ROWS, model), BF), own(sa), own(so), own(su), own(sd),
+        scratch_shapes=[act] * 7 + [full, full, pltpu.VMEM((max(tokens, 2 * length), BLOCK), F32), wide, wide,
+                        pltpu.VMEM((ROWS, model), BF), own((shard, 3 * model + small.shape[1])), own(so.shape), own(su.shape), own(sd.shape),
                         pltpu.VMEM((8, model), F32), pltpu.VMEM((1, hidden), F32), pltpu.VMEM((8, model), F32),
-                        pltpu.VMEM((1, hidden), F32), part, part, *buffers, *gather_sems(4, depth),
-                        *scatter_sems(len(cuts), depth), pltpu.SemaphoreType.DMA((4,)), pltpu.SemaphoreType.DMA((2,)),
-                        pltpu.SemaphoreType.DMA((2, iterations))],
+                        pltpu.VMEM((1, hidden), F32), *buffers, *gather_sems(5, depth),
+                        *scatter_sems(len(cuts), depth), pltpu.SemaphoreType.DMA((4,)), pltpu.SemaphoreType.DMA((1,)),
+                        pltpu.SemaphoreType.DMA((2, iterations)),
+                        pltpu.SemaphoreType.DMA((1 + 3 * len(groups),))],
         compiler_params=params(0),
         name="layer",
-    )(x, seg, sa, so, su, sd, og)
+    )(x, seg, sq, sk, sv, small, so, su, sd, og)
+
+
+def hand_over_kernel(count, shard, parts, *refs):
+    ins, small = refs[:count], refs[count]
+    outs, vectors = refs[count + 1 : 2 * count + 1], refs[2 * count + 1 : 2 * count + 10]
+    rooms, sems = refs[2 * count + 10 : -1], refs[-1]
+    fetches = [pltpu.make_async_copy(a, b, sems.at[0, n]) for n, (a, b) in enumerate(zip(ins, rooms))]
+    copies = [pltpu.make_async_copy(a, b, sems.at[1, n]) for n, (a, b) in enumerate(zip(rooms, outs))]
+    for copy in fetches:
+        copy.start()
+    for n in range(8):
+        vectors[n][...] = small[n, :shard]
+    rows = jnp.concatenate([small[8:16, :], jnp.zeros((8, BLOCK), F32)], axis=1)
+    total = rows[0]
+    for i in range(1, parts):
+        total = total + pltpu.roll(rows, i * shard, 1)[i]
+    vectors[8][...] = total[: parts * shard]
+    for fetch, copy in zip(fetches, copies):
+        fetch.wait()
+        copy.start()
+    for copy in copies:
+        copy.wait()
+
+
+def hand_over(results, small, shard, parts):
+    count = len(results)
+    return pl.pallas_call(
+        functools.partial(hand_over_kernel, count, shard, parts),
+        out_shape=[sds(r.shape, r.dtype) for r in results] + [sds((shard,), F32)] * 8 + [sds((parts * shard,), F32)],
+        in_specs=[ANY] * count + [V],
+        out_specs=[ANY] * count + [V] * 9,
+        scratch_shapes=[pltpu.VMEM(r.shape, r.dtype) for r in results] + [pltpu.SemaphoreType.DMA((2, count))],
+        name="hand_over",
+    )(*results, small)
 
 
 def local_ring(depth, *args):
@@ -1064,26 +1312,14 @@
         b_up[i * shard : (i + 1) * shard] for i in range(parts)
     ], axis=1)
     small = jnp.pad(small, ((0, 0), (0, 2 * BLOCK - 8 - parts)))
-    sa = jnp.concatenate([w_query, w_key, w_value, small], axis=1)
-    out, pooled, gtok, gq, gk, gv, go, gu, gd, gs, _, _ = run_layer(depth, x, segments, sa, w_out, w_up, w_down, og)
-    gbq, gbv, gbo, gg1, gs1, gbd, gg2, gs2 = [gs[i, :shard] for i in range(8)]
-    gb_up = gs[8 : 8 + parts, :shard].reshape(parts * shard)
+    *results, gs, _, _ = run_layer(depth, x, segments, w_query, w_key, w_value, small, w_out, w_up, w_down, og)
+    out, pooled, gtok, gq, gk, gv, go, gu, gd, gbq, gbv, gbo, gg1, gs1, gbd, gg2, gs2, gb_up = hand_over(
+        results, gs, shard, parts
+    )
     return (
         out.reshape(tokens.shape), pooled, gtok.reshape(tokens.shape),
         gq, gbq, gk, gv, gbv, go, gbo, gg1, gs1, gu, gb_up, gd, gbd, gg2, gs2,
     )
-
-
-def project(x, wa, vec, q, k, v):
-    model = x.shape[1]
-
-    def step(rt):
-        rows = ds(rt * ROWS, ROWS)
-        q[rows, :] = (nn(x[rows, :], wa[:, :model]) + vec[0:1, :]).astype(BF)
-        k[rows, :] = nn(x[rows, :], wa[:, model : 2 * model]).astype(BF)
-        v[rows, :] = (nn(x[rows, :], wa[:, 2 * model : 3 * model]) + vec[1:2, :]).astype(BF)
-
-    loop(x.shape[0] // ROWS, step)
 
 
 def mid_kernel(*refs):
@@ -1231,33 +1467,69 @@
 def plain_views(length, bias, probs):
     spans, offsets, _ = key_windows(length)
 
-    def view(held):
-        return lambda i, qb: held.at[i, pl.ds(offsets[qb], (spans[qb][1] - spans[qb][0]) * BLOCK)]
-
-    return view(bias), view(probs)
-
-
-def qkv_kernel(x, wa, vec, seg, q, k, v, o, probs, bias):
-    length, pairs = seg.shape[1], x.shape[1] // BLOCK
-    bias_at, probs_at = plain_views(length, bias, probs)
-    make_bias(seg, bias_at)
-    project(x, wa, vec, q, k, v)
-    loop(seg.shape[0] * pairs, lambda i: attend_pair(i, length, pairs, q, k, v, o, probs_at, bias_at))
-
-
-def back_kernel(length, q, k, v, do, probs, x, dh1, wa, gtok, g_qkv, gb, dq, dk, dv, dk_sum, dv_sum):
-    pairs, model = x.shape[1] // BLOCK, x.shape[1]
-    loop(
-        x.shape[0] // length * pairs,
-        lambda i: attend_back_pair(i, length, pairs, q, k, v, do, plain_views(length, None, probs)[1], dq, dk, dv, dk_sum, dv_sum),
+    def rows(held, i):
+        return lambda qb: held.at[i, pl.ds(offsets[qb], (spans[qb][1] - spans[qb][0]) * BLOCK)]
+
+    return functools.partial(rows, bias), functools.partial(rows, probs)
+
+
+def pair_columns(pairs, pair):
+    return [ds((part * pairs + pair) * BLOCK, BLOCK) for part in range(3)] + [ds(pair * BLOCK, BLOCK)]
+
+
+def qkv_kernel(x, wa, vec, seg, qkv, o, probs, bias):
+    length, model = seg.shape[1], x.shape[1]
+    pairs = model // BLOCK
+    bias_of, probs_of = plain_views(length, bias, probs)
+    make_bias(seg, lambda row, qb: bias_of(row)(qb))
+    for n, row in enumerate((0, None, 1)):
+        cs = slice(n * model, (n + 1) * model)
+
+        def project(rt, cs=cs, row=row):
+            rows = ds(rt * ROWS, ROWS)
+            value = nn(x[rows, :], wa[:, cs])
+            qkv[rows, cs] = (value if row is None else value + vec[row : row + 1, :]).astype(BF)
+
+        loop(x.shape[0] // ROWS, project)
+
+    def step(i):
+        row = i // pairs
+        cq, ck, cv, co = pair_columns(pairs, i % pairs)
+        attend_pair(row, length, (qkv, cq), (qkv, ck), (qkv, cv), (o, co), probs_of(i), bias_of(row))
+
+    loop(seg.shape[0] * pairs, step)
+
+
+def back_kernel(length, qkv_in, do, probs, x, dh1, wa, gtok, g_qkv, gb, qkv, dq, dk_sum, dv_sum):
+    model = x.shape[1]
+    pairs = model // BLOCK
+    qkv[...] = qkv_in[...]
+    probs_of = plain_views(length, None, probs)[1]
+
+    def step(i):
+        row = i // pairs
+        cq, ck, cv, co = pair_columns(pairs, i % pairs)
+        attend_back_pair(row, length, (qkv, cq), (qkv, ck), (qkv, cv), (do, co), dq, probs_of(i), dk_sum, dv_sum)
+
+    loop(x.shape[0] // length * pairs, step)
+    qkv[:, :model] = dq[...]
+
+    def weight_step(t):
+        rows = ds(t * (model // 2), model // 2)
+        for n in range(3):
+            cs = slice(n * model, (n + 1) * model)
+            g_qkv[rows, cs] = tn(x[:, rows], qkv[:, cs]).astype(BF)
+
+    loop(2, weight_step)
+
+    def token_step(rt):
+        rows = ds(rt * ROWS, ROWS)
+        gtok[rows, :] = (dh1[rows, :] + nt(qkv[rows, :], wa[...])).astype(BF)
+
+    loop(x.shape[0] // ROWS, token_step)
+    gb[...] = jnp.concatenate(
+        [csum(qkv[:, :model].astype(F32)), csum(qkv[:, 2 * model :].astype(F32)), jnp.zeros((6, model), F32)], axis=0
     )
-
-    def store(n, t, value):
-        g_qkv[ds(t * (model // 2), model // 2), n * model : (n + 1) * model] = value
-
-    qkv_grads(x, (dq, dk, dv), store)
-    token_grads(dh1, (dq, dk, dv), wa, gtok)
-    gb[...] = jnp.concatenate([csum(dq[...].astype(F32)), csum(dv[...].astype(F32)), jnp.zeros((6, model), F32)], axis=0)
 
 
 def local_plain(*args):
@@ -1278,27 +1550,27 @@
     bup = gathered(b_up).astype(F32)[None]
     wo, wu, wd = gathered(w_out), gathered(w_up), gathered(w_down)
     act = sds((count, model), BF)
-    q, k, v, o, probs = pl.pallas_call(
+    wide = sds((count, 3 * model), BF)
+    qkv, o, probs = pl.pallas_call(
         qkv_kernel,
-        out_shape=(act, act, act, act, sds((seqs * model // BLOCK, band, 2 * BLOCK), BF)),
+        out_shape=(wide, act, sds((seqs * model // BLOCK, band, 2 * BLOCK), BF)),
         in_specs=[V] * 4,
-        out_specs=(V,) * 5,
+        out_specs=(V,) * 3,
         scratch_shapes=[pltpu.VMEM((seqs, band, BLOCK), F32)],
         compiler_params=params(),
         name="attention",
     )(x, wa, vec, segments)
     out, pooled, g_down, g_up, g_out, do, dh1, gv, gbu = run_mid(x, o, og, segments, wo, wu, wd, vec, bup)
-    kept = pltpu.VMEM((count, model), BF)
     part = pltpu.VMEM((length, BLOCK), F32)
     gtok, g_qkv, gb = pl.pallas_call(
         functools.partial(back_kernel, length),
         out_shape=(act, sds((model, 3 * model), BF), sds((8, model), F32)),
-        in_specs=[V] * 8,
+        in_specs=[V] * 6,
         out_specs=(V,) * 3,
-        scratch_shapes=[kept, kept, kept, part, part],
+        scratch_shapes=[pltpu.VMEM((count, 3 * model), BF), pltpu.VMEM((count, model), BF), part, part],
         compiler_params=params(),
         name="attention_back",
-    )(q, k, v, do, probs, x, dh1, wa)
+    )(qkv, do, probs, x, dh1, wa)
     vectors = jnp.concatenate([gb[:2], gv[2:8]], axis=0).T
 
     def shared(t):
@@ -1324,7 +1596,7 @@
 
     def whole(*args):
         shard = args[2].shape[0] // owners
-        ring = owners % 4 == 0 and mesh.shape["rep"] == 2 and shard % 16 == 0
+        ring = owners % 8 == 0 and mesh.shape["rep"] == 2 and shard % 16 == 0
         body = functools.partial(local_ring, owners // 4) if ring else local_plain
         return jax.shard_map(body, mesh=mesh, in_specs=placed, out_specs=results, check_vma=False)(*args)
 

time: 233 us -> 219 us (0.940)
  local copies, waits for them, and re-layouts: 13.5 us -> 2.43 us
    unnamed x25 -> x0, local copies, waits for them, and re-layouts: 8.84 us -> none
    pallas_call x1, Pallas kernels: 216 us -> 210 us  [run_layer(): pl.pallas_call(functools.partial(layer_kernel, depth, parts, tuple(cuts))...]
    pallas_call x0 -> x1, Pallas kernels: none -> 5.13 us  [hand_over(): pl.pallas_call(functools.partial(hand_over_kernel, count, shard, parts),...]
where the time goes in v3:
time: 219 us; the launch traced here: 218 us
  Pallas kernels  215 us (98%)
  local copies, waits for them, and re-layouts  2.43 us (1%)
    pallas_call x1, Pallas kernels, run_layer(): pl.pallas_call(functools.partial(layer_kernel, depth, parts, tuple(cuts))...  210 us
    pallas_call x1, Pallas kernels, hand_over(): pl.pallas_call(functools.partial(hand_over_kernel, count, shard, parts),...  5.13 us

profile of v3, /device:TPU:0, one launch (start us, length us, event | category | flops | bytes accessed | tf_op | source)
XLA Modules:
  0.0 218.2 jit_solution(3619449928036321996)
XLA Ops:
  0.7 0.9 slice_bitcast_fusion
  1.5 0.8 stack.51
  2.4 0.1 copy.48
  2.5 0.6 pad.4.refs_5_
  3.1 209.9 %layer.1 = (bf16[1024,768]{1,0:T(8,128)(2,1)}, f32[2,8,768]{2,1,0:T(8,128)}, bf16[1024,768]{1,0:T(8,128)(2,1)}, f32[48,768]{1,0:T(8,128)}, f32[48,768]{1,0:T(8,1...) custom-call(bf16[1024,768]{1,0:T(8,128)(2,1)} %bitcast.20, ...), custom_call_target="tpu_custom_call" | custom-call | tf_op jit(solution)/shard_map/layer/pallas_call | solution.py:1250
  212.9 5.1 %hand_over.1 = (bf16[1024,768]{1,0:T(8,128)(2,1)}, f32[2,8,768]{2,1,0:T(8,128)}, bf16[1024,768]{1,0:T(8,128)(2,1)}, f32[48,768]{1,0:T(8,128)}, f32[48,768]{1,0:T...) custom-call(bf16[1024,768]{1,0:T(8,128)(2,1)} %get-tuple-element.46., ...), custom_call_target="tpu_custom_call" | custom-call | tf_op jit(solution)/shard_map/hand_over/pallas_call | solution.py:1293

commit v4 on v3

--- a/solution.py
+++ b/solution.py
@@ -358,7 +358,7 @@
 
 
 def scatter_sems(groups, depth):
-    kinds = [(groups, 2), (groups,), (groups,), (groups, 2, depth - 1), (groups,)]
+    kinds = [(groups, 2, depth), (groups,), (groups,), (groups, 2, depth - 1), (groups,)]
     return [pltpu.SemaphoreType.DMA(k) for k in kinds] * 2 + [pltpu.SemaphoreType.DMA((groups, 5))]
 
 
@@ -396,6 +396,7 @@
 
 class Scatter:
     first, second, along, last = ("y", 2), ("x", 2), 1.0, 1.0
+    pieces = False
 
     def __init__(self, place, g, grad, landing, buffers, sems):
         self.p, self.g, self.grad, self.landing = place, g, grad, landing
@@ -408,7 +409,18 @@
 
     def copy_c(self, x):
         p = self.p
-        return remote(self.grad.at[:, x, 1 - p.c], self.in_c.at[x], self.sc.at[self.g, x], self.rc.at[self.g, x], p.sib)
+        return remote(
+            self.grad.at[:, x, 1 - p.c], self.in_c.at[x], self.sc.at[self.g, x, 0], self.rc.at[self.g, x, 0], p.sib
+        )
+
+    def copy_piece(self, z, x):
+        p = self.p
+        return remote(
+            self.grad.at[z, x, 1 - p.c], self.in_c.at[x, z], self.sc.at[self.g, x, z], self.rc.at[self.g, x, z], p.sib
+        )
+
+    def copies_c(self, x):
+        return [self.copy_piece(z, x) for z in range(self.depth)] if self.pieces else [self.copy_c(x)]
 
     def copy_y(self):
         p = self.p
@@ -453,7 +465,8 @@
     def cores(self, turn):
         p = self.p
         x = 1 - p.x if turn == 0 else p.x
-        self.copy_c(x).wait_recv()
+        for copy in self.copies_c(x):
+            copy.wait_recv()
         add_into(
             self.depth,
             self.rows,
@@ -552,7 +565,8 @@
     def end(self):
         p, top = self.p, self.depth - 1
         for x in (0, 1):
-            self.copy_c(x).wait_send()
+            for copy in self.copies_c(x):
+                copy.wait_send()
         self.end_y()
         self.copy_x().wait_send()
         for direction in (0, 1):
@@ -774,8 +788,9 @@
 
             return then
 
-        self.push(self.send("c", at, 4 * size), steps[0], after(0))
-        self.push(self.send("c", at, 4 * size), steps[1])
+        part = 0 if scatter.pieces else 4
+        self.push(self.send("c", at, part * size), steps[0], after(0))
+        self.push(self.send("c", at, part * size), steps[1])
 
     def due(self, now):
         found = []
@@ -1039,23 +1054,6 @@
     for row in range(seqs):
         onehot = (seg[row : row + 1, :] == lax.broadcasted_iota(jnp.int32, (SEGS, length), 0)).astype(F32)
         pooled[row] = pooled[row] / jnp.sum(onehot, axis=1, keepdims=True)
-
-    pair_rows = 2 * sd.shape[0]
-
-    def up_back(cc):
-        cs = ds(cc * pair_rows, pair_rows, BLOCK)
-        weight = wd[cc // 2, cc % 2].reshape(pair_rows, model)
-        total = jnp.zeros((1, pair_rows), F32)
-        for rt in range(tiles):
-            rows = slice(rt * ROWS, (rt + 1) * ROWS)
-            du = (nt(df[rows, :], weight) * sl[rows, cs].astype(F32)).astype(BF)
-            sl[rows, cs] = du
-            total += csum(du.astype(F32))
-        gbu[:, cs] = total
-        wd[cc // 2, cc % 2] = tn(g[:, cs], df[...]).astype(BF).reshape(2, sd.shape[0], model)
-
-    clock.loop(hidden // pair_rows, up_back, 1.7)
-    links.rate, links.lag = SCATTER
 
     base = {}
     at = 0
@@ -1091,10 +1089,32 @@
         kind = HalfScatter if name in LIGHT else Scatter
         scatters.setdefault(name, []).append(kind(place, n, grad, landing, sets[n], ssems))
 
+    for s in scatters["d"]:
+        s.pieces = True
+    pair_rows = 2 * sd.shape[0]
+
+    def up_back(cc):
+        cs = ds(cc * pair_rows, pair_rows, BLOCK)
+        weight = wd[cc // 2, cc % 2].reshape(pair_rows, model)
+        total = jnp.zeros((1, pair_rows), F32)
+        for rt in range(tiles):
+            rows = slice(rt * ROWS, (rt + 1) * ROWS)
+            du = (nt(df[rows, :], weight) * sl[rows, cs].astype(F32)).astype(BF)
+            sl[rows, cs] = du
+            total += csum(du.astype(F32))
+        gbu[:, cs] = total
+        wd[cc // 2, cc % 2] = tn(g[:, cs], df[...]).astype(BF).reshape(2, sd.shape[0], model)
+        for s in scatters["d"]:
+            s.copy_piece(cc // 2, cc % 2).start()
+
+    clock.loop(hidden // pair_rows, up_back, 1.7)
+    links.rate, links.lag = SCATTER
+
     def send_home(name, number=None):
         for n, s in enumerate(scatters[name]):
             if number is None or n == number:
-                s.begin()
+                if not s.pieces:
+                    s.begin()
                 links.scatter(s, clock.now)
 
     send_home("d")

time: 219 us -> 217 us (level)
  no operation moved by 1% of the time
where the time goes in v4:
time: 217 us
  Pallas kernels  213 us (98%)
  local copies, waits for them, and re-layouts  2.43 us (1%)
    pallas_call x1, Pallas kernels, run_layer(): pl.pallas_call(functools.partial(layer_kernel, depth, parts, tuple(cuts))...  208 us
    pallas_call x1, Pallas kernels, hand_over(): pl.pallas_call(functools.partial(hand_over_kernel, count, shard, parts),...  5.13 us

profile of v4, /device:TPU:0, one launch (start us, length us, event | category | flops | bytes accessed | tf_op | source)
XLA Modules:
  0.0 216.6 jit_solution(6997029672497079448)
XLA Ops:
  0.7 0.9 slice_bitcast_fusion
  1.5 0.8 stack.51
  2.4 0.1 copy.48
  2.5 0.6 pad.4.refs_5_
  3.1 208.2 %layer.1 = (bf16[1024,768]{1,0:T(8,128)(2,1)}, f32[2,8,768]{2,1,0:T(8,128)}, bf16[1024,768]{1,0:T(8,128)(2,1)}, f32[48,768]{1,0:T(8,128)}, f32[48,768]{1,0:T(8,1...) custom-call(bf16[1024,768]{1,0:T(8,128)(2,1)} %bitcast.20, ...), custom_call_target="tpu_custom_call" | custom-call | tf_op jit(solution)/shard_map/layer/pallas_call | solution.py:1270
  211.3 5.1 %hand_over.1 = (bf16[1024,768]{1,0:T(8,128)(2,1)}, f32[2,8,768]{2,1,0:T(8,128)}, bf16[1024,768]{1,0:T(8,128)(2,1)}, f32[48,768]{1,0:T(8,128)}, f32[48,768]{1,0:T...) custom-call(bf16[1024,768]{1,0:T(8,128)(2,1)} %get-tuple-element.46., ...), custom_call_target="tpu_custom_call" | custom-call | tf_op jit(solution)/shard_map/hand_over/pallas_call | solution.py:1313

commit v5 on v4

--- a/solution.py
+++ b/solution.py
@@ -702,7 +702,7 @@
 
 
 ROWS = 256
-CHUNK = 512
+CHUNK = 768
 
 
 def phi_parts(u):

time: 217 us -> 216 us (level)
  no operation moved by 1% of the time
where the time goes in v5:
time: 216 us
  Pallas kernels  212 us (98%)
  local copies, waits for them, and re-layouts  2.43 us (1%)
    pallas_call x1, Pallas kernels, run_layer(): pl.pallas_call(functools.partial(layer_kernel, depth, parts, tuple(cuts))...  207 us
    pallas_call x1, Pallas kernels, hand_over(): pl.pallas_call(functools.partial(hand_over_kernel, count, shard, parts),...  5.13 us

profile of v5, /device:TPU:0, one launch (start us, length us, event | category | flops | bytes accessed | tf_op | source)
XLA Modules:
  0.0 215.6 jit_solution(3518556524319378654)
XLA Ops:
  0.7 0.9 slice_bitcast_fusion
  1.5 0.8 stack.51
  2.4 0.1 copy.48
  2.5 0.6 pad.4.refs_5_
  3.1 207.2 %layer.1 = (bf16[1024,768]{1,0:T(8,128)(2,1)}, f32[2,8,768]{2,1,0:T(8,128)}, bf16[1024,768]{1,0:T(8,128)(2,1)}, f32[48,768]{1,0:T(8,128)}, f32[48,768]{1,0:T(8,1...) custom-call(bf16[1024,768]{1,0:T(8,128)(2,1)} %bitcast.20, ...), custom_call_target="tpu_custom_call" | custom-call | tf_op jit(solution)/shard_map/layer/pallas_call | solution.py:1270
  210.3 5.1 %hand_over.1 = (bf16[1024,768]{1,0:T(8,128)(2,1)}, f32[2,8,768]{2,1,0:T(8,128)}, bf16[1024,768]{1,0:T(8,128)(2,1)}, f32[48,768]{1,0:T(8,128)}, f32[48,768]{1,0:T...) custom-call(bf16[1024,768]{1,0:T(8,128)(2,1)} %get-tuple-element.46., ...), custom_call_target="tpu_custom_call" | custom-call | tf_op jit(solution)/shard_map/hand_over/pallas_call | solution.py:1313
